TPU v7x, 32 devices: a whole 2x2x4 slice. The times are simulated.
32 devices in a mesh: seq: 4 (over x, core), fsdp: 8 (over z, y).
Axes of the slice: x: 2, y: 2, z: 4, core: 2. Of those that a mesh axis runs over, the one named last changes fastest.
Arguments:
- inputs: bfloat16 [8, 2048, 2048], P('fsdp', 'seq'), may hold values from -6 to 6
- teacher: bfloat16 [8, 2048, 2048], P('fsdp', 'seq'), may hold values from -6 to 6
- segment_ids: int32 [8, 2048], P('fsdp', 'seq'), may hold values from 0 to 15, never falling along the last dimension, each value on 1 to 1024 neighbouring positions
- valid: int32 [8, 2048], P('fsdp', 'seq'), may hold values from 0 to 1, as said below
- decay_rate: float32 [16], replicated, may hold values from 4.8828126e-05 to 0.03125
- w_query: bfloat16 [2048, 2048], P(('seq', 'fsdp')), may hold values from -0.125 to 0.125
- w_key: bfloat16 [2048, 2048], P(('seq', 'fsdp')), may hold values from -0.125 to 0.125
- w_value: bfloat16 [2048, 2048], P(('seq', 'fsdp')), may hold values from -0.125 to 0.125
- w_gate: bfloat16 [2048, 2048], P(('seq', 'fsdp')), may hold values from -0.125 to 0.125
- w_out: bfloat16 [2048, 2048], P(('seq', 'fsdp')), may hold values from -0.25 to 0.25
- w_first: bfloat16 [2048, 5632], P(('seq', 'fsdp')), may hold values from -0.125 to 0.125
- w_second: bfloat16 [2048, 5632], P(('seq', 'fsdp')), may hold values from -0.125 to 0.125
- w_down: bfloat16 [5632, 2048], P(('seq', 'fsdp')), may hold values from -0.078125 to 0.078125
Outputs:
- layer_out: bfloat16 [8, 2048, 2048], P('fsdp', 'seq')
- mse_loss: float32 [], replicated
- input_grad: float32 [8, 2048, 2048], P('fsdp', 'seq')
- grad_query: float32 [2048, 2048], P(('seq', 'fsdp'))
- grad_key: float32 [2048, 2048], P(('seq', 'fsdp'))
- grad_value: float32 [2048, 2048], P(('seq', 'fsdp'))
- grad_gate: float32 [2048, 2048], P(('seq', 'fsdp'))
- grad_out: float32 [2048, 2048], P(('seq', 'fsdp'))
- grad_first: float32 [2048, 5632], P(('seq', 'fsdp'))
- grad_second: float32 [2048, 5632], P(('seq', 'fsdp'))
- grad_down: float32 [5632, 2048], P(('seq', 'fsdp'))
Inputs may be any that keep to these rules, and one draw needn't show every extreme that they name: `segment_ids`: along a sequence the ids never fall; a document has 1 to 1024 tokens. The first token of every sequence is valid.
All inputs are finite; a program needn't handle non-finite values.
Results may differ from a plain program's by a relative error of at most 0.009.
Values may be sent and summed in bfloat16 or wider, within the bound.
A program may use at most 352 MiB of HBM per device.

v0:
```python
import jax
import jax.numpy as jnp
from jax import lax
from jax.sharding import PartitionSpec as P

PRECISE = lax.Precision.HIGHEST


def prefix(part, axis, combine, identity):
    place = lax.axis_index(axis)
    gathered = jax.tree.map(lambda a: lax.all_gather(a, axis), part)
    state = jax.tree.map(lambda a, e: jnp.zeros_like(a) + jnp.asarray(e, a.dtype), part, identity)

    def prefix_one(lap, state):
        return combine(
            state, jax.tree.map(lambda a: lax.dynamic_index_in_dim(a, lap, 0, False), gathered)
        )

    return lax.fori_loop(0, place, prefix_one, state)


def entering(array, axis, join, neutral):
    count = lax.axis_size(axis)
    place = lax.axis_index(axis)
    ahead = count - 1 - place
    gathered = jax.tree.map(
        lambda a, kind: lax.all_gather(a.astype(kind), axis),
        array,
        (jnp.int32, jnp.int32, jnp.bfloat16, jnp.bfloat16),
    )
    state = jax.tree.map(lambda a, e: jnp.zeros_like(a) + jnp.asarray(e, a.dtype), array, neutral)

    def entering_one(lap, state):
        source = count - 1 - lap
        return join(
            state,
            jax.tree.map(
                lambda a, own: lax.dynamic_index_in_dim(a, source, 0, False).astype(own.dtype),
                gathered,
                array,
            ),
        )

    return lax.fori_loop(0, ahead, entering_one, state)


def normalize(tensor):
    factor = lax.rsqrt(jnp.mean(tensor * tensor, axis=-1, keepdims=True) + 1e-06)
    return (tensor * factor, factor)


def normalize_back(normed, factor, gradient):
    return factor * (gradient - normed * jnp.mean(gradient * normed, axis=-1, keepdims=True))


def silu_slope(pre_act):
    sigmoid_at = jax.nn.sigmoid(pre_act)
    return sigmoid_at * (1.0 + pre_act * (1.0 - sigmoid_at))


def product(left_side, right_side):
    return jnp.dot(left_side, right_side, preferred_element_type=jnp.float32)


def rows_product(left_side, right_side):
    return lax.dot_general(
        left_side, right_side, (((0,), (0,)), ((), ())), preferred_element_type=jnp.float32
    )


def back_product(gradient, weight):
    return lax.dot_general(
        gradient, weight, (((1,), (1,)), ((), ())), preferred_element_type=jnp.float32
    )


def carry_forward(earlier, later):
    first_early, last_early, fade_early, state_early = earlier
    first_later, last_later, fade_later, state_later = later
    joined = (last_early == first_later) | (last_early < 0) | (first_later < 0)
    link = jnp.where(joined[:, None], fade_later, 0.0)
    return (
        jnp.where(first_early >= 0, first_early, first_later),
        jnp.where(last_later >= 0, last_later, last_early),
        fade_early * link,
        state_later + link[..., None, None] * state_early,
    )


def carry_backward(earlier, later):
    first_high, last_high, fade_high, grad_high = earlier
    first_lower, last_lower, fade_lower, grad_lower = later
    joined = (last_lower == first_high) | (last_lower < 0) | (first_high < 0)
    link = jnp.where(joined[:, None], fade_lower, 0.0)
    return (
        jnp.where(first_lower >= 0, first_lower, first_high),
        jnp.where(last_high >= 0, last_high, last_lower),
        fade_high * link,
        grad_lower + link[..., None, None] * grad_high,
    )


def on_device(
    inputs,
    teacher,
    segment_ids,
    valid,
    decay_rate,
    w_query,
    w_key,
    w_value,
    w_gate,
    w_out,
    w_first,
    w_second,
    w_down,
):
    micro_count, block_len, model_width = inputs.shape
    head_count = decay_rate.shape[0]
    head_dim = model_width // head_count
    row_count = micro_count * block_len
    flat_in = inputs.astype(jnp.float32).reshape(row_count, model_width)

    def split_heads(tensor):
        return tensor.reshape(micro_count, block_len, head_count, head_dim).transpose(0, 2, 1, 3)

    def merge_heads(tensor):
        return tensor.transpose(0, 2, 1, 3).reshape(row_count, model_width)

    attn_full = (
        lax.all_gather(w_query, ("seq", "fsdp"), axis=0, tiled=True),
        lax.all_gather(w_key, ("seq", "fsdp"), axis=0, tiled=True),
        lax.all_gather(w_value, ("seq", "fsdp"), axis=0, tiled=True),
        lax.all_gather(w_gate, ("seq", "fsdp"), axis=0, tiled=True),
        lax.all_gather(w_out, ("seq", "fsdp"), axis=0, tiled=True),
    )
    full_query, full_key, full_value, full_gate, full_out = attn_full
    normed_one, scale_one = normalize(flat_in)
    normed_low = normed_one.astype(jnp.bfloat16)
    pre_query = product(normed_low, full_query)
    pre_key = product(normed_low, full_key)
    pre_value = product(normed_low, full_value)
    pre_gate = product(normed_low, full_gate)
    query_heads = split_heads(jax.nn.silu(pre_query).astype(jnp.bfloat16))
    key_heads = split_heads(jax.nn.silu(pre_key).astype(jnp.bfloat16))
    value_heads = split_heads(jax.nn.silu(pre_value).astype(jnp.bfloat16))
    gate_act = jax.nn.silu(pre_gate)
    query_wide = query_heads.astype(jnp.float32)
    key_wide = key_heads.astype(jnp.float32)
    value_wide = value_heads.astype(jnp.float32)
    position = jnp.arange(block_len)
    same_doc = segment_ids[:, :, None] == segment_ids[:, None, :]
    before = position[:, None] >= position[None, :]
    distance = jnp.maximum(position[:, None] - position[None, :], 0).astype(jnp.float32)
    inner_mask = jnp.where(
        (same_doc & before)[:, None],
        jnp.exp(-decay_rate[None, :, None, None] * distance[None, None]),
        0.0,
    )
    first_id = segment_ids[:, 0]
    last_id = segment_ids[:, block_len - 1]
    tail_decay = jnp.where(
        (segment_ids == last_id[:, None])[:, None, :],
        jnp.exp(
            -decay_rate[None, :, None] * (block_len - 1 - position).astype(jnp.float32)[None, None]
        ),
        0.0,
    )
    fade_all = jnp.where(
        (first_id == last_id)[:, None], jnp.exp(-decay_rate * block_len)[None, :], 0.0
    )
    state_local = jnp.einsum(
        "mhjd,mhje->mhde", key_wide * tail_decay[..., None], value_wide, precision=PRECISE
    )
    identity = (
        jnp.full((micro_count,), -1, jnp.int32),
        jnp.full((micro_count,), -1, jnp.int32),
        jnp.ones((micro_count, head_count), jnp.float32),
        jnp.zeros_like(state_local),
    )
    first_in, last_in, fade_in, state_in = prefix(
        (first_id, last_id, fade_all, state_local), "seq", carry_forward, identity
    )
    entry_decay = jnp.where(
        (segment_ids == last_in[:, None])[:, None, :],
        jnp.exp(-decay_rate[None, :, None] * (position + 1).astype(jnp.float32)[None, None]),
        0.0,
    )
    scores = jnp.einsum(
        "mhtd,mhjd->mhtj", query_heads, key_heads, preferred_element_type=jnp.float32
    )
    weighted = scores * inner_mask
    mixed_heads = jnp.einsum("mhtj,mhjd->mhtd", weighted, value_wide, precision=PRECISE)
    mixed_heads = mixed_heads + entry_decay[..., None] * jnp.einsum(
        "mhtd,mhde->mhte", query_wide, state_in, precision=PRECISE
    )
    mixed = merge_heads(mixed_heads)
    attn_normed, attn_scale = normalize(mixed)
    joined = (attn_normed * gate_act).astype(jnp.bfloat16)
    hidden = flat_in + product(joined, full_out)
    glu_full = (
        lax.all_gather(w_first, ("seq", "fsdp"), axis=0, tiled=True),
        lax.all_gather(w_second, ("seq", "fsdp"), axis=0, tiled=True),
        lax.all_gather(w_down, ("seq", "fsdp"), axis=0, tiled=True),
    )
    full_first, full_second, full_down = glu_full
    normed_two, scale_two = normalize(hidden)
    second_low = normed_two.astype(jnp.bfloat16)
    part_one = product(second_low, full_first)
    part_two = product(second_low, full_second)
    glu_low = (part_one * part_two).astype(jnp.bfloat16)
    final_rows = hidden + product(glu_low, full_down)
    layer_out = final_rows.astype(jnp.bfloat16).reshape(micro_count, block_len, model_width)
    keep_mask = valid.astype(jnp.float32).reshape(row_count, 1)
    error_rows = final_rows - teacher.astype(jnp.float32).reshape(row_count, model_width)
    valid_count, loss_sum = lax.psum(
        (jnp.sum(keep_mask), jnp.sum(keep_mask * error_rows * error_rows)), ("seq", "fsdp")
    )
    loss_value = loss_sum / (model_width * valid_count)
    total_tokens = row_count * lax.axis_size("seq") * lax.axis_size("fsdp")
    grad_final = total_tokens / valid_count * keep_mask * error_rows
    back_glu = (
        lax.all_gather(w_first, ("seq", "fsdp"), axis=0, tiled=True),
        lax.all_gather(w_second, ("seq", "fsdp"), axis=0, tiled=True),
        lax.all_gather(w_down, ("seq", "fsdp"), axis=0, tiled=True),
    )
    back_first, back_second, back_down = back_glu
    grad_low = grad_final.astype(jnp.bfloat16)
    grad_w_down = rows_product(glu_low, grad_low)
    grad_glu = back_product(grad_low, back_down)
    grad_one = (grad_glu * part_two).astype(jnp.bfloat16)
    grad_two = (grad_glu * part_one).astype(jnp.bfloat16)
    grad_w_first = rows_product(second_low, grad_one)
    grad_w_second = rows_product(second_low, grad_two)
    grad_normed_two = back_product(grad_one, back_first) + back_product(grad_two, back_second)
    share_first, share_second, share_down = (
        lax.psum_scatter(grad_w_first, ("seq", "fsdp"), scatter_dimension=0, tiled=True),
        lax.psum_scatter(grad_w_second, ("seq", "fsdp"), scatter_dimension=0, tiled=True),
        lax.psum_scatter(grad_w_down, ("seq", "fsdp"), scatter_dimension=0, tiled=True),
    )
    grad_hidden = grad_final + normalize_back(normed_two, scale_two, grad_normed_two)
    back_attn = (
        lax.all_gather(w_query, ("seq", "fsdp"), axis=0, tiled=True),
        lax.all_gather(w_key, ("seq", "fsdp"), axis=0, tiled=True),
        lax.all_gather(w_value, ("seq", "fsdp"), axis=0, tiled=True),
        lax.all_gather(w_gate, ("seq", "fsdp"), axis=0, tiled=True),
        lax.all_gather(w_out, ("seq", "fsdp"), axis=0, tiled=True),
    )
    back_query, back_key, back_value, back_gate, back_out = back_attn
    hidden_low = grad_hidden.astype(jnp.bfloat16)
    grad_w_out = rows_product(joined, hidden_low)
    grad_joined = back_product(hidden_low, back_out)
    grad_gate_pre = (grad_joined * attn_normed * silu_slope(pre_gate)).astype(jnp.bfloat16)
    grad_mixed = normalize_back(attn_normed, attn_scale, grad_joined * gate_act).astype(
        jnp.bfloat16
    )
    grad_heads = split_heads(grad_mixed)
    grad_wide = grad_heads.astype(jnp.float32)
    grad_scores = (
        jnp.einsum("mhtd,mhjd->mhtj", grad_heads, value_heads, preferred_element_type=jnp.float32)
        * inner_mask
    )
    grad_state_in = jnp.einsum(
        "mhtd,mhte->mhde", query_wide * entry_decay[..., None], grad_wide, precision=PRECISE
    )
    first_out, last_out, fade_out, grad_state_out = entering(
        (first_id, last_id, fade_all, grad_state_in), "seq", carry_backward, identity
    )
    grad_state_end = jnp.where((last_id == first_out)[:, None, None, None], grad_state_out, 0.0)
    grad_query_heads = jnp.einsum("mhtj,mhjd->mhtd", grad_scores, key_wide, precision=PRECISE)
    grad_query_heads = grad_query_heads + entry_decay[..., None] * jnp.einsum(
        "mhte,mhde->mhtd", grad_wide, state_in, precision=PRECISE
    )
    grad_key_heads = jnp.einsum("mhtj,mhtd->mhjd", grad_scores, query_wide, precision=PRECISE)
    grad_key_heads = grad_key_heads + tail_decay[..., None] * jnp.einsum(
        "mhje,mhde->mhjd", value_wide, grad_state_end, precision=PRECISE
    )
    grad_value_heads = jnp.einsum("mhtj,mhtd->mhjd", weighted, grad_wide, precision=PRECISE)
    grad_value_heads = grad_value_heads + tail_decay[..., None] * jnp.einsum(
        "mhjd,mhde->mhje", key_wide, grad_state_end, precision=PRECISE
    )
    grad_query_pre = (merge_heads(grad_query_heads) * silu_slope(pre_query)).astype(jnp.bfloat16)
    grad_key_pre = (merge_heads(grad_key_heads) * silu_slope(pre_key)).astype(jnp.bfloat16)
    grad_value_pre = (merge_heads(grad_value_heads) * silu_slope(pre_value)).astype(jnp.bfloat16)
    grad_w_query = rows_product(normed_low, grad_query_pre)
    grad_w_key = rows_product(normed_low, grad_key_pre)
    grad_w_value = rows_product(normed_low, grad_value_pre)
    grad_w_gate = rows_product(normed_low, grad_gate_pre)
    grad_normed_one = back_product(grad_query_pre, back_query) + back_product(
        grad_key_pre, back_key
    )
    grad_normed_one = (
        grad_normed_one
        + back_product(grad_value_pre, back_value)
        + back_product(grad_gate_pre, back_gate)
    )
    share_query, share_key, share_value, share_gate, share_out = (
        lax.psum_scatter(grad_w_query, ("seq", "fsdp"), scatter_dimension=0, tiled=True),
        lax.psum_scatter(grad_w_key, ("seq", "fsdp"), scatter_dimension=0, tiled=True),
        lax.psum_scatter(grad_w_value, ("seq", "fsdp"), scatter_dimension=0, tiled=True),
        lax.psum_scatter(grad_w_gate, ("seq", "fsdp"), scatter_dimension=0, tiled=True),
        lax.psum_scatter(grad_w_out, ("seq", "fsdp"), scatter_dimension=0, tiled=True),
    )
    input_grad = grad_hidden + normalize_back(normed_one, scale_one, grad_normed_one)
    return (
        layer_out,
        loss_value,
        input_grad.reshape(micro_count, block_len, model_width),
        share_query,
        share_key,
        share_value,
        share_gate,
        share_out,
        share_first,
        share_second,
        share_down,
    )


def solution(mesh):
    in_specs = (
        P("fsdp", "seq", None),
        P("fsdp", "seq", None),
        P("fsdp", "seq"),
        P("fsdp", "seq"),
        P(),
        P(("seq", "fsdp"), None),
        P(("seq", "fsdp"), None),
        P(("seq", "fsdp"), None),
        P(("seq", "fsdp"), None),
        P(("seq", "fsdp"), None),
        P(("seq", "fsdp"), None),
        P(("seq", "fsdp"), None),
        P(("seq", "fsdp"), None),
    )
    out_specs = (
        P("fsdp", "seq", None),
        P(),
        P("fsdp", "seq", None),
        P(("seq", "fsdp"), None),
        P(("seq", "fsdp"), None),
        P(("seq", "fsdp"), None),
        P(("seq", "fsdp"), None),
        P(("seq", "fsdp"), None),
        P(("seq", "fsdp"), None),
        P(("seq", "fsdp"), None),
        P(("seq", "fsdp"), None),
    )
    return jax.shard_map(
        on_device, mesh=mesh, in_specs=in_specs, out_specs=out_specs, check_vma=False
    )
```

profile of v0, /device:TPU:0, one launch (start us, length us, event | category | flops | bytes accessed | tf_op | source)
XLA Modules:
  0.0 5814.3 jit_solution(1748188651600747495)
XLA Ops:
  18.7 72.5 %all-gather.17.cloned.1.call-done = bf16[2048,2048]{1,0:T(8,128)(2,1)} async-done(((bf16[64,2048]{1,0:T(8,128)(2,1)}), bf16[2048,2048]{1,0:T(8,128)(2,1)}) %all-gather.17.cloned.1.call-update) | async-done | bytes 8388624 | tf_op jit(solution)/shard_map/all_gather | solution.py:132
  91.1 7.6 fusion.108
  102.5 67.7 %all-gather.19.cloned.1.call-done = bf16[2048,2048]{1,0:T(8,128)(2,1)} async-done(((bf16[64,2048]{1,0:T(8,128)(2,1)}), bf16[2048,2048]{1,0:T(8,128)(2,1)}) %all-gather.19.cloned.1.call-update) | async-done | bytes 8388624 | tf_op jit(solution)/shard_map/all_gather | solution.py:133
  170.1 7.6 fusion.106
  208.6 40.7 all-gather.15.cloned.1.call-done
  249.3 11.6 multiply_convert_fusion.11
  268.8 8.4 fusion.51
  277.2 19.1 fusion.7
  310.6 54.0 all-gather.21.cloned.1.call-done
  364.6 11.2 multiply_convert_fusion.8
  375.9 67.6 %all-gather.23.cloned.1.call-done = bf16[2048,2048]{1,0:T(8,128)(2,1)} async-done(((bf16[64,2048]{1,0:T(8,128)(2,1)}), bf16[2048,2048]{1,0:T(8,128)(2,1)}) %all-gather.23.cloned.1.call-update) | async-done | bytes 8388624 | tf_op jit(solution)/shard_map/all_gather | solution.py:135
  443.5 7.7 multiply_reduce_fusion.2
  453.5 136.2 %all-gather.27.cloned.1.call-done = bf16[2048,5632]{1,0:T(8,128)(2,1)} async-done(((bf16[64,5632]{1,0:T(8,128)(2,1)}), bf16[2048,5632]{1,0:T(8,128)(2,1)}) %all-gather.27.cloned.1.call-update) | async-done | bytes 23068688 | tf_op jit(solution)/shard_map/all_gather | solution.py:203
  589.7 19.2 fusion.113
  608.9 126.5 %all-gather.25.cloned.1.call-done = bf16[2048,5632]{1,0:T(8,128)(2,1)} async-done(((bf16[64,5632]{1,0:T(8,128)(2,1)}), bf16[2048,5632]{1,0:T(8,128)(2,1)}) %all-gather.25.cloned.1.call-update) | async-done | bytes 23068688 | tf_op jit(solution)/shard_map/all_gather | solution.py:202
  735.4 22.7 multiply_convert_fusion.2
  758.1 123.1 %all-gather.29.cloned.1.call-done = bf16[5632,2048]{1,0:T(8,128)(2,1)} async-done(((bf16[176,2048]{1,0:T(8,128)(2,1)}), bf16[5632,2048]{1,0:T(8,128)(2,1)}) %all-gather.29.cloned.1.call-update) | async-done | bytes 23068688 | tf_op jit(solution)/shard_map/all_gather | solution.py:204
  881.1 21.2 fusion.37
  902.4 38.8 all-reduce.5
  946.0 25.3 multiply_convert_fusion
  971.3 19.7 fusion.114
  990.9 19.7 multiply_reduce_fusion.1
  1016.4 13.0 multiply_reduce_fusion
  1039.8 10.0 fusion.53
  1053.0 19.3 fusion.11
  1088.2 8.4 fusion.102
  1096.7 12.8 fusion.96
  1109.6 13.2 fusion.76
  1123.6 7.4 all-reduce.3
  1131.1 15.0 fusion.9
  1146.2 13.6 while.33
  1179.1 8.3 fusion.100
  1187.6 15.1 fusion.5
  1219.4 8.5 fusion.98
  1228.0 24.1 fusion.118
  1252.1 24.1 fusion.119
  1276.3 24.3 fusion.120
  1301.9 10.8 fusion.115
  1312.7 9.6 fusion.117
  1328.8 12.9 fusion.32
  1346.9 109.0 %reduce-scatter.9.cloned.1.call-done = f32[64,2048]{1,0:T(8,128)} async-done(((f32[2048,2048]{1,0:T(8,128)}), f32[64,2048]{1,0:T(8,128)}) %reduce-scatter.9.cloned.1.call-update) | async-done | bytes 524304 | tf_op jit(solution)/shard_map/reduce_scatter | solution.py:298
  1455.9 360.1 %reduce-scatter.15.cloned.1.call-done = f32[64,2048]{1,0:T(8,128)} async-done(((f32[2048,2048]{1,0:T(8,128)}), f32[64,2048]{1,0:T(8,128)}) %reduce-scatter.15.cloned.1.call-update) | async-done | bytes 524304 | tf_op jit(solution)/shard_map/reduce_scatter | solution.py:301
  1816.0 360.2 %reduce-scatter.17.cloned.1.call-done = f32[64,2048]{1,0:T(8,128)} async-done(((f32[2048,2048]{1,0:T(8,128)}), f32[64,2048]{1,0:T(8,128)}) %reduce-scatter.17.cloned.1.call-update) | async-done | bytes 524304 | tf_op jit(solution)/shard_map/reduce_scatter | solution.py:302
  2176.2 360.1 %reduce-scatter.11.cloned.1.call-done = f32[64,2048]{1,0:T(8,128)} async-done(((f32[2048,2048]{1,0:T(8,128)}), f32[64,2048]{1,0:T(8,128)}) %reduce-scatter.11.cloned.1.call-update) | async-done | bytes 524304 | tf_op jit(solution)/shard_map/reduce_scatter | solution.py:299
  2536.3 360.1 %reduce-scatter.13.cloned.1.call-done = f32[64,2048]{1,0:T(8,128)} async-done(((f32[2048,2048]{1,0:T(8,128)}), f32[64,2048]{1,0:T(8,128)}) %reduce-scatter.13.cloned.1.call-update) | async-done | bytes 524304 | tf_op jit(solution)/shard_map/reduce_scatter | solution.py:300
  2896.4 969.4 %reduce-scatter.19.cloned.1.call-done = f32[64,5632]{1,0:T(8,128)} async-done(((f32[2048,5632]{1,0:T(8,128)}), f32[64,5632]{1,0:T(8,128)}) %reduce-scatter.19.cloned.1.call-update) | async-done | bytes 1441808 | tf_op jit(solution)/shard_map/reduce_scatter | solution.py:237
  3865.7 970.1 %reduce-scatter.21.cloned.1.call-done = f32[64,5632]{1,0:T(8,128)} async-done(((f32[2048,5632]{1,0:T(8,128)}), f32[64,5632]{1,0:T(8,128)}) %reduce-scatter.21.cloned.1.call-update) | async-done | bytes 1441808 | tf_op jit(solution)/shard_map/reduce_scatter | solution.py:238
  4835.8 970.1 %reduce-scatter.23.cloned.1.call-done = f32[176,2048]{1,0:T(8,128)} async-done(((f32[5632,2048]{1,0:T(8,128)}), f32[176,2048]{1,0:T(8,128)}) %reduce-scatter.23.cloned.1.call-update) | async-done | bytes 1441808 | tf_op jit(solution)/shard_map/reduce_scatter | solution.py:239
  (218 shorter events, 161.6 us)
Async XLA Ops:
  7.2 84.0 %all-gather.17.cloned.1.call-start = ((), (), s32[]{:S(2)}) async-start(), calls=%async_computation.9 | async-start | bytes 8650752 | tf_op jit(solution)/shard_map/all_gather | solution.py:132
  7.9 162.2 %all-gather.19.cloned.1.call-start = ((), (), s32[]{:S(2)}) async-start(), calls=%async_computation.10 | async-start | bytes 8650752 | tf_op jit(solution)/shard_map/all_gather | solution.py:133
  8.7 240.6 %all-gather.15.cloned.1.call-start = ((), (), s32[]{:S(2)}) async-start(), calls=%async_computation.8 | async-start | bytes 8650752 | tf_op jit(solution)/shard_map/all_gather | solution.py:131
  9.4 286.9 %all-gather.31.cloned.1.call-start = ((), (), s32[]{:S(2)}) async-start(), calls=%async_computation.24 | async-start | bytes 5242880 | tf_op jit(solution)/shard_map/all_gather | solution.py:11
  16.5 280.0 %copy-start.49 = (f32[16]{0:T(128)}, f32[16]{0:T(128)S(1)}, u32[]{:S(2)}) copy-start(f32[16]{0:T(128)S(1)} %get-tuple-element.298) | copy-start | bytes 196
  18.6 346.1 %copy-start.44 = (f32[512]{0:T(512)}, f32[512]{0:T(512)S(1)}, u32[]{:S(2)}) copy-start(f32[512]{0:T(512)S(1)} %add_rsqrt_fusion.2) | copy-start | bytes 6148
  18.6 162.8 %copy-start.33 = (f32[16,512]{1,0:T(8,128)}, f32[16,512]{1,0:T(8,128)S(1)}, u32[]{:S(2)}) copy-start(f32[16,512]{1,0:T(8,128)S(1)} %exponential_select_fusion.2) | copy-start | bytes 98308
  102.4 166.4 %copy-start.2 = (bf16[64,8,16,128]{3,2,1,0:T(8,128)(2,1)}, bf16[64,8,16,128]{3,2,1,0:T(8,128)(2,1)S(1)}, u32[]{:S(2)}) copy-start(bf16[64,8,16,128]{3,2,1,0:T(8,128)(2,1)S(1)} %copy.88) | copy-start | bytes 6291460
  182.8 24.8 copy-start.48
  182.8 25.6 copy-start.43
  189.8 174.8 %all-gather.21.cloned.1.call-start = ((), (), s32[]{:S(2)}) async-start(), calls=%async_computation.11 | async-start | bytes 8650752 | tf_op jit(solution)/shard_map/all_gather | solution.py:134
  190.4 253.1 %all-gather.23.cloned.1.call-start = ((), (), s32[]{:S(2)}) async-start(), calls=%async_computation.12 | async-start | bytes 8650752 | tf_op jit(solution)/shard_map/all_gather | solution.py:135
  191.0 398.6 %all-gather.27.cloned.1.call-start = ((), (), s32[]{:S(2)}) async-start(), calls=%async_computation.14 | async-start | bytes 23789568 | tf_op jit(solution)/shard_map/all_gather | solution.py:203
  191.8 543.6 %all-gather.25.cloned.1.call-start = ((), (), s32[]{:S(2)}) async-start(), calls=%async_computation.13 | async-start | bytes 23789568 | tf_op jit(solution)/shard_map/all_gather | solution.py:202
  192.5 688.6 %all-gather.29.cloned.1.call-start = ((), (), s32[]{:S(2)}) async-start(), calls=%async_computation.15 | async-start | bytes 23789568 | tf_op jit(solution)/shard_map/all_gather | solution.py:204
  193.2 952.8 %all-gather.33.cloned.1.call-start = ((), (), s32[]{:S(2)}) async-start(), calls=%async_computation.25 | async-start | bytes 2621440 | tf_op jit(solution)/shard_map/all_gather | solution.py:27
  208.4 68.8 %copy-start.31 = (f32[512,512]{1,0:T(8,128)}, f32[512,512]{1,0:T(8,128)S(1)}, u32[]{:S(2)}) copy-start(f32[512,512]{1,0:T(8,128)S(1)} %maximum_convert_fusion) | copy-start | bytes 3145732
  208.6 68.6 %copy-start.37 = (pred[512,512]{1,0:T(8,128)(4,1)}, pred[512,512]{1,0:T(8,128)(4,1)S(1)}, u32[]{:S(2)}) copy-start(pred[512,512]{1,0:T(8,128)(4,1)S(1)} %fusion.80) | copy-start | bytes 786436
  296.4 8.4 copy-start
  304.8 59.8 %copy-start.19 = (bf16[1,512,2048]{2,1,0:T(8,128)(2,1)S(1)}, bf16[1,512,2048]{2,1,0:T(8,128)(2,1)}, u32[]{:S(2)}) copy-start(bf16[1,512,2048]{2,1,0:T(8,128)(2,1)} %param.17) | copy-start | bytes 6291460
  310.6 65.2 %copy-start.46 = (f32[512]{0:T(512)}, f32[512]{0:T(512)S(1)}, u32[]{:S(2)}) copy-start(f32[512]{0:T(512)S(1)} %add_rsqrt_fusion.1) | copy-start | bytes 6148
  453.5 136.2 %copy-start.30 = (bf16[512,2048]{1,0:T(8,128)(2,1)}, bf16[512,2048]{1,0:T(8,128)(2,1)S(1)}, u32[]{:S(2)}) copy-start(bf16[512,2048]{1,0:T(8,128)(2,1)S(1)} %multiply_convert_fusion.13) | copy-start | bytes 6291460
  608.9 272.3 %copy-start.18 = (bf16[1,512,2048]{2,1,0:T(8,128)(2,1)S(1)}, bf16[1,512,2048]{2,1,0:T(8,128)(2,1)}, u32[]{:S(2)}) copy-start(bf16[1,512,2048]{2,1,0:T(8,128)(2,1)} %param.18) | copy-start | bytes 6291460
  990.9 19.7 copy-start.14
  990.9 19.7 copy-start.16
  1016.4 13.1 copy-start.23
  1039.8 10.0 copy-start.8
  1039.8 10.0 copy-start.9
  1039.8 10.0 copy-start.36
  1052.9 19.4 copy-start.1
  1052.9 403.0 %reduce-scatter.9.cloned.1.call-start = ((), (), s32[]{:S(2)}) async-start(), calls=%async_computation.16 | async-start | bytes 17301504 | tf_op jit(solution)/shard_map/reduce_scatter | solution.py:298
  1053.0 19.3 copy-start.10
  1096.7 719.3 %reduce-scatter.15.cloned.1.call-start = ((), (), s32[]{:S(2)}) async-start(), calls=%async_computation.19 | async-start | bytes 17301504 | tf_op jit(solution)/shard_map/reduce_scatter | solution.py:301
  1109.5 1066.7 %reduce-scatter.17.cloned.1.call-start = ((), (), s32[]{:S(2)}) async-start(), calls=%async_computation.20 | async-start | bytes 17301504 | tf_op jit(solution)/shard_map/reduce_scatter | solution.py:302
  1122.8 1413.5 %reduce-scatter.11.cloned.1.call-start = ((), (), s32[]{:S(2)}) async-start(), calls=%async_computation.17 | async-start | bytes 17301504 | tf_op jit(solution)/shard_map/reduce_scatter | solution.py:299
  1131.1 15.1 copy-start.40
  1131.1 15.1 copy-start.42
  1146.2 14.3 copy-start.34
  1187.5 15.2 copy-start.3
  1187.5 1708.8 %reduce-scatter.13.cloned.1.call-start = ((), (), s32[]{:S(2)}) async-start(), calls=%async_computation.18 | async-start | bytes 17301504 | tf_op jit(solution)/shard_map/reduce_scatter | solution.py:300
  1227.9 2637.8 %reduce-scatter.19.cloned.1.call-start = ((), (), s32[]{:S(2)}) async-start(), calls=%async_computation.21 | async-start | bytes 47579136 | tf_op jit(solution)/shard_map/reduce_scatter | solution.py:237
  1252.1 3583.8 %reduce-scatter.21.cloned.1.call-start = ((), (), s32[]{:S(2)}) async-start(), calls=%async_computation.22 | async-start | bytes 47579136 | tf_op jit(solution)/shard_map/reduce_scatter | solution.py:238
  1276.2 4529.7 %reduce-scatter.23.cloned.1.call-start = ((), (), s32[]{:S(2)}) async-start(), calls=%async_computation.23 | async-start | bytes 47579136 | tf_op jit(solution)/shard_map/reduce_scatter | solution.py:239
  1301.9 10.8 copy-start.29
  1301.9 20.4 slice-start
  1312.7 9.6 copy-start.27
  1312.7 9.6 slice-start.1
  1328.8 12.9 copy-start.17
  (24 other events, 105.1 us)
Sparse Core Ops, SparseCore 0:
  11.0 80.0 all-gather.16
  94.1 75.9 all-gather.18
  173.1 76.1 all-gather.14
  251.3 33.0 all-gather.30
  287.2 77.3 all-gather.20
  367.5 75.9 all-gather.22
  446.4 143.1 all-gather.26
  592.6 142.7 all-gather.24
  738.3 142.7 all-gather.28
  1053.0 23.5 all-gather.32
  1096.8 359.0 reduce-scatter.8
  1458.6 357.3 reduce-scatter.14
  1818.8 357.3 reduce-scatter.16
  2178.9 357.3 reduce-scatter.10
  2539.0 357.3 reduce-scatter.12
  2899.1 966.5 reduce-scatter.18
  3868.5 967.3 reduce-scatter.20
  4838.6 967.3 reduce-scatter.22
where the time goes:
time: 5820 us; the launch traced here: 5810 us
  waiting for transfers between devices  5150 us (88%)
  matrix products  469 us (8%)
    reduce_scatter x1, waiting for transfers between devices, on_device(): lax.psum_scatter(grad_w_down, ('seq', 'fsdp'), scatter_dimension=0, tiled...  970 us
    reduce_scatter x1, waiting for transfers between devices, on_device(): lax.psum_scatter(grad_w_second, ('seq', 'fsdp'), scatter_dimension=0, til...  970 us
    reduce_scatter x1, waiting for transfers between devices, on_device(): lax.psum_scatter(grad_w_first, ('seq', 'fsdp'), scatter_dimension=0, tile...  969 us
    reduce_scatter x1, waiting for transfers between devices, on_device(): lax.psum_scatter(grad_w_out, ('seq', 'fsdp'), scatter_dimension=0, tiled=...  360 us
    reduce_scatter x1, waiting for transfers between devices, on_device(): lax.psum_scatter(grad_w_key, ('seq', 'fsdp'), scatter_dimension=0, tiled=...  360 us
    reduce_scatter x1, waiting for transfers between devices, on_device(): lax.psum_scatter(grad_w_gate, ('seq', 'fsdp'), scatter_dimension=0, tiled...  360 us
    reduce_scatter x1, waiting for transfers between devices, on_device(): lax.psum_scatter(grad_w_value, ('seq', 'fsdp'), scatter_dimension=0, tile...  360 us
    all_gather x1, waiting for transfers between devices, on_device(): lax.all_gather(w_second, ('seq', 'fsdp'), axis=0, tiled=True)  136 us
  transfers between devices with their start and end apart: 18, of which 16 were waited for; matrix products, arithmetic and copies ran while one was open for 7% of the time, Pallas kernels for 0%

commit v1 on v0

v1 whole, which is shorter than its diff:
```python
import functools

import jax
import jax.numpy as jnp
from jax import lax
from jax.experimental import pallas as pl
from jax.experimental.pallas import tpu as pltpu
from jax.sharding import PartitionSpec as P

CHUNK = 256
WIDE = jnp.float32
LOW = jnp.bfloat16
VMEM_BYTES = 56 * 1024 * 1024


def dot(left, right, left_dim=1, right_dim=0):
    return lax.dot_general(
        left, right, (((left_dim,), (right_dim,)), ((), ())), preferred_element_type=WIDE
    )


def decays(rate, place_col, place_row, chunk):
    rows = jnp.exp(-rate * place_col)
    cols = jnp.exp(rate * place_row)
    entry = jnp.exp(-rate * (place_col + 1.0))
    tail = jnp.exp(-rate * (chunk - 1.0 - place_col))
    return rows, cols, entry, tail


def masks(bounds_ref, seg_col, seg_row, n, chunk):
    before = bounds_ref[n]
    last = bounds_ref[n + 1]
    row = lax.broadcasted_iota(jnp.int32, (chunk, chunk), 0)
    col = lax.broadcasted_iota(jnp.int32, (chunk, chunk), 1)
    inner = (seg_col == seg_row) & (row >= col)
    return inner, seg_col == before, seg_col == last, jnp.where(before == last, 1.0, 0.0)


def places(chunk):
    place_col = lax.broadcasted_iota(jnp.int32, (chunk, 1), 0).astype(WIDE)
    place_row = lax.broadcasted_iota(jnp.int32, (1, chunk), 1).astype(WIDE)
    return place_col, place_row


def attend_kernel(
    heads, hd, rate_ref, bounds_ref, segc_ref, segr_ref, z_ref, au_ref, a_ref, ss_ref, st_ref, state
):
    n = pl.program_id(0)
    chunk = z_ref.shape[0]

    @pl.when(n == 0)
    def _():
        state[...] = jnp.zeros_like(state)

    inner, entry_on, tail_on, carry = masks(bounds_ref, segc_ref[...], segr_ref[...], n, chunk)
    place_col, place_row = places(chunk)
    total = jnp.zeros((chunk, 1), WIDE)
    for h in range(heads):
        rate = rate_ref[h]
        base = h * 4 * hd
        zq, zk, zv, zu = (z_ref[:, base + i * hd : base + (i + 1) * hd] for i in range(4))
        q = (zq * jax.nn.sigmoid(zq)).astype(LOW)
        k = (zk * jax.nn.sigmoid(zk)).astype(LOW)
        v = (zv * jax.nn.sigmoid(zv)).astype(LOW)
        u = zu * jax.nn.sigmoid(zu)
        rows, cols, entry, tail = decays(rate, place_col, place_row, chunk)
        scores = dot(q, k, 1, 1)
        weighted = jnp.where(inner, scores * rows * cols, 0.0).astype(LOW)
        held = state[h]
        st_ref[0, h] = held.astype(LOW)
        a = dot(weighted, v) + jnp.where(entry_on, entry, 0.0) * dot(q, held.astype(LOW))
        kt = (k.astype(WIDE) * jnp.where(tail_on, tail, 0.0)).astype(LOW)
        state[h] = carry * jnp.exp(jnp.full((1, 1), -rate * chunk, WIDE)) * held + dot(kt, v, 0, 0)
        a_ref[:, h * hd : (h + 1) * hd] = a
        au_ref[:, h * hd : (h + 1) * hd] = (a * u).astype(LOW)
        total = total + jnp.sum(a * a, axis=1, keepdims=True)
    ss_ref[...] = total


def attend(z, seg, bounds, rates, heads, hd):
    length = z.shape[0]
    count = length // CHUNK
    block = lambda width: pl.BlockSpec((CHUNK, width), lambda n, *_: (n, 0))
    return pl.pallas_call(
        functools.partial(attend_kernel, heads, hd),
        grid_spec=pltpu.PrefetchScalarGridSpec(
            num_scalar_prefetch=2,
            grid=(count,),
            in_specs=[
                block(1),
                pl.BlockSpec((1, CHUNK), lambda n, *_: (0, n)),
                block(heads * 4 * hd),
            ],
            out_specs=[
                block(heads * hd),
                block(heads * hd),
                block(1),
                pl.BlockSpec((1, heads, hd, hd), lambda n, *_: (n, 0, 0, 0)),
            ],
            scratch_shapes=[pltpu.VMEM((heads, hd, hd), WIDE)],
        ),
        out_shape=[
            jax.ShapeDtypeStruct((length, heads * hd), LOW),
            jax.ShapeDtypeStruct((length, heads * hd), WIDE),
            jax.ShapeDtypeStruct((length, 1), WIDE),
            jax.ShapeDtypeStruct((count, heads, hd, hd), LOW),
        ],
        compiler_params=pltpu.CompilerParams(vmem_limit_bytes=VMEM_BYTES),
        cost_estimate=pl.CostEstimate(
            flops=length * heads * hd * CHUNK * 6,
            bytes_accessed=length * heads * hd * 22,
            transcendentals=length * heads * hd * 4,
        ),
        name="attend",
    )(rates, bounds, seg.reshape(length, 1), seg.reshape(1, length), z)


def slope(z):
    sg = jax.nn.sigmoid(z)
    return sg * (1.0 + z * (1.0 - sg))


def attend_back_kernel(
    heads,
    hd,
    count,
    rate_ref,
    bounds_ref,
    segc_ref,
    segr_ref,
    z_ref,
    a_ref,
    dj_ref,
    ra_ref,
    m_ref,
    st_ref,
    dz_ref,
    o_ref,
    later,
):
    n = count - 1 - pl.program_id(0)
    chunk = z_ref.shape[0]

    @pl.when(pl.program_id(0) == 0)
    def _():
        later[...] = jnp.zeros_like(later)

    inner, entry_on, tail_on, carry = masks(bounds_ref, segc_ref[...], segr_ref[...], n, chunk)
    place_col, place_row = places(chunk)
    ra = ra_ref[...]
    m = m_ref[...]
    for h in range(heads):
        rate = rate_ref[h]
        base = h * 4 * hd
        span = slice(h * hd, (h + 1) * hd)
        zq, zk, zv, zu = (z_ref[:, base + i * hd : base + (i + 1) * hd] for i in range(4))
        q = (zq * jax.nn.sigmoid(zq)).astype(LOW)
        k = (zk * jax.nn.sigmoid(zk)).astype(LOW)
        v = (zv * jax.nn.sigmoid(zv)).astype(LOW)
        u = zu * jax.nn.sigmoid(zu)
        an = a_ref[:, span] * ra
        dj = dj_ref[:, span]
        o_ref[:, span] = (an * u).astype(LOW)
        da = (ra * (dj * u - an * m)).astype(LOW)
        rows, cols, entry, tail = decays(rate, place_col, place_row, chunk)
        entry = jnp.where(entry_on, entry, 0.0)
        tail = jnp.where(tail_on, tail, 0.0)
        decay = jnp.where(inner, rows * cols, 0.0)
        weighted = (dot(q, k, 1, 1) * decay).astype(LOW)
        grads = (dot(da, v, 1, 1) * decay).astype(LOW)
        held = st_ref[0, h]
        after = later[h]
        after_low = after.astype(LOW)
        dq = dot(grads, k) + entry * dot(da, held, 1, 1)
        dk = dot(grads, q, 0, 0) + tail * dot(v, after_low, 1, 1)
        dv = dot(weighted, da, 0, 0) + tail * dot(k, after_low)
        qe = (q.astype(WIDE) * entry).astype(LOW)
        later[h] = carry * jnp.exp(jnp.full((1, 1), -rate * chunk, WIDE)) * after + dot(qe, da, 0, 0)
        dz_ref[:, base : base + hd] = (dq * slope(zq)).astype(LOW)
        dz_ref[:, base + hd : base + 2 * hd] = (dk * slope(zk)).astype(LOW)
        dz_ref[:, base + 2 * hd : base + 3 * hd] = (dv * slope(zv)).astype(LOW)
        dz_ref[:, base + 3 * hd : base + 4 * hd] = (dj * an * slope(zu)).astype(LOW)


def attend_back(z, a, dj, ra, m, states, seg, bounds, rates, heads, hd):
    length = z.shape[0]
    count = length // CHUNK
    block = lambda width: pl.BlockSpec((CHUNK, width), lambda n, *_: (count - 1 - n, 0))
    return pl.pallas_call(
        functools.partial(attend_back_kernel, heads, hd, count),
        grid_spec=pltpu.PrefetchScalarGridSpec(
            num_scalar_prefetch=2,
            grid=(count,),
            in_specs=[
                block(1),
                pl.BlockSpec((1, CHUNK), lambda n, *_: (0, count - 1 - n)),
                block(heads * 4 * hd),
                block(heads * hd),
                block(heads * hd),
                block(1),
                block(1),
                pl.BlockSpec((1, heads, hd, hd), lambda n, *_: (count - 1 - n, 0, 0, 0)),
            ],
            out_specs=[block(heads * 4 * hd), block(heads * hd)],
            scratch_shapes=[pltpu.VMEM((heads, hd, hd), WIDE)],
        ),
        out_shape=[
            jax.ShapeDtypeStruct((length, heads * 4 * hd), LOW),
            jax.ShapeDtypeStruct((length, heads * hd), LOW),
        ],
        compiler_params=pltpu.CompilerParams(vmem_limit_bytes=VMEM_BYTES),
        cost_estimate=pl.CostEstimate(
            flops=length * heads * hd * CHUNK * 12,
            bytes_accessed=length * heads * hd * 34,
            transcendentals=length * heads * hd * 8,
        ),
        name="attend_back",
    )(rates, bounds, seg.reshape(length, 1), seg.reshape(1, length), z, a, dj, ra, m, states)


class Moves:
    def __init__(self):
        self.seq = lax.axis_size("seq")
        self.fsdp = lax.axis_size("fsdp")
        self.inner = 2 if self.fsdp == 8 else 4
        self.outer = self.fsdp // self.inner
        self.chips = self.seq // 2
        s = lax.axis_index("seq")
        f = lax.axis_index("fsdp")
        self.s, self.f = s, f
        self.chip, self.core = s // 2, s % 2
        self.out_at, self.in_at = f // self.inner, f % self.inner
        chips, inner, outer = self.chips, self.inner, self.outer
        self.core_perm = [(i, i ^ 1) for i in range(self.seq)]
        self.chip_perm = [
            (x * 2 + c, (x + 1) % chips * 2 + c) for x in range(chips) for c in range(2)
        ]
        self.out_perm = [
            (o * inner + i, (o + 1) % outer * inner + i)
            for o in range(outer)
            for i in range(inner)
        ]
        self.in_perm = [
            (o * inner + i, o * inner + (i + 1) % inner)
            for o in range(outer)
            for i in range(inner)
        ]

    def to_core(self, v):
        return lax.ppermute(v, "seq", self.core_perm)

    def to_chip(self, v):
        return lax.ppermute(v, "seq", self.chip_perm)

    def to_out(self, v):
        return lax.ppermute(v, "fsdp", self.out_perm)

    def to_in(self, v):
        return lax.ppermute(v, "fsdp", self.in_perm)

    def gather_seq(self, v):
        whole = jnp.zeros((self.seq,) + v.shape, v.dtype)
        now = v
        for k in range(self.chips):
            later = self.to_chip(now) if k < self.chips - 1 else None
            other = self.to_core(now)
            chip = (self.chip - k) % self.chips
            whole = lax.dynamic_update_index_in_dim(whole, now, chip * 2 + self.core, 0)
            whole = lax.dynamic_update_index_in_dim(whole, other, chip * 2 + 1 - self.core, 0)
            now = later
        return whole.reshape((-1,) + v.shape[1:])

    def scatter_seq(self, part, kind):
        held = None
        for k in range(self.chips):
            term = part((self.chip - 1 - k) % self.chips)
            give = lax.dynamic_index_in_dim(term, 1 - self.core, 0, False)
            keep = lax.dynamic_index_in_dim(term, self.core, 0, False)
            total = keep.astype(WIDE) + self.to_core(give).astype(WIDE)
            if held is not None:
                total = total + held.astype(WIDE)
            if k < self.chips - 1:
                held = self.to_chip(total.astype(kind))
        return total

    def swap_seq(self, blocks):
        pick = lambda i: lax.dynamic_index_in_dim(blocks, i, 0, False)
        whole = lax.dynamic_update_index_in_dim(jnp.zeros_like(blocks), pick(self.s), self.s, 0)
        for dx in range(self.chips):
            for dc in range(2):
                if dx == 0 and dc == 0:
                    continue
                to = (self.chip + dx) % self.chips * 2 + (self.core ^ dc)
                source = (self.chip - dx) % self.chips * 2 + (self.core ^ dc)
                perm = [
                    (x * 2 + c, (x + dx) % self.chips * 2 + (c ^ dc))
                    for x in range(self.chips)
                    for c in range(2)
                ]
                got = lax.ppermute(pick(to), "seq", perm)
                whole = lax.dynamic_update_index_in_dim(whole, got, source, 0)
        return whole

    def gather_fsdp(self, v):
        a, r, n = v.shape
        whole = jnp.zeros((a, self.fsdp, r, n), v.dtype)
        now = v
        for k in range(self.outer):
            later = self.to_out(now) if k < self.outer - 1 else None
            out_at = (self.out_at - k) % self.outer
            piece = now
            for j in range(self.inner):
                in_at = (self.in_at - j) % self.inner
                whole = lax.dynamic_update_slice_in_dim(
                    whole, piece[:, None], out_at * self.inner + in_at, 1
                )
                if j < self.inner - 1:
                    piece = self.to_in(piece)
            now = later
        return whole.reshape(a * self.fsdp * r, n)

    def scatter_fsdp(self, g, a):
        n = g.shape[1]
        r = g.shape[0] // (a * self.fsdp)
        g = g.reshape(a, self.fsdp, r, n)
        pick = lambda o, i: lax.dynamic_slice_in_dim(g, o * self.inner + i, 1, 1)[:, 0]
        held = None
        for k in range(self.outer):
            out_at = (self.out_at - 1 - k) % self.outer
            total = None
            for j in range(self.inner):
                term = pick(out_at, (self.in_at - 1 - j) % self.inner).astype(WIDE)
                total = term if total is None else term + self.to_in(total.astype(LOW)).astype(WIDE)
            if held is not None:
                total = total + held.astype(WIDE)
            if k < self.outer - 1:
                held = self.to_out(total.astype(LOW))
        return total

    def sum_all(self, v):
        for axis, size in (("seq", self.seq), ("fsdp", self.fsdp)):
            step = 1
            while step < size:
                v = v + lax.ppermute(v, axis, [(i, i ^ step) for i in range(size)])
                step *= 2
        return v


def on_device(
    inputs,
    teacher,
    segment_ids,
    valid,
    decay_rate,
    w_query,
    w_key,
    w_value,
    w_gate,
    w_out,
    w_first,
    w_second,
    w_down,
):
    move = Moves()
    seq = move.seq
    batch, block_len, width = inputs.shape
    assert batch == 1
    heads_all = decay_rate.shape[0]
    hd = width // heads_all
    heads = heads_all // seq
    own_rows = w_query.shape[0]
    ff = w_first.shape[1]
    ffs = ff // seq
    cols = heads * 4 * hd

    keep = valid.astype(WIDE).reshape(block_len, 1)
    count = move.sum_all(jnp.sum(keep).reshape(1, 1))

    seg = move.gather_seq(segment_ids.reshape(block_len))
    length = seg.shape[0]
    bounds = jnp.concatenate([jnp.full((1,), -1, jnp.int32), seg[CHUNK - 1 :: CHUNK]])
    rates = lax.dynamic_slice_in_dim(decay_rate, move.s * heads, heads, 0)

    attn_own = jnp.stack(
        [w.reshape(own_rows, seq, heads, hd) for w in (w_query, w_key, w_value, w_gate)], axis=3
    )
    attn_own = attn_own.reshape(own_rows, seq, cols).transpose(1, 0, 2)
    glu_own = jnp.stack([w_first.reshape(own_rows, seq, ffs), w_second.reshape(own_rows, seq, ffs)])
    glu_own = glu_own.transpose(2, 0, 1, 3)

    full_attn = move.gather_fsdp(move.swap_seq(attn_own))
    full_out = move.gather_fsdp(w_out[None])
    glu_mid = move.swap_seq(glu_own)
    full_first = move.gather_fsdp(glu_mid[:, 0])
    full_second = move.gather_fsdp(glu_mid[:, 1])
    full_down = move.gather_fsdp(w_down[None])

    x32 = inputs.reshape(block_len, width).astype(WIDE)
    r1 = lax.rsqrt(jnp.mean(x32 * x32, axis=-1, keepdims=True) + 1e-6)
    n1 = x32 * r1
    n1_all = move.gather_seq(n1.astype(LOW))
    z = dot(n1_all, full_attn)
    au, a, ss, states = attend(z, seg, bounds, rates, heads, hd)

    def rows_of(v, chip):
        return lax.dynamic_slice_in_dim(v, chip * 2 * block_len, 2 * block_len, 0)

    def scatter_product(pairs):
        def part(chip):
            total = sum(dot(rows_of(v, chip), w, 1, d) for v, w, d in pairs)
            return total.astype(LOW).reshape(2, block_len, -1)

        return move.scatter_seq(part, LOW)

    out_rows = scatter_product([(au, full_out, 0)])
    ss_own = move.scatter_seq(lambda chip: rows_of(ss, chip).reshape(2, block_len, 1), WIDE)
    ra = lax.rsqrt(ss_own / width + 1e-6)
    mixed_out = out_rows * ra
    hsum = x32 + mixed_out
    r2 = lax.rsqrt(jnp.mean(hsum * hsum, axis=-1, keepdims=True) + 1e-6)
    m2 = hsum * r2
    n2_all = move.gather_seq(m2.astype(LOW))

    g1 = dot(n2_all, full_first)
    g2 = dot(n2_all, full_second)
    p = (g1 * g2).astype(LOW)
    g1 = g1.astype(LOW)
    g2 = g2.astype(LOW)
    y = hsum + scatter_product([(p, full_down, 0)])
    layer_out = y.astype(LOW).reshape(1, block_len, width)

    error = y - teacher.reshape(block_len, width).astype(WIDE)
    loss = move.sum_all(jnp.sum(keep * error * error).reshape(1, 1)) / (width * count)
    tokens = block_len * seq * move.fsdp
    dy = tokens / count * keep * error
    dy_all = move.gather_seq(dy.astype(LOW))

    grad_down = dot(p, dy_all, 0, 0).astype(LOW)
    dp = dot(dy_all, full_down, 1, 1)
    dg1 = (dp * g2.astype(WIDE)).astype(LOW)
    dg2 = (dp * g1.astype(WIDE)).astype(LOW)
    dn2 = scatter_product([(dg1, full_first, 1), (dg2, full_second, 1)])
    grad_first = dot(n2_all, dg1, 0, 0).astype(LOW)
    grad_second = dot(n2_all, dg2, 0, 0).astype(LOW)
    dh = dy + r2 * (dn2 - m2 * jnp.mean(dn2 * m2, axis=-1, keepdims=True))
    dhb = dh.astype(LOW)
    mean_own = jnp.mean(dhb.astype(WIDE) * mixed_out, axis=-1, keepdims=True)
    dh_all = move.gather_seq(dhb)
    small = move.gather_seq(jnp.concatenate([ra, mean_own], axis=1))

    dj = dot(dh_all, full_out, 1, 1)
    dz, o = attend_back(
        z, a, dj, small[:, :1], small[:, 1:], states, seg, bounds, rates, heads, hd
    )
    grad_out = dot(o, dh_all, 0, 0).astype(LOW)
    grad_attn = dot(n1_all, dz, 0, 0).astype(LOW)
    dn1 = scatter_product([(dz, full_attn, 1)])
    input_grad = dh + r1 * (dn1 - n1 * jnp.mean(dn1 * n1, axis=-1, keepdims=True))

    share_down = move.scatter_fsdp(grad_down, 1)[0]
    share_first = move.scatter_fsdp(grad_first, seq).astype(LOW)
    share_second = move.scatter_fsdp(grad_second, seq).astype(LOW)
    share_first = move.swap_seq(share_first).transpose(1, 0, 2).reshape(own_rows, ff).astype(WIDE)
    share_second = move.swap_seq(share_second).transpose(1, 0, 2).reshape(own_rows, ff).astype(WIDE)
    share_out = move.scatter_fsdp(grad_out, 1)[0]
    share_attn = move.swap_seq(move.scatter_fsdp(grad_attn, seq).astype(LOW))
    share_attn = share_attn.reshape(seq, own_rows, heads, 4, hd).transpose(3, 1, 0, 2, 4)
    share_attn = share_attn.reshape(4, own_rows, width).astype(WIDE)

    return (
        layer_out,
        loss.reshape(()),
        input_grad.reshape(1, block_len, width),
        share_attn[0],
        share_attn[1],
        share_attn[2],
        share_attn[3],
        share_out,
        share_first,
        share_second,
        share_down,
    )


def solution(mesh):
    rows = P(("seq", "fsdp"), None)
    tokens = P("fsdp", "seq", None)
    return jax.shard_map(
        on_device,
        mesh=mesh,
        in_specs=(tokens, tokens, P("fsdp", "seq"), P("fsdp", "seq"), P()) + (rows,) * 8,
        out_specs=(tokens, P(), tokens) + (rows,) * 8,
        check_vma=False,
    )
```

time: 5820 us -> 1480 us (0.25)
  waiting for transfers between devices: 5150 us -> 758 us
  matrix products: 469 us -> 272 us
  starting transfers between devices: 0.72 us -> 150 us
  local copies, waits for them, and re-layouts: 56.6 us -> 175 us
    reduce_scatter x8 -> x0, waiting for transfers between devices: 4460 us -> none  [the longest x1 970 us: on_device(): lax.psum_scatter(grad_w_down, ('seq', 'fsdp'), scatter_dimension=0, tiled...]
    ppermute x0 -> x128, waiting for transfers between devices: none -> 758 us  [the longest x40 328 us: to_in(): return lax.ppermute(v, 'fsdp', self.in_perm)]
    all_gather x10 -> x0, waiting for transfers between devices: 688 us -> none  [the longest x1 136 us: on_device(): lax.all_gather(w_second, ('seq', 'fsdp'), axis=0, tiled=True)]
    dot_general x36 -> x20, matrix products: 469 us -> 272 us  [dot(): lax.dot_general(left, right, (((left_dim,), (right_dim,)), ((), ())), pre...]
    ppermute x0 -> x128, starting transfers between devices: none -> 150 us  [the longest x10 68 us: sum_all(): v = v + lax.ppermute(v, axis, [(i, i ^ step) for i in range(size)])]
    dynamic_update_slice x0 -> x78, local copies, waits for them, and re-layouts: none -> 87.7 us  [the longest x39 34.4 us: gather_fsdp(): lax.dynamic_update_slice_in_dim(whole, piece[:, None], out_at * self.inne...]
  transfers between devices with their start and end apart: 18 -> 128, of which waited for: 16 -> 55; matrix products, arithmetic and copies ran while one was open for 7% -> 22% of each run, Pallas kernels for 0% -> 3%
where the time goes in v1:
time: 1480 us; the launch traced here: 1470 us
  waiting for transfers between devices  758 us (51%)
  matrix products  272 us (18%)
  local copies, waits for them, and re-layouts  175 us (12%)
  starting transfers between devices  150 us (10%)
  other arithmetic  66 us (4%)
  Pallas kernels  37.8 us (3%)
    ppermute x40, waiting for transfers between devices, to_in(): return lax.ppermute(v, 'fsdp', self.in_perm)  328 us
    dot_general x20, matrix products, dot(): lax.dot_general(left, right, (((left_dim,), (right_dim,)), ((), ())), pre...  272 us
    ppermute x30, waiting for transfers between devices, to_out(): return lax.ppermute(v, 'fsdp', self.out_perm)  201 us
    ppermute x11, waiting for transfers between devices, to_chip(): return lax.ppermute(v, 'seq', self.chip_perm)  140 us
    ppermute x15, waiting for transfers between devices, swap_seq(): got = lax.ppermute(pick(to), 'seq', perm)  80 us
    ppermute x10, starting transfers between devices, sum_all(): v = v + lax.ppermute(v, axis, [(i, i ^ step) for i in range(size)])  68 us
    ppermute x40, starting transfers between devices, to_in(): return lax.ppermute(v, 'fsdp', self.in_perm)  43.9 us
    dynamic_update_slice x39, local copies, waits for them, and re-layouts, gather_fsdp(): lax.dynamic_update_slice_in_dim(whole, piece[:, None], out_at * self.inne...  34.4 us
  transfers between devices with their start and end apart: 128, of which 55 were waited for; matrix products, arithmetic and copies ran while one was open for 22% of the time, Pallas kernels for 3%

profile of v1, /device:TPU:0, one launch (start us, length us, event | category | flops | bytes accessed | tf_op | source)
XLA Modules:
  0.0 1470.9 jit_solution(10797113275796917883)
XLA Ops:
  62.8 46.0 %collective-permute-done.7 = bf16[64,2048]{1,0:T(8,128)(2,1)S(1)} collective-permute-done((bf16[64,2048]{1,0:T(8,128)(2,1)}, bf16[64,2048]{1,0:T(8,128)(2,1)S(1)}, u32[]{:S(2)}, u32[]{:S(2)}) %collective-permute-start.7) | collective-permute-done | bytes 262176 | tf_op jit(solution)/shard_map/ppermute | solution.py:300
  171.9 25.1 %collective-permute-done.20 = bf16[1,64,2048]{2,1,0:T(8,128)(2,1)S(1)} collective-permute-done((bf16[1,64,2048]{2,1,0:T(8,128)(2,1)S(1)}, bf16[1,64,2048]{2,1,0:T(8,128)(2,1)S(1)}, u32[]{:S(2)}, u32[]{:S(2)}) %collective-permute-start.20) | collective-permute-done | bytes 262176 | tf_op jit(solution)/shard_map/ppermute | solution.py:259
  200.5 18.1 %collective-permute-done.22 = bf16[1,64,2048]{2,1,0:T(8,128)(2,1)S(1)} collective-permute-done((bf16[1,64,2048]{2,1,0:T(8,128)(2,1)S(1)}, bf16[1,64,2048]{2,1,0:T(8,128)(2,1)S(1)}, u32[]{:S(2)}, u32[]{:S(2)}) %collective-permute-start.22) | collective-permute-done | bytes 262176 | tf_op jit(solution)/shard_map/ppermute | solution.py:259
  220.8 14.6 collective-permute-done.43
  237.3 19.0 %collective-permute-done.36 = bf16[4,64,1408]{2,1,0:T(8,128)(2,1)S(1)} collective-permute-done((bf16[4,64,1408]{2,1,0:T(8,128)(2,1)S(1)}, bf16[4,64,1408]{2,1,0:T(8,128)(2,1)S(1)}, u32[]{:S(2)}, u32[]{:S(2)}) %collective-permute-start.36) | collective-permute-done | bytes 720928 | tf_op jit(solution)/shard_map/ppermute | solution.py:256
  257.9 20.8 %collective-permute-done.10 = bf16[4,64,2048]{2,1,0:T(8,128)(2,1)S(1)} collective-permute-done((bf16[4,64,2048]{2,1,0:T(8,128)(2,1)}, bf16[4,64,2048]{2,1,0:T(8,128)(2,1)S(1)}, u32[]{:S(2)}, u32[]{:S(2)}) %collective-permute-start.10) | collective-permute-done | bytes 1048608 | tf_op jit(solution)/shard_map/ppermute | solution.py:256
  280.5 13.7 collective-permute-done.52
  297.6 14.2 collective-permute-done.12
  315.8 19.4 %collective-permute-done.13 = bf16[4,64,2048]{2,1,0:T(8,128)(2,1)S(1)} collective-permute-done((bf16[4,64,2048]{2,1,0:T(8,128)(2,1)S(1)}, bf16[4,64,2048]{2,1,0:T(8,128)(2,1)S(1)}, u32[]{:S(2)}, u32[]{:S(2)}) %collective-permute-start.13) | collective-permute-done | bytes 1048608 | tf_op jit(solution)/shard_map/ppermute | solution.py:259
  342.4 31.6 %collective-permute-done.15 = bf16[4,64,2048]{2,1,0:T(8,128)(2,1)S(1)} collective-permute-done((bf16[4,64,2048]{2,1,0:T(8,128)(2,1)S(1)}, bf16[4,64,2048]{2,1,0:T(8,128)(2,1)S(1)}, u32[]{:S(2)}, u32[]{:S(2)}) %collective-permute-start.15) | collective-permute-done | bytes 1048608 | tf_op jit(solution)/shard_map/ppermute | solution.py:259
  374.7 20.7 %fusion.102.z_ref = f32[2048,2048]{1,0:T(8,128)} fusion(bf16[2048,2048]{1,0:T(8,128)(2,1)S(1)} %bitcast.563, bf16[2048,2048]{1,0:T(8,128)(2,1)S(1)} %bitcast.567), kind=kOutput, calls=%fused_computation.294 | convolution fusion | flops 17179869184 | bytes 33554432 | tf_op jit(solution)/shard_map/dot_general | solution.py:17
  395.4 16.3 %attend.1 = (bf16[2048,512]{1,0:T(8,128)(2,1)}, f32[2048,512]{1,0:T(8,128)}, f32[2048,1]{1,0:T(8,128)}, bf16[8,4,128,128]{3,2,1,0:T(8,128)(2,1)}) custom-call(f32[4]{0:T(128)} %dynamic_slice.272.rate_ref, s32[9]{0:T(128)} %pad_add_fusion.bounds_ref, s32[2048,1]{1,0:T(8,128)} %bitcast.537, s32[1,2048]{1,0:T(1,128)} %bitcast.620, f32[2048,2048]{1,0:T(8,128)} %fusion.102.z_ref), custom_call_target="tpu_custom_call" | custom-call | flops 1610612736 | bytes 23068672 | tf_op jit(solution)/shard_map/attend/pallas_call | solution.py:84
  442.1 33.5 %collective-permute-done.28 = f32[512,1]{0,1:T(1,128)S(1)} collective-permute-done((f32[512,1]{0,1:T(1,128)S(1)}, f32[512,1]{0,1:T(1,128)S(1)}, u32[]{:S(2)}, u32[]{:S(2)}) %collective-permute-start.28) | collective-permute-done | bytes 2080 | tf_op jit(solution)/shard_map/ppermute | solution.py:253
  498.5 11.6 collective-permute-done.39
  512.0 13.6 collective-permute-done.55
  526.5 12.2 collective-permute-done.30
  541.9 12.7 collective-permute-done.41
  556.5 19.1 %fusion.103 = f32[2048,1408]{1,0:T(8,128)} fusion(bf16[2048,2048]{1,0:T(8,128)(2,1)S(1)} %bitcast.555, bf16[2048,1408]{1,0:T(8,128)(2,1)} %bitcast.92), kind=kOutput, calls=%fused_computation.295 | convolution fusion | flops 11811160064 | bytes 25690112 | tf_op jit(solution)/shard_map/dot_general | solution.py:17
  575.6 20.4 %multiply_convert_fusion.2 = (bf16[2048,1408]{1,0:T(8,128)(2,1)S(1)}, bf16[2048,1408]{1,0:T(8,128)(2,1)}) fusion(f32[2048,1408]{1,0:T(8,128)} %fusion.103, bf16[2048,2048]{1,0:T(8,128)(2,1)} %bitcast.556, bf16[2048,1408]{1,0:T(8,128)(2,1)} %bitcast.76), kind=kOutput, calls=%fused_computation.2 | convolution fusion | flops 11819810816 | bytes 37224448 | tf_op jit(solution)/shard_map/dot_general | solution.py:17
  623.3 41.8 %collective-permute-start.65 = (f32[1,1]{1,0:T(1,128)}, f32[1,1]{1,0:T(1,128)}, u32[]{:S(2)}, u32[]{:S(2)}) collective-permute-start(f32[1,1]{1,0:T(1,128)} %add.943), channel_id=1, source_target_pairs={{0,16},{8,24},{16,0},{24,8},{1,17},{9,25},{17,1},{25,9},{2,18},{10... | collective-permute-start | bytes 20 | tf_op jit(solution)/shard_map/ppermute | solution.py:344
  695.4 43.4 %collective-permute-done.70 = bf16[512,2048]{1,0:T(8,128)(2,1)S(1)} collective-permute-done((bf16[512,2048]{1,0:T(8,128)(2,1)}, bf16[512,2048]{1,0:T(8,128)(2,1)S(1)}, u32[]{:S(2)}, u32[]{:S(2)}) %collective-permute-start.70) | collective-permute-done | bytes 2097184 | tf_op jit(solution)/shard_map/ppermute | solution.py:253
  746.7 24.3 %multiply_convert_fusion.1 = (bf16[2048,1408]{1,0:T(8,128)(2,1)}, bf16[2048,1408]{1,0:T(8,128)(2,1)}) fusion(f32[2048,1408]{1,0:T(8,128)} %fusion.103, bf16[2048,1408]{1,0:T(8,128)(2,1)} %get-tuple-element.90, bf16[2048,2048]{1,0:T(8,128)(2,1)} %bitcast.551, bf16[1408,2048]{1,0:T(8,128)(2,1)} %bitcast.102), kind=kOutput, calls=%fused_computation.1 | convolution fusion | flops 11831345152 | bytes 42991616 | tf_op jit(solution)/shard_map/dot_general | solution.py:17
  771.0 11.9 fusion.34
  782.9 10.9 fusion.37
  793.9 16.3 %convolution_convert_fusion.2 = bf16[2048,1408]{1,0:T(8,128)(2,1)S(1)} fusion(bf16[2048,2048]{1,0:T(8,128)(2,1)S(1)} %bitcast.559, bf16[2048,1408]{1,0:T(8,128)(2,1)} %get-tuple-element.36), kind=kOutput, calls=%fused_computation.7 | convolution fusion | flops 11814043648 | bytes 19922944 | tf_op jit(solution)/shard_map/dot_general | solution.py:17
  810.2 14.2 convolution_convert_fusion.1
  824.4 16.0 %convolution_convert_fusion.3 = bf16[2048,1408]{1,0:T(8,128)(2,1)S(1)} fusion(bf16[2048,2048]{1,0:T(8,128)(2,1)S(1)} %bitcast.560, bf16[2048,1408]{1,0:T(8,128)(2,1)} %get-tuple-element.35), kind=kOutput, calls=%fused_computation.8 | convolution fusion | flops 11814043648 | bytes 19922944 | tf_op jit(solution)/shard_map/dot_general | solution.py:17
  840.4 11.3 add_convert_fusion
  855.3 11.2 add_convert_fusion.1
  871.8 14.1 collective-permute-done.114
  887.5 29.2 %collective-permute-done.104 = bf16[4,64,1408]{2,1,0:T(8,128)(2,1)S(1)} collective-permute-done((bf16[4,64,1408]{2,1,0:T(8,128)(2,1)S(1)}, bf16[4,64,1408]{2,1,0:T(8,128)(2,1)S(1)}, u32[]{:S(2)}, u32[]{:S(2)}) %collective-permute-start.104) | collective-permute-done | bytes 720928 | tf_op jit(solution)/shard_map/ppermute | solution.py:259
  917.2 29.6 %collective-permute-done.124 = bf16[1,176,2048]{2,1,0:T(8,128)(2,1)S(1)} collective-permute-done((bf16[1,176,2048]{2,1,0:T(8,128)(2,1)S(1)}, bf16[1,176,2048]{2,1,0:T(8,128)(2,1)S(1)}, u32[]{:S(2)}, u32[]{:S(2)}) %collective-permute-start.124) | collective-permute-done | bytes 720928 | tf_op jit(solution)/shard_map/ppermute | solution.py:259
  952.6 15.0 %collective-permute-done.105 = bf16[4,64,1408]{2,1,0:T(8,128)(2,1)S(1)} collective-permute-done((bf16[4,64,1408]{2,1,0:T(8,128)(2,1)S(1)}, bf16[4,64,1408]{2,1,0:T(8,128)(2,1)S(1)}, u32[]{:S(2)}, u32[]{:S(2)}) %collective-permute-start.105) | collective-permute-done | bytes 720928 | tf_op jit(solution)/shard_map/ppermute | solution.py:256
  969.5 13.6 collective-permute-done.125
  985.0 13.5 collective-permute-done.116
  1000.9 11.3 collective-permute-done.106
  1018.4 23.2 %collective-permute-done.122 = bf16[1,176,2048]{2,1,0:T(8,128)(2,1)S(1)} collective-permute-done((bf16[1,176,2048]{2,1,0:T(8,128)(2,1)S(1)}, bf16[1,176,2048]{2,1,0:T(8,128)(2,1)S(1)}, u32[]{:S(2)}, u32[]{:S(2)}) %collective-permute-start.122) | collective-permute-done | bytes 720928 | tf_op jit(solution)/shard_map/ppermute | solution.py:259
  1048.5 15.4 %collective-permute-done.107 = bf16[4,64,1408]{2,1,0:T(8,128)(2,1)S(1)} collective-permute-done((bf16[4,64,1408]{2,1,0:T(8,128)(2,1)S(1)}, bf16[4,64,1408]{2,1,0:T(8,128)(2,1)S(1)}, u32[]{:S(2)}, u32[]{:S(2)}) %collective-permute-start.107) | collective-permute-done | bytes 720928 | tf_op jit(solution)/shard_map/ppermute | solution.py:256
  1107.0 40.4 %collective-permute-done.76 = bf16[512,2048]{1,0:T(8,128)(2,1)S(1)} collective-permute-done((bf16[512,2048]{1,0:T(8,128)(2,1)}, bf16[512,2048]{1,0:T(8,128)(2,1)S(1)}, u32[]{:S(2)}, u32[]{:S(2)}) %collective-permute-start.76) | collective-permute-done | bytes 2097184 | tf_op jit(solution)/shard_map/ppermute | solution.py:253
  1185.3 21.6 %attend_back.1 = (bf16[2048,2048]{1,0:T(8,128)(2,1)}, bf16[2048,512]{1,0:T(8,128)(2,1)}) custom-call(f32[4]{0:T(128)} %dynamic_slice.272.rate_ref, s32[9]{0:T(128)} %pad_add_fusion.bounds_ref, s32[2048,1]{1,0:T(8,128)} %bitcast.538, s32[1,2048]{1,0:T(1,128)} %bitcast.621, f32[2048,2048]{1,0:T(8,128)} %fusion.102.z_ref, f32[2048,512]{1,0:T(8,128)} %get-tuple-element.19.a_ref, ...), custom_call_target="tpu_custom_call" | custom-call | flops 3221225472 | bytes 35651584 | tf_op jit(solution)/shard_map/attend_back/pallas_call | solution.py:189
  1206.8 14.2 fusion.31
  1221.1 11.1 fusion.28
  1232.2 22.8 %convolution_convert_fusion = bf16[2048,2048]{1,0:T(8,128)(2,1)S(1)} fusion(bf16[2048,2048]{1,0:T(8,128)(2,1)S(1)} %bitcast.566, bf16[2048,2048]{1,0:T(8,128)(2,1)} %get-tuple-element.21), kind=kOutput, calls=%fused_computation.5 | convolution fusion | flops 17184063488 | bytes 25165824 | tf_op jit(solution)/shard_map/dot_general | solution.py:17
  1269.9 13.4 collective-permute-done.87
  1287.2 23.6 %collective-permute-done.97 = bf16[1,64,2048]{2,1,0:T(8,128)(2,1)S(1)} collective-permute-done((bf16[1,64,2048]{2,1,0:T(8,128)(2,1)S(1)}, bf16[1,64,2048]{2,1,0:T(8,128)(2,1)S(1)}, u32[]{:S(2)}, u32[]{:S(2)}) %collective-permute-start.97) | collective-permute-done | bytes 262176 | tf_op jit(solution)/shard_map/ppermute | solution.py:259
  1329.0 26.5 %collective-permute-done.95 = bf16[1,64,2048]{2,1,0:T(8,128)(2,1)S(1)} collective-permute-done((bf16[1,64,2048]{2,1,0:T(8,128)(2,1)S(1)}, bf16[1,64,2048]{2,1,0:T(8,128)(2,1)S(1)}, u32[]{:S(2)}, u32[]{:S(2)}) %collective-permute-start.95) | collective-permute-done | bytes 262176 | tf_op jit(solution)/shard_map/ppermute | solution.py:259
  1394.0 24.4 %collective-permute-done.94 = bf16[1,64,2048]{2,1,0:T(8,128)(2,1)S(1)} collective-permute-done((bf16[1,64,2048]{2,1,0:T(8,128)(2,1)S(1)}, bf16[1,64,2048]{2,1,0:T(8,128)(2,1)S(1)}, u32[]{:S(2)}, u32[]{:S(2)}) %collective-permute-start.94) | collective-permute-done | bytes 262176 | tf_op jit(solution)/shard_map/ppermute | solution.py:259
  1423.7 20.2 %collective-permute-done.90 = bf16[4,64,2048]{2,1,0:T(8,128)(2,1)S(1)} collective-permute-done((bf16[4,64,2048]{2,1,0:T(8,128)(2,1)S(1)}, bf16[4,64,2048]{2,1,0:T(8,128)(2,1)S(1)}, u32[]{:S(2)}, u32[]{:S(2)}) %collective-permute-start.90) | collective-permute-done | bytes 1048608 | tf_op jit(solution)/shard_map/ppermute | solution.py:256
  (578 shorter events, 492.2 us)
Async XLA Ops:
  0.7 120.2 %collective-permute-start.16 = (bf16[1,64,2048]{2,1,0:T(8,128)(2,1)}, bf16[1,64,2048]{2,1,0:T(8,128)(2,1)}, u32[]{:S(2)}, u32[]{:S(2)}) collective-permute-start(bf16[1,64,2048]{2,1,0:T(8,128)(2,1)} %bitcast.615), channel_id=1, source_target_pairs={{0,1},{1,0},{2,3},{3,2},{4,5},{5,4},{6,7},{7,6},{8,9},{9,8},{10,11... | collective-permute-start | bytes 786440 | tf_op jit(solution)/shard_map/ppermute | solution.py:259
  3.7 120.5 %collective-permute-start.17 = (bf16[1,64,2048]{2,1,0:T(8,128)(2,1)}, bf16[1,64,2048]{2,1,0:T(8,128)(2,1)}, u32[]{:S(2)}, u32[]{:S(2)}) collective-permute-start(bf16[1,64,2048]{2,1,0:T(8,128)(2,1)} %bitcast.616), channel_id=1, source_target_pairs={{0,2},{1,3},{2,4},{3,5},{4,6},{5,7},{6,0},{7,1},{8,10},{9,11},{10,... | collective-permute-start | bytes 786440 | tf_op jit(solution)/shard_map/ppermute | solution.py:256
  5.3 48.7 %collective-permute-start = (s32[512]{0:T(512)}, s32[512]{0:T(512)S(1)}, u32[]{:S(2)}, u32[]{:S(2)}) collective-permute-start(s32[512]{0:T(512)} %bitcast.633), channel_id=1, source_target_pairs={{0,8},{8,0},{16,24},{24,16},{1,9},{9,1},{17,25},{25,17},{2,10},{10... | collective-permute-start | bytes 6152 | tf_op jit(solution)/shard_map/ppermute | solution.py:250
  54.0 241.7 %collective-permute-start.3 = (bf16[512,2048]{1,0:T(8,128)(2,1)}, bf16[512,2048]{1,0:T(8,128)(2,1)}, u32[]{:S(2)}, u32[]{:S(2)}) collective-permute-start(bf16[512,2048]{1,0:T(8,128)(2,1)} %fusion.5), channel_id=1, source_target_pairs={{0,8},{8,0},{16,24},{24,16},{1,9},{9,1},{17,25},{25,17},{2,10},{10... | collective-permute-start | bytes 6291464 | tf_op jit(solution)/shard_map/ppermute | solution.py:250
  55.0 240.7 %collective-permute-start.4 = (bf16[512,2048]{1,0:T(8,128)(2,1)}, bf16[512,2048]{1,0:T(8,128)(2,1)}, u32[]{:S(2)}, u32[]{:S(2)}) collective-permute-start(bf16[512,2048]{1,0:T(8,128)(2,1)} %fusion.5), channel_id=1, source_target_pairs={{0,16},{8,24},{16,0},{24,8},{1,17},{9,25},{17,1},{25,9},{2,18},{10... | collective-permute-start | bytes 6291464 | tf_op jit(solution)/shard_map/ppermute | solution.py:253
  59.6 49.1 %collective-permute-start.7 = (bf16[64,2048]{1,0:T(8,128)(2,1)}, bf16[64,2048]{1,0:T(8,128)(2,1)S(1)}, u32[]{:S(2)}, u32[]{:S(2)}) collective-permute-start(bf16[64,2048]{1,0:T(8,128)(2,1)} %get-tuple-element.77), channel_id=1, source_target_pairs={{0,16},{8,24},{16,0},{24,8},{1,17},{9,25},{17,1},{25,9},{2,18},{10... | collective-permute-start | bytes 786440 | tf_op jit(solution)/shard_map/ppermute | solution.py:300
  117.2 51.4 %collective-permute-start.49 = (bf16[1,176,2048]{2,1,0:T(8,128)(2,1)}, bf16[1,176,2048]{2,1,0:T(8,128)(2,1)S(1)}, u32[]{:S(2)}, u32[]{:S(2)}) collective-permute-start(bf16[1,176,2048]{2,1,0:T(8,128)(2,1)} %bitcast.610), channel_id=1, source_target_pairs={{0,1},{1,0},{2,3},{3,2},{4,5},{5,4},{6,7},{7,6},{8,9},{9,8},{10,11... | collective-permute-start | bytes 2162696 | tf_op jit(solution)/shard_map/ppermute | solution.py:259
  120.9 50.1 %collective-permute-start.50 = (bf16[1,176,2048]{2,1,0:T(8,128)(2,1)S(1)}, bf16[1,176,2048]{2,1,0:T(8,128)(2,1)S(1)}, u32[]{:S(2)}, u32[]{:S(2)}) collective-permute-start(bf16[1,176,2048]{2,1,0:T(8,128)(2,1)S(1)} %bitcast.611), channel_id=1, source_target_pairs={{0,2},{1,3},{2,4},{3,5},{4,6},{5,7},{6,0},{7,1},{8,10},{9,11},{10,... | collective-permute-start | bytes 2162696 | tf_op jit(solution)/shard_map/ppermute | solution.py:256
  167.3 90.5 %collective-permute-start.9 = (bf16[4,64,2048]{2,1,0:T(8,128)(2,1)}, bf16[4,64,2048]{2,1,0:T(8,128)(2,1)S(1)}, u32[]{:S(2)}, u32[]{:S(2)}) collective-permute-start(bf16[4,64,2048]{2,1,0:T(8,128)(2,1)} %bitcast_dynamic-update-slice_fusion.60), channel_id=1, source_target_pairs={{0,1},{1,0},{2,3},{3,2},{4,5},{5,4},{6,7},{7,6},{8,9},{9,8},{10,11... | collective-permute-start | bytes 3145736 | tf_op jit(solution)/shard_map/ppermute | solution.py:259
  278.8 137.4 %collective-permute-start.44 = (bf16[4,64,1408]{2,1,0:T(8,128)(2,1)S(1)}, bf16[4,64,1408]{2,1,0:T(8,128)(2,1)S(1)}, u32[]{:S(2)}, u32[]{:S(2)}) collective-permute-start(bf16[4,64,1408]{2,1,0:T(8,128)(2,1)S(1)} %collective-permute-done.43), channel_id=1, source_target_pairs={{0,1},{1,0},{2,3},{3,2},{4,5},{5,4},{6,7},{7,6},{8,9},{9,8},{10,11... | collective-permute-start | bytes 2162696 | tf_op jit(solution)/shard_map/ppermute | solution.py:259
  295.7 46.3 %collective-permute-start.5 = (bf16[512,2048]{1,0:T(8,128)(2,1)}, bf16[512,2048]{1,0:T(8,128)(2,1)S(1)}, u32[]{:S(2)}, u32[]{:S(2)}) collective-permute-start(bf16[512,2048]{1,0:T(8,128)(2,1)} %collective-permute-done.4), channel_id=1, source_target_pairs={{0,8},{8,0},{16,24},{24,16},{1,9},{9,1},{17,25},{25,17},{2,10},{10... | collective-permute-start | bytes 6291464 | tf_op jit(solution)/shard_map/ppermute | solution.py:250
  315.5 101.7 %collective-permute-start.45 = (bf16[4,64,1408]{2,1,0:T(8,128)(2,1)S(1)}, bf16[4,64,1408]{2,1,0:T(8,128)(2,1)S(1)}, u32[]{:S(2)}, u32[]{:S(2)}) collective-permute-start(bf16[4,64,1408]{2,1,0:T(8,128)(2,1)S(1)} %collective-permute-done.43), channel_id=1, source_target_pairs={{0,2},{1,3},{2,4},{3,5},{4,6},{5,7},{6,0},{7,1},{8,10},{9,11},{10,... | collective-permute-start | bytes 2162696 | tf_op jit(solution)/shard_map/ppermute | solution.py:256
  335.2 83.0 %collective-permute-start.37 = (bf16[4,64,1408]{2,1,0:T(8,128)(2,1)S(1)}, bf16[4,64,1408]{2,1,0:T(8,128)(2,1)S(1)}, u32[]{:S(2)}, u32[]{:S(2)}) collective-permute-start(bf16[4,64,1408]{2,1,0:T(8,128)(2,1)S(1)} %collective-permute-done.36), channel_id=1, source_target_pairs={{0,1},{1,0},{2,3},{3,2},{4,5},{5,4},{6,7},{7,6},{8,9},{9,8},{10,11... | collective-permute-start | bytes 2162696 | tf_op jit(solution)/shard_map/ppermute | solution.py:259
  342.0 85.6 %collective-permute-start.38 = (bf16[4,64,1408]{2,1,0:T(8,128)(2,1)S(1)}, bf16[4,64,1408]{2,1,0:T(8,128)(2,1)S(1)}, u32[]{:S(2)}, u32[]{:S(2)}) collective-permute-start(bf16[4,64,1408]{2,1,0:T(8,128)(2,1)S(1)} %collective-permute-done.36), channel_id=1, source_target_pairs={{0,2},{1,3},{2,4},{3,5},{4,6},{5,7},{6,0},{7,1},{8,10},{9,11},{10,... | collective-permute-start | bytes 2162696 | tf_op jit(solution)/shard_map/ppermute | solution.py:256
  374.0 55.5 %collective-permute-start.53 = (bf16[1,176,2048]{2,1,0:T(8,128)(2,1)S(1)}, bf16[1,176,2048]{2,1,0:T(8,128)(2,1)S(1)}, u32[]{:S(2)}, u32[]{:S(2)}) collective-permute-start(bf16[1,176,2048]{2,1,0:T(8,128)(2,1)S(1)} %collective-permute-done.52), channel_id=1, source_target_pairs={{0,1},{1,0},{2,3},{3,2},{4,5},{5,4},{6,7},{7,6},{8,9},{9,8},{10,11... | collective-permute-start | bytes 2162696 | tf_op jit(solution)/shard_map/ppermute | solution.py:259
  418.2 58.9 %collective-permute-start.47 = (bf16[4,64,1408]{2,1,0:T(8,128)(2,1)S(1)}, bf16[4,64,1408]{2,1,0:T(8,128)(2,1)}, u32[]{:S(2)}, u32[]{:S(2)}) collective-permute-start(bf16[4,64,1408]{2,1,0:T(8,128)(2,1)S(1)} %collective-permute-done.45), channel_id=1, source_target_pairs={{0,2},{1,3},{2,4},{3,5},{4,6},{5,7},{6,0},{7,1},{8,10},{9,11},{10,... | collective-permute-start | bytes 2162696 | tf_op jit(solution)/shard_map/ppermute | solution.py:256
  425.0 54.2 %collective-permute-start.23 = (bf16[512,2048]{1,0:T(8,128)(2,1)}, bf16[512,2048]{1,0:T(8,128)(2,1)}, u32[]{:S(2)}, u32[]{:S(2)}) collective-permute-start(bf16[512,2048]{1,0:T(8,128)(2,1)} %dynamic-slice_bitcast_fusion.7), channel_id=1, source_target_pairs={{0,8},{8,0},{16,24},{24,16},{1,9},{9,1},{17,25},{25,17},{2,10},{10... | collective-permute-start | bytes 6291464 | tf_op jit(solution)/shard_map/ppermute | solution.py:250
  427.6 52.1 %collective-permute-start.25 = (bf16[512,2048]{1,0:T(8,128)(2,1)}, bf16[512,2048]{1,0:T(8,128)(2,1)}, u32[]{:S(2)}, u32[]{:S(2)}) collective-permute-start(bf16[512,2048]{1,0:T(8,128)(2,1)} %fusion.21), channel_id=1, source_target_pairs={{0,16},{8,24},{16,0},{24,8},{1,17},{9,25},{17,1},{25,9},{2,18},{10... | collective-permute-start | bytes 6291464 | tf_op jit(solution)/shard_map/ppermute | solution.py:253
  477.7 47.8 %collective-permute-start.55 = (bf16[1,176,2048]{2,1,0:T(8,128)(2,1)}, bf16[1,176,2048]{2,1,0:T(8,128)(2,1)S(1)}, u32[]{:S(2)}, u32[]{:S(2)}) collective-permute-start(bf16[1,176,2048]{2,1,0:T(8,128)(2,1)} %collective-permute-done.54), channel_id=1, source_target_pairs={{0,1},{1,0},{2,3},{3,2},{4,5},{5,4},{6,7},{7,6},{8,9},{9,8},{10,11... | collective-permute-start | bytes 2162696 | tf_op jit(solution)/shard_map/ppermute | solution.py:259
  479.2 61.8 %collective-permute-start.48 = (bf16[4,64,1408]{2,1,0:T(8,128)(2,1)}, bf16[4,64,1408]{2,1,0:T(8,128)(2,1)S(1)}, u32[]{:S(2)}, u32[]{:S(2)}) collective-permute-start(bf16[4,64,1408]{2,1,0:T(8,128)(2,1)} %collective-permute-done.47), channel_id=1, source_target_pairs={{0,1},{1,0},{2,3},{3,2},{4,5},{5,4},{6,7},{7,6},{8,9},{9,8},{10,11... | collective-permute-start | bytes 2162696 | tf_op jit(solution)/shard_map/ppermute | solution.py:259
  479.8 74.9 %collective-permute-start.41 = (bf16[4,64,1408]{2,1,0:T(8,128)(2,1)S(1)}, bf16[4,64,1408]{2,1,0:T(8,128)(2,1)S(1)}, u32[]{:S(2)}, u32[]{:S(2)}) collective-permute-start(bf16[4,64,1408]{2,1,0:T(8,128)(2,1)S(1)} %collective-permute-done.40), channel_id=1, source_target_pairs={{0,1},{1,0},{2,3},{3,2},{4,5},{5,4},{6,7},{7,6},{8,9},{9,8},{10,11... | collective-permute-start | bytes 2162696 | tf_op jit(solution)/shard_map/ppermute | solution.py:259
  494.7 44.0 %collective-permute-start.30 = (bf16[512,2048]{1,0:T(8,128)(2,1)S(1)}, bf16[512,2048]{1,0:T(8,128)(2,1)S(1)}, u32[]{:S(2)}, u32[]{:S(2)}) collective-permute-start(bf16[512,2048]{1,0:T(8,128)(2,1)S(1)} %get-tuple-element.32), channel_id=1, source_target_pairs={{0,16},{8,24},{16,0},{24,8},{1,17},{9,25},{17,1},{25,9},{2,18},{10... | collective-permute-start | bytes 6291464 | tf_op jit(solution)/shard_map/ppermute | solution.py:253
  510.1 45.4 %collective-permute-start.29 = (bf16[512,2048]{1,0:T(8,128)(2,1)S(1)}, bf16[512,2048]{1,0:T(8,128)(2,1)S(1)}, u32[]{:S(2)}, u32[]{:S(2)}) collective-permute-start(bf16[512,2048]{1,0:T(8,128)(2,1)S(1)} %get-tuple-element.32), channel_id=1, source_target_pairs={{0,8},{8,0},{16,24},{24,16},{1,9},{9,1},{17,25},{25,17},{2,10},{10... | collective-permute-start | bytes 6291464 | tf_op jit(solution)/shard_map/ppermute | solution.py:250
  617.6 65.3 %collective-permute-start.56 = (bf16[512,2048]{1,0:T(8,128)(2,1)S(1)}, bf16[512,2048]{1,0:T(8,128)(2,1)S(1)}, u32[]{:S(2)}, u32[]{:S(2)}) collective-permute-start(bf16[512,2048]{1,0:T(8,128)(2,1)S(1)} %dynamic-slice_bitcast_fusion.5), channel_id=1, source_target_pairs={{0,8},{8,0},{16,24},{24,16},{1,9},{9,1},{17,25},{25,17},{2,10},{10... | collective-permute-start | bytes 6291464 | tf_op jit(solution)/shard_map/ppermute | solution.py:250
  619.1 63.9 %collective-permute-start.58 = (bf16[512,2048]{1,0:T(8,128)(2,1)S(1)}, bf16[512,2048]{1,0:T(8,128)(2,1)}, u32[]{:S(2)}, u32[]{:S(2)}) collective-permute-start(bf16[512,2048]{1,0:T(8,128)(2,1)S(1)} %fusion.18), channel_id=1, source_target_pairs={{0,16},{8,24},{16,0},{24,8},{1,17},{9,25},{17,1},{25,9},{2,18},{10... | collective-permute-start | bytes 6291464 | tf_op jit(solution)/shard_map/ppermute | solution.py:253
  623.3 43.5 %collective-permute-start.65 = (f32[1,1]{1,0:T(1,128)}, f32[1,1]{1,0:T(1,128)}, u32[]{:S(2)}, u32[]{:S(2)}) collective-permute-start(f32[1,1]{1,0:T(1,128)} %add.943), channel_id=1, source_target_pairs={{0,16},{8,24},{16,0},{24,8},{1,17},{9,25},{17,1},{25,9},{2,18},{10... | collective-permute-start | bytes 20 | tf_op jit(solution)/shard_map/ppermute | solution.py:344
  694.5 44.3 %collective-permute-start.70 = (bf16[512,2048]{1,0:T(8,128)(2,1)}, bf16[512,2048]{1,0:T(8,128)(2,1)S(1)}, u32[]{:S(2)}, u32[]{:S(2)}) collective-permute-start(bf16[512,2048]{1,0:T(8,128)(2,1)} %get-tuple-element.29), channel_id=1, source_target_pairs={{0,16},{8,24},{16,0},{24,8},{1,17},{9,25},{17,1},{25,9},{2,18},{10... | collective-permute-start | bytes 6291464 | tf_op jit(solution)/shard_map/ppermute | solution.py:253
  695.4 43.4 %collective-permute-start.69 = (bf16[512,2048]{1,0:T(8,128)(2,1)}, bf16[512,2048]{1,0:T(8,128)(2,1)}, u32[]{:S(2)}, u32[]{:S(2)}) collective-permute-start(bf16[512,2048]{1,0:T(8,128)(2,1)} %get-tuple-element.29), channel_id=1, source_target_pairs={{0,8},{8,0},{16,24},{24,16},{1,9},{9,1},{17,25},{25,17},{2,10},{10... | collective-permute-start | bytes 6291464 | tf_op jit(solution)/shard_map/ppermute | solution.py:250
  854.9 160.8 %collective-permute-start.73 = (bf16[512,2048]{1,0:T(8,128)(2,1)}, bf16[512,2048]{1,0:T(8,128)(2,1)}, u32[]{:S(2)}, u32[]{:S(2)}) collective-permute-start(bf16[512,2048]{1,0:T(8,128)(2,1)} %dynamic-slice_bitcast_fusion.2), channel_id=1, source_target_pairs={{0,8},{8,0},{16,24},{24,16},{1,9},{9,1},{17,25},{25,17},{2,10},{10... | collective-permute-start | bytes 6291464 | tf_op jit(solution)/shard_map/ppermute | solution.py:250
  868.3 79.0 %collective-permute-start.113 = (bf16[4,64,1408]{2,1,0:T(8,128)(2,1)S(1)}, bf16[4,64,1408]{2,1,0:T(8,128)(2,1)S(1)}, u32[]{:S(2)}, u32[]{:S(2)}) collective-permute-start(bf16[4,64,1408]{2,1,0:T(8,128)(2,1)S(1)} %get-tuple-element.47), channel_id=1, source_target_pairs={{0,1},{1,0},{2,3},{3,2},{4,5},{5,4},{6,7},{7,6},{8,9},{9,8},{10,11... | collective-permute-start | bytes 2162696 | tf_op jit(solution)/shard_map/ppermute | solution.py:259
  869.1 47.6 %collective-permute-start.104 = (bf16[4,64,1408]{2,1,0:T(8,128)(2,1)S(1)}, bf16[4,64,1408]{2,1,0:T(8,128)(2,1)S(1)}, u32[]{:S(2)}, u32[]{:S(2)}) collective-permute-start(bf16[4,64,1408]{2,1,0:T(8,128)(2,1)S(1)} %get-tuple-element.53), channel_id=1, source_target_pairs={{0,1},{1,0},{2,3},{3,2},{4,5},{5,4},{6,7},{7,6},{8,9},{9,8},{10,11... | collective-permute-start | bytes 2162696 | tf_op jit(solution)/shard_map/ppermute | solution.py:259
  870.7 81.3 %collective-permute-start.103 = (bf16[4,64,1408]{2,1,0:T(8,128)(2,1)S(1)}, bf16[4,64,1408]{2,1,0:T(8,128)(2,1)S(1)}, u32[]{:S(2)}, u32[]{:S(2)}) collective-permute-start(bf16[4,64,1408]{2,1,0:T(8,128)(2,1)S(1)} %get-tuple-element.51), channel_id=1, source_target_pairs={{0,1},{1,0},{2,3},{3,2},{4,5},{5,4},{6,7},{7,6},{8,9},{9,8},{10,11... | collective-permute-start | bytes 2162696 | tf_op jit(solution)/shard_map/ppermute | solution.py:259
  885.8 60.9 %collective-permute-start.124 = (bf16[1,176,2048]{2,1,0:T(8,128)(2,1)S(1)}, bf16[1,176,2048]{2,1,0:T(8,128)(2,1)S(1)}, u32[]{:S(2)}, u32[]{:S(2)}) collective-permute-start(bf16[1,176,2048]{2,1,0:T(8,128)(2,1)S(1)} %get-tuple-element.43), channel_id=1, source_target_pairs={{0,1},{1,0},{2,3},{3,2},{4,5},{5,4},{6,7},{7,6},{8,9},{9,8},{10,11... | collective-permute-start | bytes 2162696 | tf_op jit(solution)/shard_map/ppermute | solution.py:259
  998.5 45.3 %collective-permute-start.101 = (bf16[4,64,1408]{2,1,0:T(8,128)(2,1)S(1)}, bf16[4,64,1408]{2,1,0:T(8,128)(2,1)S(1)}, u32[]{:S(2)}, u32[]{:S(2)}) collective-permute-start(bf16[4,64,1408]{2,1,0:T(8,128)(2,1)S(1)} %get-tuple-element.50), channel_id=1, source_target_pairs={{0,1},{1,0},{2,3},{3,2},{4,5},{5,4},{6,7},{7,6},{8,9},{9,8},{10,11... | collective-permute-start | bytes 2162696 | tf_op jit(solution)/shard_map/ppermute | solution.py:259
  1015.7 48.2 %collective-permute-start.107 = (bf16[4,64,1408]{2,1,0:T(8,128)(2,1)S(1)}, bf16[4,64,1408]{2,1,0:T(8,128)(2,1)S(1)}, u32[]{:S(2)}, u32[]{:S(2)}) collective-permute-start(bf16[4,64,1408]{2,1,0:T(8,128)(2,1)S(1)} %fusion.68), channel_id=1, source_target_pairs={{0,2},{1,3},{2,4},{3,5},{4,6},{5,7},{6,0},{7,1},{8,10},{9,11},{10,... | collective-permute-start | bytes 2162696 | tf_op jit(solution)/shard_map/ppermute | solution.py:256
  1041.6 48.4 %collective-permute-start.74 = (bf16[512,2048]{1,0:T(8,128)(2,1)S(1)}, bf16[512,2048]{1,0:T(8,128)(2,1)S(1)}, u32[]{:S(2)}, u32[]{:S(2)}) collective-permute-start(bf16[512,2048]{1,0:T(8,128)(2,1)S(1)} %fusion.16), channel_id=1, source_target_pairs={{0,16},{8,24},{16,0},{24,8},{1,17},{9,25},{17,1},{25,9},{2,18},{10... | collective-permute-start | bytes 6291464 | tf_op jit(solution)/shard_map/ppermute | solution.py:253
  1100.2 47.1 %collective-permute-start.76 = (bf16[512,2048]{1,0:T(8,128)(2,1)}, bf16[512,2048]{1,0:T(8,128)(2,1)S(1)}, u32[]{:S(2)}, u32[]{:S(2)}) collective-permute-start(bf16[512,2048]{1,0:T(8,128)(2,1)} %get-tuple-element.26), channel_id=1, source_target_pairs={{0,16},{8,24},{16,0},{24,8},{1,17},{9,25},{17,1},{25,9},{2,18},{10... | collective-permute-start | bytes 6291464 | tf_op jit(solution)/shard_map/ppermute | solution.py:253
  1102.3 64.5 %collective-permute-start.75 = (bf16[512,2048]{1,0:T(8,128)(2,1)}, bf16[512,2048]{1,0:T(8,128)(2,1)}, u32[]{:S(2)}, u32[]{:S(2)}) collective-permute-start(bf16[512,2048]{1,0:T(8,128)(2,1)} %get-tuple-element.26), channel_id=1, source_target_pairs={{0,8},{8,0},{16,24},{24,16},{1,9},{9,1},{17,25},{25,17},{2,10},{10... | collective-permute-start | bytes 6291464 | tf_op jit(solution)/shard_map/ppermute | solution.py:250
  1103.0 59.4 %collective-permute-start.78 = (f32[512,2]{0,1:T(2,128)S(1)}, f32[512,2]{0,1:T(2,128)S(1)}, u32[]{:S(2)}, u32[]{:S(2)}) collective-permute-start(f32[512,2]{0,1:T(2,128)S(1)} %get-tuple-element.87), channel_id=1, source_target_pairs={{0,8},{8,0},{16,24},{24,16},{1,9},{9,1},{17,25},{25,17},{2,10},{10... | collective-permute-start | bytes 12296 | tf_op jit(solution)/shard_map/ppermute | solution.py:250
  1103.6 59.0 %collective-permute-start.79 = (f32[512,2]{0,1:T(2,128)S(1)}, f32[512,2]{0,1:T(2,128)S(1)}, u32[]{:S(2)}, u32[]{:S(2)}) collective-permute-start(f32[512,2]{0,1:T(2,128)S(1)} %get-tuple-element.87), channel_id=1, source_target_pairs={{0,16},{8,24},{16,0},{24,8},{1,17},{9,25},{17,1},{25,9},{2,18},{10... | collective-permute-start | bytes 12296 | tf_op jit(solution)/shard_map/ppermute | solution.py:253
  1104.9 42.5 %collective-permute-start.59 = (f32[1,1]{1,0:T(1,128)}, f32[1,1]{1,0:T(1,128)}, u32[]{:S(2)}, u32[]{:S(2)}) collective-permute-start(f32[1,1]{1,0:T(1,128)} %bitcast.112), channel_id=1, source_target_pairs={{0,8},{8,0},{16,24},{24,16},{1,9},{9,1},{17,25},{25,17},{2,10},{10... | collective-permute-start | bytes 20 | tf_op jit(solution)/shard_map/ppermute | solution.py:344
  1161.9 157.1 %collective-permute-start.108 = (bf16[64,1408]{1,0:T(8,128)(2,1)}, bf16[64,1408]{1,0:T(8,128)(2,1)}, u32[]{:S(2)}, u32[]{:S(2)}) collective-permute-start(bf16[64,1408]{1,0:T(8,128)(2,1)} %get-tuple-element.85), channel_id=1, source_target_pairs={{0,8},{8,0},{16,24},{24,16},{1,9},{9,1},{17,25},{25,17},{2,10},{10... | collective-permute-start | bytes 540680 | tf_op jit(solution)/shard_map/ppermute | solution.py:300
  1255.3 56.3 %collective-permute-start.82 = (bf16[512,2048]{1,0:T(8,128)(2,1)S(1)}, bf16[512,2048]{1,0:T(8,128)(2,1)S(1)}, u32[]{:S(2)}, u32[]{:S(2)}) collective-permute-start(bf16[512,2048]{1,0:T(8,128)(2,1)S(1)} %dynamic-slice_bitcast_fusion), channel_id=1, source_target_pairs={{0,8},{8,0},{16,24},{24,16},{1,9},{9,1},{17,25},{25,17},{2,10},{10... | collective-permute-start | bytes 6291464 | tf_op jit(solution)/shard_map/ppermute | solution.py:250
  1258.8 55.1 %collective-permute-start.86 = (bf16[4,64,2048]{2,1,0:T(8,128)(2,1)S(1)}, bf16[4,64,2048]{2,1,0:T(8,128)(2,1)S(1)}, u32[]{:S(2)}, u32[]{:S(2)}) collective-permute-start(bf16[4,64,2048]{2,1,0:T(8,128)(2,1)S(1)} %get-tuple-element.38), channel_id=1, source_target_pairs={{0,1},{1,0},{2,3},{3,2},{4,5},{5,4},{6,7},{7,6},{8,9},{9,8},{10,11... | collective-permute-start | bytes 3145736 | tf_op jit(solution)/shard_map/ppermute | solution.py:259
  1324.1 96.6 %collective-permute-start.81 = (bf16[512,2048]{1,0:T(8,128)(2,1)}, bf16[512,2048]{1,0:T(8,128)(2,1)S(1)}, u32[]{:S(2)}, u32[]{:S(2)}) collective-permute-start(bf16[512,2048]{1,0:T(8,128)(2,1)} %dynamic-slice_bitcast_fusion.1), channel_id=1, source_target_pairs={{0,8},{8,0},{16,24},{24,16},{1,9},{9,1},{17,25},{25,17},{2,10},{10... | collective-permute-start | bytes 6291464 | tf_op jit(solution)/shard_map/ppermute | solution.py:250
  1324.3 65.8 %collective-permute-start.85 = (bf16[4,64,2048]{2,1,0:T(8,128)(2,1)}, bf16[4,64,2048]{2,1,0:T(8,128)(2,1)}, u32[]{:S(2)}, u32[]{:S(2)}) collective-permute-start(bf16[4,64,2048]{2,1,0:T(8,128)(2,1)} %get-tuple-element.39), channel_id=1, source_target_pairs={{0,1},{1,0},{2,3},{3,2},{4,5},{5,4},{6,7},{7,6},{8,9},{9,8},{10,11... | collective-permute-start | bytes 3145736 | tf_op jit(solution)/shard_map/ppermute | solution.py:259
  1326.3 94.4 %collective-permute-start.83 = (bf16[512,2048]{1,0:T(8,128)(2,1)}, bf16[512,2048]{1,0:T(8,128)(2,1)}, u32[]{:S(2)}, u32[]{:S(2)}) collective-permute-start(bf16[512,2048]{1,0:T(8,128)(2,1)} %fusion.14), channel_id=1, source_target_pairs={{0,16},{8,24},{16,0},{24,8},{1,17},{9,25},{17,1},{25,9},{2,18},{10... | collective-permute-start | bytes 6291464 | tf_op jit(solution)/shard_map/ppermute | solution.py:253
  1327.0 64.6 %collective-permute-start.89 = (bf16[4,64,2048]{2,1,0:T(8,128)(2,1)}, bf16[4,64,2048]{2,1,0:T(8,128)(2,1)}, u32[]{:S(2)}, u32[]{:S(2)}) collective-permute-start(bf16[4,64,2048]{2,1,0:T(8,128)(2,1)} %fusion.45), channel_id=1, source_target_pairs={{0,2},{1,3},{2,4},{3,5},{4,6},{5,7},{6,0},{7,1},{8,10},{9,11},{10,... | collective-permute-start | bytes 3145736 | tf_op jit(solution)/shard_map/ppermute | solution.py:256
  (147 other events, 3339.6 us)

commit v2 on v1

--- a/solution.py
+++ b/solution.py
@@ -218,6 +218,408 @@
     )(rates, bounds, seg.reshape(length, 1), seg.reshape(1, length), z, a, dj, ra, m, states)
 
 
+def empty(shape, kind):
+    return pl.pallas_call(
+        lambda out: None,
+        out_shape=jax.ShapeDtypeStruct(shape, kind),
+        out_specs=pl.BlockSpec(memory_space=pl.ANY),
+        name="empty",
+    )()
+
+
+def pack_kernel(seq, heads, hd, *refs):
+    weights, glu, attn_out, glu_outs = refs[:4], refs[4:6], refs[6], refs[7:]
+    for i in range(seq):
+        for h in range(heads):
+            for m, w in enumerate(weights):
+                to, at = (h * 4 + m) * hd, (i * heads + h) * hd
+                attn_out[i, :, to : to + hd] = w[:, at : at + hd]
+        for w, out in zip(glu, glu_outs):
+            n = out.shape[2]
+            out[i] = w[:, i * n : (i + 1) * n]
+
+
+def pack_columns(weights, glu, seq, heads, hd):
+    r, kind = weights[0].shape[0], weights[0].dtype
+    n = glu[0].shape[1] // seq
+    return pl.pallas_call(
+        functools.partial(pack_kernel, seq, heads, hd),
+        out_shape=[jax.ShapeDtypeStruct((seq, r, heads * 4 * hd), kind)]
+        + [jax.ShapeDtypeStruct((seq, r, n), kind)] * 2,
+        compiler_params=pltpu.CompilerParams(vmem_limit_bytes=VMEM_BYTES),
+        name="pack_columns",
+    )(*weights, *glu)
+
+
+class Net:
+    def __init__(self, shape, send_sem, recv_sem, local_sem):
+        self.seq, self.fsdp, self.inner = shape
+        self.outer = self.fsdp // self.inner
+        self.chips = self.seq // 2
+        self.send_sem, self.recv_sem, self.local_sem = send_sem, recv_sem, local_sem
+        self.used = 0
+        self.locals = 0
+        self.s, self.f = lax.axis_index("seq"), lax.axis_index("fsdp")
+        self.chip, self.core = self.s // 2, self.s % 2
+        self.o, self.i = self.f // self.inner, self.f % self.inner
+        self.sent = []
+
+    def seq_peers(self):
+        for dx in range(self.chips):
+            for dc in range(2):
+                if dx or dc:
+                    yield dx, dc, lax.rem(self.chip + dx, self.chips) * 2 + lax.rem(self.core + dc, 2)
+
+    def at_seq(self, s):
+        return (s, self.f)
+
+    def at_inner(self, j):
+        return (self.s, self.o * self.inner + lax.rem(self.i + j, self.inner))
+
+    def at_outer(self, k):
+        return (self.s, lax.rem(self.o + k, self.outer) * self.inner + self.i)
+
+    def barrier(self):
+        peers = [self.at_seq(s) for _, _, s in self.seq_peers()]
+        peers += [self.at_inner(j) for j in range(1, self.inner)]
+        peers += [self.at_outer(1), self.at_outer(self.outer - 1)]
+        sem = pltpu.get_barrier_semaphore()
+        for peer in peers:
+            pl.semaphore_signal(sem, inc=1, device_id=peer, device_id_type=pl.DeviceIdType.MESH)
+        pl.semaphore_wait(sem, len(peers))
+
+    def send(self, src, dst, device):
+        copy = pltpu.make_async_remote_copy(
+            src_ref=src,
+            dst_ref=dst,
+            send_sem=self.send_sem.at[self.used],
+            recv_sem=self.recv_sem.at[self.used],
+            device_id=device,
+            device_id_type=pl.DeviceIdType.MESH,
+        )
+        self.used += 1
+        copy.start()
+        self.sent.append(copy)
+        return copy
+
+    def copy(self, src, dst):
+        copy = pltpu.make_async_copy(src, dst, self.local_sem.at[self.locals])
+        self.locals += 1
+        copy.start()
+        return copy
+
+    def finish(self):
+        for copy in self.sent:
+            copy.wait_send()
+        self.sent = []
+
+
+def net_shape(mesh_seq, mesh_fsdp):
+    return mesh_seq, mesh_fsdp, 2 if mesh_fsdp == 8 else 4
+
+
+class Ring:
+    def __init__(self, net, piece, full):
+        self.net, self.piece, self.full = net, piece, full
+        self.copies = [net.copy(piece, full.at[:, net.o, net.i])]
+        self.at = 0
+        self.coming = None
+        self.side = []
+
+    def step(self):
+        net, full = self.net, self.full
+        if self.at >= net.outer:
+            return
+        if self.coming is not None:
+            self.coming.wait_recv()
+        spot = full.at[:, lax.rem(net.o + net.outer - self.at, net.outer), net.i]
+        src = self.piece if self.at == 0 else spot
+        self.coming = None
+        if self.at < net.outer - 1:
+            self.coming = net.send(src, spot, net.at_outer(1))
+        for j in range(1, net.inner):
+            self.side.append(net.send(src, spot, net.at_inner(j)))
+        self.at += 1
+
+    def done(self):
+        while self.at < self.net.outer:
+            self.step()
+        for copy in self.side:
+            copy.wait_recv()
+        for copy in self.copies:
+            copy.wait()
+
+
+def swap(net, blocks, got):
+    own = net.copy(blocks.at[net.s], got.at[net.s])
+    coming = [
+        net.send(blocks.at[s], got.at[net.s], net.at_seq(s)) for _, _, s in net.seq_peers()
+    ]
+    return own, coming
+
+
+def arrive(pair):
+    own, coming = pair
+    own.wait()
+    for copy in coming:
+        copy.wait_recv()
+
+
+class Rows:
+    def __init__(self, net, own, whole):
+        t = own.shape[0]
+        self.net, self.whole = net, whole
+        spot = lambda s: whole.at[pl.ds(pl.multiple_of(s * t, t), t)]
+        self.spot = spot
+        self.far = [
+            net.send(own, spot(net.s), net.at_seq(lax.rem(net.chip + dx, net.chips) * 2 + net.core))
+            for dx in range(1, net.chips)
+        ]
+        self.near = [net.send(own, spot(net.s), net.at_seq(net.chip * 2 + 1 - net.core))]
+        self.own = net.copy(own, spot(net.s))
+
+    def turn(self):
+        net = self.net
+        for dx, copy in zip(range(1, net.chips), self.far):
+            copy.wait_recv()
+            spot = self.spot(lax.rem(net.chip + net.chips - dx, net.chips) * 2 + net.core)
+            self.near.append(net.send(spot, spot, net.at_seq(net.chip * 2 + 1 - net.core)))
+
+    def done(self):
+        for copy in self.near:
+            copy.wait_recv()
+        self.own.wait()
+
+
+def gather_kernel(
+    shape,
+    attn_ref,
+    first_ref,
+    second_ref,
+    out_ref,
+    down_ref,
+    n1_ref,
+    seg_ref,
+    attn_mid,
+    first_mid,
+    second_mid,
+    full_attn,
+    full_first,
+    full_second,
+    full_out,
+    full_down,
+    n1_all,
+    seg_all,
+    send_sem,
+    recv_sem,
+    local_sem,
+):
+    net = Net(shape, send_sem, recv_sem, local_sem)
+    net.barrier()
+    attn_swap = swap(net, attn_ref, attn_mid)
+    seg_own = net.copy(seg_ref, seg_all.at[net.s])
+    segs = [net.send(seg_ref, seg_all.at[net.s], net.at_seq(s)) for _, _, s in net.seq_peers()]
+    first_swap = swap(net, first_ref, first_mid)
+    second_swap = swap(net, second_ref, second_mid)
+    rows = Rows(net, n1_ref, n1_all)
+    arrive(attn_swap)
+    rings = [Ring(net, attn_mid, full_attn)]
+    rings[0].step()
+    rings.append(Ring(net, out_ref, full_out))
+    rings[0].step()
+    rings[0].step()
+    rings[0].step()
+    arrive(first_swap)
+    arrive(second_swap)
+    rows.turn()
+    rings.append(Ring(net, first_mid, full_first))
+    rings.append(Ring(net, second_mid, full_second))
+    rings.append(Ring(net, down_ref, full_down))
+    for ring in rings[1:]:
+        for _ in range(net.outer):
+            ring.step()
+    for ring in rings:
+        ring.done()
+    rows.done()
+    seg_own.wait()
+    for copy in segs:
+        copy.wait_recv()
+    net.finish()
+
+
+HBM = pl.BlockSpec(memory_space=pl.ANY)
+
+
+def gather_all(shape, attn, first, second, w_out, w_down, n1, seg):
+    seq, fsdp, inner = shape
+    outer = fsdp // inner
+    like = lambda v, lead: jax.ShapeDtypeStruct(lead + v.shape[-2:], v.dtype)
+    ring = lambda v: like(v, (v.shape[0], outer, inner))
+    outs = [like(v, (seq,)) for v in (attn, first, second)]
+    outs += [ring(v) for v in (attn, first, second, w_out, w_down)]
+    outs.append(jax.ShapeDtypeStruct((seq * n1.shape[0], n1.shape[1]), n1.dtype))
+    outs.append(jax.ShapeDtypeStruct((seq,) + seg.shape, seg.dtype))
+    copies = 4 * (seq - 1) + 2 * seq + 5 * (outer * inner + outer)
+    got = pl.pallas_call(
+        functools.partial(gather_kernel, shape),
+        in_specs=[HBM] * 7,
+        out_specs=[HBM] * len(outs),
+        out_shape=outs,
+        scratch_shapes=[
+            pltpu.SemaphoreType.DMA((copies,)),
+            pltpu.SemaphoreType.DMA((copies,)),
+            pltpu.SemaphoreType.DMA((16,)),
+        ],
+        compiler_params=pltpu.CompilerParams(
+            collective_id=0, has_side_effects=True, vmem_limit_bytes=VMEM_BYTES
+        ),
+        name="gather_all",
+    )(attn, first, second, w_out, w_down, n1, seg)
+    flat = lambda v: v.reshape(-1, v.shape[-1])
+    return [flat(v) for v in got[3:8]] + list(got[8:])
+
+
+class Sum:
+    def __init__(self, net, g, side, send, recv, load):
+        self.net, self.g, self.side_ref = net, g, side
+        self.send_buf, self.recv_buf, self.load = send, recv, load
+        self.side = []
+        self.ring = []
+        for k in range(net.outer):
+            o = self.spot(k)
+            now = []
+            for j in range(1, net.inner):
+                to = lax.rem(net.i + j, net.inner)
+                now.append(net.send(g.at[:, o, to], side.at[j - 1, :, o], net.at_inner(j)))
+            self.side.append(now)
+        self.at = 0
+
+    def spot(self, k):
+        return lax.rem(self.net.o + 2 * self.net.outer - 1 - k, self.net.outer)
+
+    def step(self, final=None):
+        net, k = self.net, self.at
+        self.at += 1
+        o = self.spot(k)
+        terms = self.load
+        loads = [net.copy(self.g.at[:, o, net.i], terms.at[0])]
+        for j, copy in enumerate(self.side[k]):
+            copy.wait_recv()
+            loads.append(net.copy(self.side_ref.at[j, :, o], terms.at[j + 1]))
+        if k > 0:
+            self.ring[k - 1].wait_recv()
+        for load in loads:
+            load.wait()
+        a = terms.shape[1]
+
+        def one(i, _):
+            total = terms[0, i].astype(WIDE)
+            for j in range(1, net.inner):
+                total = total + terms[j, i].astype(WIDE)
+            if k > 0:
+                total = total + self.recv_buf[k - 1, i].astype(WIDE)
+            if k < net.outer - 1:
+                self.send_buf[k, i] = total.astype(LOW)
+            else:
+                final(i, total)
+            return 0
+
+        lax.fori_loop(0, a, one, 0)
+        if k < net.outer - 1:
+            self.ring.append(net.send(self.send_buf.at[k], self.recv_buf.at[k], net.at_outer(1)))
+
+
+def scatter_kernel(shape, heads, hd, *refs):
+    names = ("down", "first", "second", "attn", "out")
+    it = iter(refs)
+    take = lambda: {name: next(it) for name in names}
+    grads = take()
+    o_down, o_first, o_second, o_out = (next(it) for _ in range(4))
+    o_attn = [next(it) for _ in range(4)]
+    sides, sends, recvs, loads = take(), take(), take(), take()
+    totals = {name: next(it) for name in ("first", "second", "attn")}
+    gots = {name: next(it) for name in ("first", "second", "attn")}
+    send_sem, recv_sem, local_sem = (next(it) for _ in range(3))
+    net = Net(shape, send_sem, recv_sem, local_sem)
+    net.barrier()
+    sums = {n: Sum(net, grads[n], sides[n], sends[n], recvs[n], loads[n]) for n in names}
+
+    def run(name, final):
+        for k in range(net.outer):
+            sums[name].step(final)
+
+    def keep(name):
+        def final(i, rows):
+            totals[name][i] = rows.astype(LOW)
+
+        return final
+
+    def place(ref):
+        def final(i, rows):
+            ref[...] = rows
+
+        return final
+
+    swaps = {}
+    run("down", place(o_down))
+    for name in ("first", "second", "attn"):
+        run(name, keep(name))
+        swaps[name] = swap(net, totals[name], gots[name])
+    run("out", place(o_out))
+    for name, ref in (("first", o_first), ("second", o_second)):
+        arrive(swaps[name])
+        n = gots[name].shape[2]
+        for i in range(net.seq):
+            ref[:, i * n : (i + 1) * n] = gots[name][i].astype(WIDE)
+    arrive(swaps["attn"])
+    for i in range(net.seq):
+        for h in range(heads):
+            for m in range(4):
+                at, to = (h * 4 + m) * hd, (i * heads + h) * hd
+                o_attn[m][:, to : to + hd] = gots["attn"][i, :, at : at + hd].astype(WIDE)
+    net.finish()
+
+
+def scatter_all(shape, heads, hd, grads):
+    seq, fsdp, inner = shape
+    outer = fsdp // inner
+    names = ("down", "first", "second", "attn", "out")
+    lead = {"down": 1, "out": 1, "first": seq, "second": seq, "attn": seq}
+    blocks = [
+        g.reshape(lead[n], outer, inner, g.shape[0] // (lead[n] * fsdp), g.shape[1])
+        for n, g in zip(names, grads)
+    ]
+    size = {n: (g.shape[0], g.shape[3], g.shape[4]) for n, g in zip(names, blocks)}
+    row = lambda n: jax.ShapeDtypeStruct((size[n][1], size[n][2]), WIDE)
+    wide = lambda n: jax.ShapeDtypeStruct((size[n][1], size[n][2] * seq), WIDE)
+    attn = jax.ShapeDtypeStruct((size["attn"][1], seq * heads * hd), WIDE)
+    outs = [row("down"), wide("first"), wide("second"), row("out")] + [attn] * 4
+    side = [
+        jax.ShapeDtypeStruct((inner - 1, size[n][0], outer) + size[n][1:], LOW) for n in names
+    ]
+    scratch = [pltpu.VMEM((outer - 1,) + size[n], LOW) for n in names] * 2
+    scratch += [pltpu.VMEM((inner,) + size[n], LOW) for n in names]
+    scratch += [pltpu.VMEM(size[n], LOW) for n in ("first", "second", "attn")] * 2
+    copies = 5 * (outer * inner + outer) + 3 * seq
+    scratch += [
+        pltpu.SemaphoreType.DMA((copies,)),
+        pltpu.SemaphoreType.DMA((copies,)),
+        pltpu.SemaphoreType.DMA((5 * outer * inner + 8,)),
+    ]
+    got = pl.pallas_call(
+        functools.partial(scatter_kernel, shape, heads, hd),
+        in_specs=[HBM] * 5,
+        out_specs=[pl.BlockSpec(memory_space=pltpu.VMEM)] * len(outs) + [HBM] * 5,
+        out_shape=outs + side,
+        scratch_shapes=scratch,
+        compiler_params=pltpu.CompilerParams(
+            collective_id=1, has_side_effects=True, vmem_limit_bytes=VMEM_BYTES
+        ),
+        name="scatter_all",
+    )(*blocks)
+    return got[:8]
+
+
 class Moves:
     def __init__(self):
         self.seq = lax.axis_size("seq")
@@ -259,91 +661,61 @@
         return lax.ppermute(v, "fsdp", self.in_perm)
 
     def gather_seq(self, v):
-        whole = jnp.zeros((self.seq,) + v.shape, v.dtype)
+        whole = empty((self.seq * v.shape[0],) + v.shape[1:], v.dtype)
+        t = v.shape[0]
         now = v
         for k in range(self.chips):
             later = self.to_chip(now) if k < self.chips - 1 else None
             other = self.to_core(now)
             chip = (self.chip - k) % self.chips
-            whole = lax.dynamic_update_index_in_dim(whole, now, chip * 2 + self.core, 0)
-            whole = lax.dynamic_update_index_in_dim(whole, other, chip * 2 + 1 - self.core, 0)
+            place = lambda whole, part, i: lax.dynamic_update_slice_in_dim(whole, part, i * t, 0)
+            whole = place(whole, now, chip * 2 + self.core)
+            whole = place(whole, other, chip * 2 + 1 - self.core)
             now = later
-        return whole.reshape((-1,) + v.shape[1:])
-
-    def scatter_seq(self, part, kind):
-        held = None
-        for k in range(self.chips):
-            term = part((self.chip - 1 - k) % self.chips)
-            give = lax.dynamic_index_in_dim(term, 1 - self.core, 0, False)
-            keep = lax.dynamic_index_in_dim(term, self.core, 0, False)
-            total = keep.astype(WIDE) + self.to_core(give).astype(WIDE)
-            if held is not None:
-                total = total + held.astype(WIDE)
-            if k < self.chips - 1:
-                held = self.to_chip(total.astype(kind))
+        return whole
+
+    def sum_axis(self, v, axis, size):
+        step = 1
+        while step < size:
+            v = v + lax.ppermute(v, axis, [(i, i ^ step) for i in range(size)])
+            step *= 2
+        return v
+
+    def sum_seq(self, v):
+        return self.sum_axis(v, "seq", self.seq)
+
+    def sum_all(self, v):
+        return self.sum_axis(self.sum_seq(v), "fsdp", self.fsdp)
+
+
+class ScatterSeq:
+    def __init__(self, move, part, kind=LOW):
+        self.move, self.part, self.kind = move, part, kind
+        self.held = None
+        self.term = None
+        for k in range(move.chips - 1):
+            total = self.own(k)
+            self.held = move.to_chip(total.astype(kind))
+
+    def own(self, k, *tokens):
+        move = self.move
+        self.term = self.part((move.chip - 1 - k) % move.chips, *tokens)
+        term = self.term.reshape((2, -1) + self.term.shape[1:])
+        give = lax.dynamic_index_in_dim(term, 1 - move.core, 0, False)
+        keep = lax.dynamic_index_in_dim(term, move.core, 0, False)
+        total = keep.astype(WIDE) + move.to_core(give).astype(WIDE)
+        if self.held is not None:
+            total = total + self.held.astype(WIDE)
         return total
 
-    def swap_seq(self, blocks):
-        pick = lambda i: lax.dynamic_index_in_dim(blocks, i, 0, False)
-        whole = lax.dynamic_update_index_in_dim(jnp.zeros_like(blocks), pick(self.s), self.s, 0)
-        for dx in range(self.chips):
-            for dc in range(2):
-                if dx == 0 and dc == 0:
-                    continue
-                to = (self.chip + dx) % self.chips * 2 + (self.core ^ dc)
-                source = (self.chip - dx) % self.chips * 2 + (self.core ^ dc)
-                perm = [
-                    (x * 2 + c, (x + dx) % self.chips * 2 + (c ^ dc))
-                    for x in range(self.chips)
-                    for c in range(2)
-                ]
-                got = lax.ppermute(pick(to), "seq", perm)
-                whole = lax.dynamic_update_index_in_dim(whole, got, source, 0)
-        return whole
-
-    def gather_fsdp(self, v):
-        a, r, n = v.shape
-        whole = jnp.zeros((a, self.fsdp, r, n), v.dtype)
-        now = v
-        for k in range(self.outer):
-            later = self.to_out(now) if k < self.outer - 1 else None
-            out_at = (self.out_at - k) % self.outer
-            piece = now
-            for j in range(self.inner):
-                in_at = (self.in_at - j) % self.inner
-                whole = lax.dynamic_update_slice_in_dim(
-                    whole, piece[:, None], out_at * self.inner + in_at, 1
-                )
-                if j < self.inner - 1:
-                    piece = self.to_in(piece)
-            now = later
-        return whole.reshape(a * self.fsdp * r, n)
-
-    def scatter_fsdp(self, g, a):
-        n = g.shape[1]
-        r = g.shape[0] // (a * self.fsdp)
-        g = g.reshape(a, self.fsdp, r, n)
-        pick = lambda o, i: lax.dynamic_slice_in_dim(g, o * self.inner + i, 1, 1)[:, 0]
-        held = None
-        for k in range(self.outer):
-            out_at = (self.out_at - 1 - k) % self.outer
-            total = None
-            for j in range(self.inner):
-                term = pick(out_at, (self.in_at - 1 - j) % self.inner).astype(WIDE)
-                total = term if total is None else term + self.to_in(total.astype(LOW)).astype(WIDE)
-            if held is not None:
-                total = total + held.astype(WIDE)
-            if k < self.outer - 1:
-                held = self.to_out(total.astype(LOW))
-        return total
-
-    def sum_all(self, v):
-        for axis, size in (("seq", self.seq), ("fsdp", self.fsdp)):
-            step = 1
-            while step < size:
-                v = v + lax.ppermute(v, axis, [(i, i ^ step) for i in range(size)])
-                step *= 2
+    def done(self, *tokens):
+        return self.own(self.move.chips - 1, *tokens)
+
+
+def after(v, *tokens):
+    if not tokens:
         return v
+    return lax.optimization_barrier((v,) + tokens)[0]
 
 
 def on_device(
@@ -373,99 +745,99 @@
     ffs = ff // seq
     cols = heads * 4 * hd
 
+    shape = net_shape(seq, move.fsdp)
     keep = valid.astype(WIDE).reshape(block_len, 1)
-    count = move.sum_all(jnp.sum(keep).reshape(1, 1))
-
-    seg = move.gather_seq(segment_ids.reshape(block_len))
-    length = seg.shape[0]
-    bounds = jnp.concatenate([jnp.full((1,), -1, jnp.int32), seg[CHUNK - 1 :: CHUNK]])
-    rates = lax.dynamic_slice_in_dim(decay_rate, move.s * heads, heads, 0)
-
-    attn_own = jnp.stack(
-        [w.reshape(own_rows, seq, heads, hd) for w in (w_query, w_key, w_value, w_gate)], axis=3
+    count_own = jnp.sum(keep).reshape(1, 1)
+
+    attn_own, first_own, second_own = pack_columns(
+        (w_query, w_key, w_value, w_gate), (w_first, w_second), seq, heads, hd
     )
-    attn_own = attn_own.reshape(own_rows, seq, cols).transpose(1, 0, 2)
-    glu_own = jnp.stack([w_first.reshape(own_rows, seq, ffs), w_second.reshape(own_rows, seq, ffs)])
-    glu_own = glu_own.transpose(2, 0, 1, 3)
-
-    full_attn = move.gather_fsdp(move.swap_seq(attn_own))
-    full_out = move.gather_fsdp(w_out[None])
-    glu_mid = move.swap_seq(glu_own)
-    full_first = move.gather_fsdp(glu_mid[:, 0])
-    full_second = move.gather_fsdp(glu_mid[:, 1])
-    full_down = move.gather_fsdp(w_down[None])
-
     x32 = inputs.reshape(block_len, width).astype(WIDE)
     r1 = lax.rsqrt(jnp.mean(x32 * x32, axis=-1, keepdims=True) + 1e-6)
     n1 = x32 * r1
-    n1_all = move.gather_seq(n1.astype(LOW))
+    full_attn, full_first, full_second, full_out, full_down, n1_all, seg = gather_all(
+        shape,
+        attn_own,
+        first_own,
+        second_own,
+        w_out[None],
+        w_down[None],
+        n1.astype(LOW),
+        segment_ids.reshape(1, block_len),
+    )
+    seg = seg.reshape(seq * block_len)
+    length = seg.shape[0]
+    count = move.sum_all(after(count_own, n1_all))
+
+    bounds = jnp.concatenate([jnp.full((1,), -1, jnp.int32), seg[CHUNK - 1 :: CHUNK]])
+    rates = lax.dynamic_slice_in_dim(decay_rate, move.s * heads, heads, 0)
+
     z = dot(n1_all, full_attn)
     au, a, ss, states = attend(z, seg, bounds, rates, heads, hd)
+    ss_all = move.sum_seq(ss.reshape(length))
 
     def rows_of(v, chip):
         return lax.dynamic_slice_in_dim(v, chip * 2 * block_len, 2 * block_len, 0)
 
-    def scatter_product(pairs):
-        def part(chip):
-            total = sum(dot(rows_of(v, chip), w, 1, d) for v, w, d in pairs)
-            return total.astype(LOW).reshape(2, block_len, -1)
-
-        return move.scatter_seq(part, LOW)
-
-    out_rows = scatter_product([(au, full_out, 0)])
-    ss_own = move.scatter_seq(lambda chip: rows_of(ss, chip).reshape(2, block_len, 1), WIDE)
-    ra = lax.rsqrt(ss_own / width + 1e-6)
-    mixed_out = out_rows * ra
+    def product_scatter(pairs):
+        def part(chip, *tokens):
+            left = [rows_of(after(v, *tokens), chip) for v, _, _ in pairs]
+            return sum(dot(l, w, 1, d) for l, (_, w, d) in zip(left, pairs)).astype(LOW)
+
+        return ScatterSeq(move, part)
+
+    out_sum = product_scatter([(au, full_out, 0)])
+    ra_all = lax.rsqrt(ss_all / width + 1e-6).reshape(length, 1)
+    ra = lax.dynamic_slice_in_dim(ra_all, move.s * block_len, block_len, 0)
+    mixed_out = out_sum.done() * ra
     hsum = x32 + mixed_out
     r2 = lax.rsqrt(jnp.mean(hsum * hsum, axis=-1, keepdims=True) + 1e-6)
     m2 = hsum * r2
-    n2_all = move.gather_seq(m2.astype(LOW))
+    m2_low = m2.astype(LOW)
+    n2_all = move.gather_seq(m2_low)
 
     g1 = dot(n2_all, full_first)
     g2 = dot(n2_all, full_second)
     p = (g1 * g2).astype(LOW)
     g1 = g1.astype(LOW)
     g2 = g2.astype(LOW)
-    y = hsum + scatter_product([(p, full_down, 0)])
+    y_sum = product_scatter([(p, full_down, 0)])
+    y = hsum + y_sum.done()
     layer_out = y.astype(LOW).reshape(1, block_len, width)
 
     error = y - teacher.reshape(block_len, width).astype(WIDE)
-    loss = move.sum_all(jnp.sum(keep * error * error).reshape(1, 1)) / (width * count)
     tokens = block_len * seq * move.fsdp
     dy = tokens / count * keep * error
-    dy_all = move.gather_seq(dy.astype(LOW))
-
-    grad_down = dot(p, dy_all, 0, 0).astype(LOW)
+    dyb = dy.astype(LOW)
+    dy_all = move.gather_seq(dyb)
+
     dp = dot(dy_all, full_down, 1, 1)
     dg1 = (dp * g2.astype(WIDE)).astype(LOW)
     dg2 = (dp * g1.astype(WIDE)).astype(LOW)
-    dn2 = scatter_product([(dg1, full_first, 1), (dg2, full_second, 1)])
-    grad_first = dot(n2_all, dg1, 0, 0).astype(LOW)
-    grad_second = dot(n2_all, dg2, 0, 0).astype(LOW)
+    dn2_sum = product_scatter([(dg1, full_first, 1), (dg2, full_second, 1)])
+    grad_down = dot(after(p, dn2_sum.term), dy_all, 0, 0).astype(LOW)
+    dn2 = dn2_sum.done(grad_down)
     dh = dy + r2 * (dn2 - m2 * jnp.mean(dn2 * m2, axis=-1, keepdims=True))
     dhb = dh.astype(LOW)
-    mean_own = jnp.mean(dhb.astype(WIDE) * mixed_out, axis=-1, keepdims=True)
+    mean_own = jnp.mean(after(dhb, dn2_sum.term).astype(WIDE) * mixed_out, axis=-1)
     dh_all = move.gather_seq(dhb)
-    small = move.gather_seq(jnp.concatenate([ra, mean_own], axis=1))
-
-    dj = dot(dh_all, full_out, 1, 1)
-    dz, o = attend_back(
-        z, a, dj, small[:, :1], small[:, 1:], states, seg, bounds, rates, heads, hd
+    mean_all = move.gather_seq(mean_own).reshape(length, 1)
+    grad_first = dot(after(n2_all, mean_own), dg1, 0, 0).astype(LOW)
+    grad_second = dot(after(n2_all, grad_first), dg2, 0, 0).astype(LOW)
+
+    dj = dot(dh_all, after(full_out, grad_second), 1, 1)
+    dz, o = attend_back(z, a, dj, ra_all, mean_all, states, seg, bounds, rates, heads, hd)
+    dn1_sum = product_scatter([(dz, full_attn, 1)])
+    grad_attn = dot(after(n1_all, dn1_sum.term), dz, 0, 0).astype(LOW)
+    grad_out = dot(after(o, grad_attn), dh_all, 0, 0).astype(LOW)
+    dn1 = dn1_sum.done(grad_out)
+    input_grad = dh + r1 * (dn1 - n1 * jnp.mean(dn1 * n1, axis=-1, keepdims=True))
+    loss_own = after(jnp.sum(keep * error * error).reshape(1, 1), dhb)
+    loss = move.sum_all(loss_own) / (width * count)
+
+    share_down, share_first, share_second, share_out, *share_attn = scatter_all(
+        shape, heads, hd, (grad_down, grad_first, grad_second, grad_attn, grad_out)
     )
-    grad_out = dot(o, dh_all, 0, 0).astype(LOW)
-    grad_attn = dot(n1_all, dz, 0, 0).astype(LOW)
-    dn1 = scatter_product([(dz, full_attn, 1)])
-    input_grad = dh + r1 * (dn1 - n1 * jnp.mean(dn1 * n1, axis=-1, keepdims=True))
-
-    share_down = move.scatter_fsdp(grad_down, 1)[0]
-    share_first = move.scatter_fsdp(grad_first, seq).astype(LOW)
-    share_second = move.scatter_fsdp(grad_second, seq).astype(LOW)
-    share_first = move.swap_seq(share_first).transpose(1, 0, 2).reshape(own_rows, ff).astype(WIDE)
-    share_second = move.swap_seq(share_second).transpose(1, 0, 2).reshape(own_rows, ff).astype(WIDE)
-    share_out = move.scatter_fsdp(grad_out, 1)[0]
-    share_attn = move.swap_seq(move.scatter_fsdp(grad_attn, seq).astype(LOW))
-    share_attn = share_attn.reshape(seq, own_rows, heads, 4, hd).transpose(3, 1, 0, 2, 4)
-    share_attn = share_attn.reshape(4, own_rows, width).astype(WIDE)
 
     return (
         layer_out,

time: 1480 us -> 1420 us (0.959)
  Pallas kernels: 37.8 us -> 678 us
  waiting for transfers between devices: 758 us -> 223 us
  local copies, waits for them, and re-layouts: 175 us -> 53.7 us
  starting transfers between devices: 150 us -> 113 us
    pallas_call x0 -> x7, Pallas kernels: none -> 640 us  [the longest x1 325 us: gather_all(): pl.pallas_call(functools.partial(gather_kernel, shape), in_specs=[HBM] *...]
    ppermute x95 -> x12, waiting for transfers between devices: 616 us -> 59.1 us  [sum_axis(): v = v + lax.ppermute(v, axis, [(i, i ^ step) for i in range(size)])]
    dynamic_update_slice x78 -> x13, local copies, waits for them, and re-layouts: 87.7 us -> 25.4 us  [gather_seq(): lax.dynamic_update_slice_in_dim(whole, part, i * t, 0)]
    ppermute x95 -> x12, starting transfers between devices: 136 us -> 99.3 us  [sum_axis(): v = v + lax.ppermute(v, axis, [(i, i ^ step) for i in range(size)])]
    another operation x22 -> x2, local copies, waits for them, and re-layouts: 31.9 us -> 2.12 us  [the longest x1 2.04 us: attend(): seg.reshape(length, 1)]
    ppermute x11 -> x8, waiting for transfers between devices: 140 us -> 163 us  [to_chip(): return lax.ppermute(v, 'seq', self.chip_perm)]
  transfers between devices with their start and end apart: 128 -> 36, of which waited for: 55 -> 17; matrix products, arithmetic and copies ran while one was open for 22% -> 8% of each run, Pallas kernels for 3% -> 22%
where the time goes in v2:
time: 1420 us; the launch traced here: 1410 us
  Pallas kernels  678 us (48%)
  matrix products  266 us (19%)
  waiting for transfers between devices  223 us (16%)
  starting transfers between devices  113 us (8%)
  other arithmetic  63.5 us (4%)
  local copies, waits for them, and re-layouts  53.7 us (4%)
    pallas_call x1, Pallas kernels, gather_all(): pl.pallas_call(functools.partial(gather_kernel, shape), in_specs=[HBM] *...  325 us
    pallas_call x1, Pallas kernels, scatter_all(): pl.pallas_call(functools.partial(scatter_kernel, shape, heads, hd), in_sp...  311 us
    dot_general x20, matrix products, dot(): lax.dot_general(left, right, (((left_dim,), (right_dim,)), ((), ())), pre...  266 us
    ppermute x8, waiting for transfers between devices, to_chip(): return lax.ppermute(v, 'seq', self.chip_perm)  163 us
    ppermute x12, starting transfers between devices, sum_axis(): v = v + lax.ppermute(v, axis, [(i, i ^ step) for i in range(size)])  99.3 us
    ppermute x12, waiting for transfers between devices, sum_axis(): v = v + lax.ppermute(v, axis, [(i, i ^ step) for i in range(size)])  59.1 us
  transfers between devices with their start and end apart: 36, of which 17 were waited for; matrix products, arithmetic and copies ran while one was open for 8% of the time, Pallas kernels for 22%

profile of v2, /device:TPU:0, one launch (start us, length us, event | category | flops | bytes accessed | tf_op | source)
XLA Modules:
  0.0 1407.9 jit_solution(16144424863763093119)
XLA Ops:
  2.8 3.3 fusion.2.n1_ref
  6.1 3.2 pack_columns.1
  9.3 324.9 %gather_all.1 = (bf16[4,64,2048]{2,1,0:T(8,128)(2,1)}, bf16[4,64,1408]{2,1,0:T(8,128)(2,1)}, bf16[4,64,1408]{2,1,0:T(8,128)(2,1)}, bf16[4,4,2,64,2048]{4,3,2,1,0...) custom-call(bf16[4,64,2048]{2,1,0:T(8,128)(2,1)} %get-tuple-element., ...), custom_call_target="tpu_custom_call" | custom-call | tf_op jit(solution)/shard_map/gather_all/pallas_call | solution.py:463
  337.0 24.2 %fusion.51.z_ref = f32[2048,2048]{1,0:T(8,128)} fusion(bf16[2048,2048]{1,0:T(8,128)(2,1)} %get-tuple-element.72, bf16[2048,2048]{1,0:T(8,128)(2,1)} %bitcast.177), kind=kOutput, calls=%fused_computation.113 | convolution fusion | flops 17179869184 | bytes 33554432 | tf_op jit(solution)/shard_map/dot_general | solution.py:17
  362.5 16.9 %attend.1 = (bf16[2048,512]{1,0:T(8,128)(2,1)}, f32[2048,512]{1,0:T(8,128)}, f32[2048,1]{1,0:T(8,128)}, bf16[8,4,128,128]{3,2,1,0:T(8,128)(2,1)}) custom-call(f32[4]{0:T(128)} %dynamic_slice.83.rate_ref, s32[9]{0:T(128)} %pad_add_fusion.bounds_ref, s32[2048,1]{1,0:T(8,128)} %copy.24.segc_ref, s32[1,2048]{1,0:T(1,128)} %bitcast.167, f32[2048,2048]{1,0:T(8,128)} %fusion.51.z_ref), custom_call_target="tpu_custom_call" | custom-call | flops 1610612736 | bytes 23068672 | tf_op jit(solution)/shard_map/attend/pallas_call | solution.py:84
  379.4 3.6 convolution_convert_fusion.6
  386.5 4.3 convolution_convert_fusion.7
  394.7 3.8 fusion.17
  402.2 44.7 %collective-permute-done.4 = f32[2048]{0:T(1024)S(1)} collective-permute-done((f32[2048]{0:T(1024)S(1)}, f32[2048]{0:T(1024)S(1)}, u32[]{:S(2)}, u32[]{:S(2)}) %collective-permute-start.4) | collective-permute-done | bytes 8224 | tf_op jit(solution)/shard_map/ppermute | solution.py:680
  447.5 4.3 multiply_reduce_fusion.2
  456.3 45.4 %collective-permute-done.6 = bf16[512,2048]{1,0:T(8,128)(2,1)} collective-permute-done((bf16[512,2048]{1,0:T(8,128)(2,1)S(1)}, bf16[512,2048]{1,0:T(8,128)(2,1)}, u32[]{:S(2)}, u32[]{:S(2)}) %collective-permute-start.6) | collective-permute-done | bytes 2097184 | tf_op jit(solution)/shard_map/ppermute | solution.py:655
  501.7 3.4 constant_dynamic-update-slice_fusion.14
  505.0 3.3 constant_dynamic-update-slice_fusion.13
  511.6 17.0 %fusion.52 = f32[2048,1408]{1,0:T(8,128)} fusion(bf16[2048,2048]{1,0:T(8,128)(2,1)} %constant_dynamic-update-slice_fusion.12, bf16[2048,1408]{1,0:T(8,128)(2,1)S(1)} %bitcast.185), kind=kOutput, calls=%fused_computation.114 | convolution fusion | flops 11811160064 | bytes 25690112 | tf_op jit(solution)/shard_map/dot_general | solution.py:17
  528.6 19.1 %multiply_convert_fusion.2 = (bf16[2048,1408]{1,0:T(8,128)(2,1)}, bf16[2048,1408]{1,0:T(8,128)(2,1)}) fusion(f32[2048,1408]{1,0:T(8,128)} %fusion.52, bf16[2048,2048]{1,0:T(8,128)(2,1)S(1)} %copy-done.11, bf16[2048,1408]{1,0:T(8,128)(2,1)} %bitcast.189), kind=kOutput, calls=%fused_computation.2 | convolution fusion | flops 11819810816 | bytes 37224448 | tf_op jit(solution)/shard_map/dot_general | solution.py:17
  547.7 10.1 convolution_convert_fusion.4
  558.6 8.7 convolution_convert_fusion.5
  575.7 42.6 %collective-permute-start.12 = (f32[1,1]{1,0:T(1,128)}, f32[1,1]{1,0:T(1,128)}, u32[]{:S(2)}, u32[]{:S(2)}) collective-permute-start(f32[1,1]{1,0:T(1,128)} %add.265), channel_id=1, source_target_pairs={{0,16},{8,24},{16,0},{24,8},{1,17},{9,25},{17,1},{25,9},{2,18},{10... | collective-permute-start | bytes 20 | tf_op jit(solution)/shard_map/ppermute | solution.py:680
  628.6 3.5 collective-permute-start.15
  633.9 9.1 constant_dynamic-update-slice_fusion.11
  644.5 41.6 %collective-permute-done.17 = bf16[512,2048]{1,0:T(8,128)(2,1)S(1)} collective-permute-done((bf16[512,2048]{1,0:T(8,128)(2,1)S(1)}, bf16[512,2048]{1,0:T(8,128)(2,1)S(1)}, u32[]{:S(2)}, u32[]{:S(2)}) %collective-permute-start.17) | collective-permute-done | bytes 2097184 | tf_op jit(solution)/shard_map/ppermute | solution.py:655
  691.8 23.4 %multiply_convert_fusion = (bf16[2048,1408]{1,0:T(8,128)(2,1)}, bf16[2048,1408]{1,0:T(8,128)(2,1)}) fusion(bf16[2048,1408]{1,0:T(8,128)(2,1)} %get-tuple-element.98, f32[2048,1408]{1,0:T(8,128)} %fusion.52, bf16[2048,2048]{1,0:T(8,128)(2,1)} %constant_dynamic-update-slice_fusion.8, bf16[1408,2048]{1,0:T(8,128)(2,1)} %bitcast.194), kind=kOutput, calls=%fused_computation | convolution fusion | flops 11831345152 | bytes 42991616 | tf_op jit(solution)/shard_map/dot_general | solution.py:17
  715.1 11.8 fusion.34
  727.0 11.0 add_convert_fusion.1
  738.0 16.8 %convolution_convert_fusion.3 = bf16[1408,2048]{1,0:T(8,128)(2,1)} fusion(bf16[2048,1408]{1,0:T(8,128)(2,1)} %get-tuple-element.60, bf16[2048,2048]{1,0:T(8,128)(2,1)S(1)} %bitcast.144), kind=kOutput, calls=%fused_computation.8 | convolution fusion | flops 11814043648 | bytes 19922944 | tf_op jit(solution)/shard_map/dot_general | solution.py:17
  754.8 12.1 fusion.31
  767.3 10.0 add_convert_fusion
  785.5 43.9 %collective-permute-done.21 = bf16[512,2048]{1,0:T(8,128)(2,1)} collective-permute-done((bf16[512,2048]{1,0:T(8,128)(2,1)}, bf16[512,2048]{1,0:T(8,128)(2,1)}, u32[]{:S(2)}, u32[]{:S(2)}) %collective-permute-start.21) | collective-permute-done | bytes 2097184 | tf_op jit(solution)/shard_map/ppermute | solution.py:655
  829.4 5.3 multiply_reduce_fusion.1
  834.8 7.5 constant_dynamic-update-slice_fusion.7
  842.4 4.5 multiply_reduce_fusion
  849.2 15.8 %convolution_convert_fusion.2 = bf16[2048,1408]{1,0:T(8,128)(2,1)} fusion(bf16[2048,2048]{1,0:T(8,128)(2,1)S(1)} %bitcast.146, bf16[2048,1408]{1,0:T(8,128)(2,1)S(1)} %bitcast.199), kind=kOutput, calls=%fused_computation.7 | convolution fusion | flops 11814043648 | bytes 19922944 | tf_op jit(solution)/shard_map/dot_general | solution.py:17
  865.0 32.1 %collective-permute-done.28 = bf16[512,2048]{1,0:T(8,128)(2,1)} collective-permute-done((bf16[512,2048]{1,0:T(8,128)(2,1)}, bf16[512,2048]{1,0:T(8,128)(2,1)}, u32[]{:S(2)}, u32[]{:S(2)}) %collective-permute-start.28) | collective-permute-done | bytes 2097184 | tf_op jit(solution)/shard_map/ppermute | solution.py:655
  897.1 15.7 %convolution_convert_fusion.1 = bf16[2048,1408]{1,0:T(8,128)(2,1)} fusion(bf16[2048,2048]{1,0:T(8,128)(2,1)S(1)} %bitcast.146, bf16[2048,1408]{1,0:T(8,128)(2,1)S(1)} %bitcast.201), kind=kOutput, calls=%fused_computation.6 | convolution fusion | flops 11814043648 | bytes 19922944 | tf_op jit(solution)/shard_map/dot_general | solution.py:17
  915.7 3.5 constant_dynamic-update-slice_fusion.6
  919.2 3.3 constant_dynamic-update-slice_fusion.5
  922.5 3.2 constant_dynamic-update-slice_fusion.4
  925.7 9.8 fusion.53.dj_ref
  935.5 21.6 %attend_back.1 = (bf16[2048,2048]{1,0:T(8,128)(2,1)}, bf16[2048,512]{1,0:T(8,128)(2,1)}) custom-call(f32[4]{0:T(128)} %dynamic_slice.83.rate_ref, s32[9]{0:T(128)} %pad_add_fusion.bounds_ref, s32[2048,1]{1,0:T(8,128)} %copy.24.segc_ref, s32[1,2048]{1,0:T(1,128)} %bitcast.168, f32[2048,2048]{1,0:T(8,128)} %fusion.51.z_ref, ...), custom_call_target="tpu_custom_call" | custom-call | flops 3221225472 | bytes 35651584 | tf_op jit(solution)/shard_map/attend_back/pallas_call | solution.py:189
  957.1 12.7 fusion.24
  969.9 21.5 %convolution_convert_fusion = bf16[2048,2048]{1,0:T(8,128)(2,1)} fusion(bf16[2048,2048]{1,0:T(8,128)(2,1)S(1)} %bitcast.181, bf16[2048,2048]{1,0:T(8,128)(2,1)} %get-tuple-element.74), kind=kOutput, calls=%fused_computation.5 | convolution fusion | flops 17184063488 | bytes 25165824 | tf_op jit(solution)/shard_map/dot_general | solution.py:17
  991.4 5.9 convolution_convert_fusion.8
  997.8 12.9 fusion.27
  1020.9 39.7 %collective-permute-start.23 = (f32[1,1]{1,0:T(1,128)}, f32[1,1]{1,0:T(1,128)}, u32[]{:S(2)}, u32[]{:S(2)}) collective-permute-start(f32[1,1]{1,0:T(1,128)} %add.276), channel_id=1, source_target_pairs={{0,16},{8,24},{16,0},{24,8},{1,17},{9,25},{17,1},{25,9},{2,18},{10... | collective-permute-start | bytes 20 | tf_op jit(solution)/shard_map/ppermute | solution.py:680
  1072.0 3.5 collective-permute-start.26
  1077.2 311.5 %scatter_all.1 = (f32[176,2048]{1,0:T(8,128)}, f32[64,5632]{1,0:T(8,128)}, f32[64,5632]{1,0:T(8,128)}, f32[64,2048]{1,0:T(8,128)}, f32[64,2048]{1,0:T(8,128)}, /...) custom-call(bf16[1,4,2,176,2048]{4,3,2,1,0:T(8,128)(2,1)} %bitcast.1, ...), custom_call_target="tpu_custom_call" | custom-call | tf_op jit(solution)/shard_map/scatter_all/pallas_call | solution.py:609
  1388.8 3.7 fusion.3
  1392.5 6.8 fusion.7
  (239 shorter events, 91.6 us)
Async XLA Ops:
  2.8 331.4 %copy-start.28 = (f32[512]{0:T(512)}, f32[512]{0:T(512)S(1)}, u32[]{:S(2)}) copy-start(f32[512]{0:T(512)S(1)} %add_rsqrt_fusion.2) | copy-start | bytes 6148
  386.5 8.2 collective-permute-start.1
  394.2 52.7 %collective-permute-start = (bf16[512,2048]{1,0:T(8,128)(2,1)}, bf16[512,2048]{1,0:T(8,128)(2,1)}, u32[]{:S(2)}, u32[]{:S(2)}) collective-permute-start(bf16[512,2048]{1,0:T(8,128)(2,1)} %dynamic-slice_bitcast_fusion.7), channel_id=1, source_target_pairs={{0,8},{8,0},{16,24},{24,16},{1,9},{9,1},{17,25},{25,17},{2,10},{10... | collective-permute-start | bytes 6291464 | tf_op jit(solution)/shard_map/ppermute | solution.py:652
  398.5 48.9 %collective-permute-start.2 = (bf16[512,2048]{1,0:T(8,128)(2,1)}, bf16[512,2048]{1,0:T(8,128)(2,1)}, u32[]{:S(2)}, u32[]{:S(2)}) collective-permute-start(bf16[512,2048]{1,0:T(8,128)(2,1)} %fusion.17), channel_id=1, source_target_pairs={{0,16},{8,24},{16,0},{24,8},{1,17},{9,25},{17,1},{25,9},{2,18},{10... | collective-permute-start | bytes 6291464 | tf_op jit(solution)/shard_map/ppermute | solution.py:655
  400.9 1.2 collective-permute-start.3
  402.1 44.7 %collective-permute-start.4 = (f32[2048]{0:T(1024)S(1)}, f32[2048]{0:T(1024)S(1)}, u32[]{:S(2)}, u32[]{:S(2)}) collective-permute-start(f32[2048]{0:T(1024)S(1)} %add.245), channel_id=1, source_target_pairs={{0,16},{8,24},{16,0},{24,8},{1,17},{9,25},{17,1},{25,9},{2,18},{10... | collective-permute-start | bytes 24584 | tf_op jit(solution)/shard_map/ppermute | solution.py:680
  402.1 45.3 %copy-start.2 = (bf16[1,512,2048]{2,1,0:T(8,128)(2,1)S(1)}, bf16[1,512,2048]{2,1,0:T(8,128)(2,1)}, u32[]{:S(2)}) copy-start(bf16[1,512,2048]{2,1,0:T(8,128)(2,1)} %param.13) | copy-start | bytes 6291460
  454.5 47.2 %collective-permute-start.6 = (bf16[512,2048]{1,0:T(8,128)(2,1)S(1)}, bf16[512,2048]{1,0:T(8,128)(2,1)}, u32[]{:S(2)}, u32[]{:S(2)}) collective-permute-start(bf16[512,2048]{1,0:T(8,128)(2,1)S(1)} %get-tuple-element.90), channel_id=1, source_target_pairs={{0,16},{8,24},{16,0},{24,8},{1,17},{9,25},{17,1},{25,9},{2,18},{10... | collective-permute-start | bytes 6291464 | tf_op jit(solution)/shard_map/ppermute | solution.py:655
  456.3 45.4 %collective-permute-start.5 = (bf16[512,2048]{1,0:T(8,128)(2,1)S(1)}, bf16[512,2048]{1,0:T(8,128)(2,1)}, u32[]{:S(2)}, u32[]{:S(2)}) collective-permute-start(bf16[512,2048]{1,0:T(8,128)(2,1)S(1)} %get-tuple-element.90), channel_id=1, source_target_pairs={{0,8},{8,0},{16,24},{24,16},{1,9},{9,1},{17,25},{25,17},{2,10},{10... | collective-permute-start | bytes 6291464 | tf_op jit(solution)/shard_map/ppermute | solution.py:652
  501.7 6.7 collective-permute-start.7
  558.1 10.9 collective-permute-start.9
  568.9 64.9 %collective-permute-start.8 = (bf16[512,2048]{1,0:T(8,128)(2,1)}, bf16[512,2048]{1,0:T(8,128)(2,1)}, u32[]{:S(2)}, u32[]{:S(2)}) collective-permute-start(bf16[512,2048]{1,0:T(8,128)(2,1)} %dynamic-slice_bitcast_fusion.5), channel_id=1, source_target_pairs={{0,8},{8,0},{16,24},{24,16},{1,9},{9,1},{17,25},{25,17},{2,10},{10... | collective-permute-start | bytes 6291464 | tf_op jit(solution)/shard_map/ppermute | solution.py:652
  571.1 62.7 %collective-permute-start.10 = (bf16[512,2048]{1,0:T(8,128)(2,1)}, bf16[512,2048]{1,0:T(8,128)(2,1)}, u32[]{:S(2)}, u32[]{:S(2)}) collective-permute-start(bf16[512,2048]{1,0:T(8,128)(2,1)} %fusion.14), channel_id=1, source_target_pairs={{0,16},{8,24},{16,0},{24,8},{1,17},{9,25},{17,1},{25,9},{2,18},{10... | collective-permute-start | bytes 6291464 | tf_op jit(solution)/shard_map/ppermute | solution.py:655
  573.1 1.4 collective-permute-start.11
  573.3 60.5 %copy-start.30 = (f32[1,512]{1,0:T(1,128)}, f32[1,512]{1,0:T(1,128)S(1)}, u32[]{:S(2)}) copy-start(f32[1,512]{1,0:T(1,128)S(1)} %convert_element_type.215) | copy-start | bytes 6148
  573.3 60.5 %copy-start.6 = (bf16[1,512,2048]{2,1,0:T(8,128)(2,1)S(1)}, bf16[1,512,2048]{2,1,0:T(8,128)(2,1)}, u32[]{:S(2)}) copy-start(bf16[1,512,2048]{2,1,0:T(8,128)(2,1)} %param.14) | copy-start | bytes 6291460
  575.7 43.7 %collective-permute-start.12 = (f32[1,1]{1,0:T(1,128)}, f32[1,1]{1,0:T(1,128)}, u32[]{:S(2)}, u32[]{:S(2)}) collective-permute-start(f32[1,1]{1,0:T(1,128)} %add.265), channel_id=1, source_target_pairs={{0,16},{8,24},{16,0},{24,8},{1,17},{9,25},{17,1},{25,9},{2,18},{10... | collective-permute-start | bytes 20 | tf_op jit(solution)/shard_map/ppermute | solution.py:680
  620.0 3.7 collective-permute-start.13
  624.3 3.7 collective-permute-start.14
  628.6 4.6 collective-permute-start.15
  643.0 43.1 %collective-permute-start.17 = (bf16[512,2048]{1,0:T(8,128)(2,1)S(1)}, bf16[512,2048]{1,0:T(8,128)(2,1)S(1)}, u32[]{:S(2)}, u32[]{:S(2)}) collective-permute-start(bf16[512,2048]{1,0:T(8,128)(2,1)S(1)} %get-tuple-element.87), channel_id=1, source_target_pairs={{0,16},{8,24},{16,0},{24,8},{1,17},{9,25},{17,1},{25,9},{2,18},{10... | collective-permute-start | bytes 6291464 | tf_op jit(solution)/shard_map/ppermute | solution.py:655
  644.5 41.6 %collective-permute-start.16 = (bf16[512,2048]{1,0:T(8,128)(2,1)S(1)}, bf16[512,2048]{1,0:T(8,128)(2,1)S(1)}, u32[]{:S(2)}, u32[]{:S(2)}) collective-permute-start(bf16[512,2048]{1,0:T(8,128)(2,1)S(1)} %get-tuple-element.87), channel_id=1, source_target_pairs={{0,8},{8,0},{16,24},{24,16},{1,9},{9,1},{17,25},{25,17},{2,10},{10... | collective-permute-start | bytes 6291464 | tf_op jit(solution)/shard_map/ppermute | solution.py:652
  686.1 4.2 collective-permute-start.18
  726.9 40.3 %slice-start.10 = ((s8[5767168]{0:T(1024)(128)(4,1)}), s8[4194304]{0:T(1024)(128)(4,1)S(1)}, s32[]{:S(2)}) async-start(s8[5767168]{0:T(1024)(128)(4,1)} %bitcast.186), calls=%async_computation.10 | async-start | bytes 8388608
  767.1 12.2 collective-permute-start.20
  778.9 6.6 collective-permute-start.19
  781.5 47.9 %copy-start.27 = (f32[512]{0:T(512)S(1)}, f32[512]{0:T(512)}, u32[]{:S(2)}) copy-start(f32[512]{0:T(512)} %copy-done.26) | copy-start | bytes 6148
  781.5 47.9 %collective-permute-start.21 = (bf16[512,2048]{1,0:T(8,128)(2,1)}, bf16[512,2048]{1,0:T(8,128)(2,1)}, u32[]{:S(2)}, u32[]{:S(2)}) collective-permute-start(bf16[512,2048]{1,0:T(8,128)(2,1)} %fusion.12), channel_id=1, source_target_pairs={{0,16},{8,24},{16,0},{24,8},{1,17},{9,25},{17,1},{25,9},{2,18},{10... | collective-permute-start | bytes 6291464 | tf_op jit(solution)/shard_map/ppermute | solution.py:655
  785.5 49.2 %copy-start.1 = (f32[512,2048]{1,0:T(8,128)S(1)}, f32[512,2048]{1,0:T(8,128)}, u32[]{:S(2)}) copy-start(f32[512,2048]{1,0:T(8,128)} %copy-done) | copy-start | bytes 12582916
  785.5 49.2 %copy-start.4 = (f32[512,2048]{1,0:T(8,128)S(1)}, f32[512,2048]{1,0:T(8,128)}, u32[]{:S(2)}) copy-start(f32[512,2048]{1,0:T(8,128)} %get-tuple-element.88) | copy-start | bytes 12582916
  846.8 50.2 %slice-start.14 = ((s8[5767168]{0:T(1024)(128)(4,1)}), s8[4194304]{0:T(1024)(128)(4,1)S(1)}, s32[]{:S(2)}) async-start(s8[5767168]{0:T(1024)(128)(4,1)} %bitcast.200), calls=%async_computation.14 | async-start | bytes 8388608
  846.9 50.2 %slice-start.15 = ((s8[5767168]{0:T(1024)(128)(4,1)}), s8[1572864]{0:T(1024)(128)(4,1)S(1)}, s32[]{:S(2)}) async-start(s8[5767168]{0:T(1024)(128)(4,1)} %bitcast.200), calls=%async_computation.15 | async-start | bytes 3145728
  846.9 66.1 %collective-permute-start.30 = (f32[512]{0:T(512)S(1)}, f32[512]{0:T(512)S(1)}, u32[]{:S(2)}, u32[]{:S(2)}) collective-permute-start(f32[512]{0:T(512)S(1)} %broadcast_multiply_fusion.2), channel_id=1, source_target_pairs={{0,8},{8,0},{16,24},{24,16},{1,9},{9,1},{17,25},{25,17},{2,10},{10... | collective-permute-start | bytes 6152 | tf_op jit(solution)/shard_map/ppermute | solution.py:652
  846.9 66.2 %collective-permute-start.31 = (f32[512]{0:T(512)S(1)}, f32[512]{0:T(512)S(1)}, u32[]{:S(2)}, u32[]{:S(2)}) collective-permute-start(f32[512]{0:T(512)S(1)} %broadcast_multiply_fusion.2), channel_id=1, source_target_pairs={{0,16},{8,24},{16,0},{24,8},{1,17},{9,25},{17,1},{25,9},{2,18},{10... | collective-permute-start | bytes 6152 | tf_op jit(solution)/shard_map/ppermute | solution.py:655
  848.7 66.9 %collective-permute-start.27 = (bf16[512,2048]{1,0:T(8,128)(2,1)}, bf16[512,2048]{1,0:T(8,128)(2,1)}, u32[]{:S(2)}, u32[]{:S(2)}) collective-permute-start(bf16[512,2048]{1,0:T(8,128)(2,1)} %get-tuple-element.65), channel_id=1, source_target_pairs={{0,8},{8,0},{16,24},{24,16},{1,9},{9,1},{17,25},{25,17},{2,10},{10... | collective-permute-start | bytes 6291464 | tf_op jit(solution)/shard_map/ppermute | solution.py:652
  848.9 48.2 %collective-permute-start.28 = (bf16[512,2048]{1,0:T(8,128)(2,1)}, bf16[512,2048]{1,0:T(8,128)(2,1)}, u32[]{:S(2)}, u32[]{:S(2)}) collective-permute-start(bf16[512,2048]{1,0:T(8,128)(2,1)} %get-tuple-element.65), channel_id=1, source_target_pairs={{0,16},{8,24},{16,0},{24,8},{1,17},{9,25},{17,1},{25,9},{2,18},{10... | collective-permute-start | bytes 6291464 | tf_op jit(solution)/shard_map/ppermute | solution.py:655
  897.1 25.4 %collective-permute-start.29 = (bf16[512,2048]{1,0:T(8,128)(2,1)}, bf16[512,2048]{1,0:T(8,128)(2,1)}, u32[]{:S(2)}, u32[]{:S(2)}) collective-permute-start(bf16[512,2048]{1,0:T(8,128)(2,1)} %collective-permute-done.28), channel_id=1, source_target_pairs={{0,8},{8,0},{16,24},{24,16},{1,9},{9,1},{17,25},{25,17},{2,10},{10... | collective-permute-start | bytes 6291464 | tf_op jit(solution)/shard_map/ppermute | solution.py:652
  914.0 1.5 collective-permute-start.32
  997.6 15.1 %collective-permute-start.34 = (bf16[512,2048]{1,0:T(8,128)(2,1)S(1)}, bf16[512,2048]{1,0:T(8,128)(2,1)S(1)}, u32[]{:S(2)}, u32[]{:S(2)}) collective-permute-start(bf16[512,2048]{1,0:T(8,128)(2,1)S(1)} %dynamic-slice_bitcast_fusion), channel_id=1, source_target_pairs={{0,8},{8,0},{16,24},{24,16},{1,9},{9,1},{17,25},{25,17},{2,10},{10... | collective-permute-start | bytes 6291464 | tf_op jit(solution)/shard_map/ppermute | solution.py:652
  1012.3 376.4 %collective-permute-start.33 = (bf16[512,2048]{1,0:T(8,128)(2,1)}, bf16[512,2048]{1,0:T(8,128)(2,1)}, u32[]{:S(2)}, u32[]{:S(2)}) collective-permute-start(bf16[512,2048]{1,0:T(8,128)(2,1)} %dynamic-slice_bitcast_fusion.1), channel_id=1, source_target_pairs={{0,8},{8,0},{16,24},{24,16},{1,9},{9,1},{17,25},{25,17},{2,10},{10... | collective-permute-start | bytes 6291464 | tf_op jit(solution)/shard_map/ppermute | solution.py:652
  1014.8 374.0 %collective-permute-start.35 = (bf16[512,2048]{1,0:T(8,128)(2,1)}, bf16[512,2048]{1,0:T(8,128)(2,1)}, u32[]{:S(2)}, u32[]{:S(2)}) collective-permute-start(bf16[512,2048]{1,0:T(8,128)(2,1)} %fusion.10), channel_id=1, source_target_pairs={{0,16},{8,24},{16,0},{24,8},{1,17},{9,25},{17,1},{25,9},{2,18},{10... | collective-permute-start | bytes 6291464 | tf_op jit(solution)/shard_map/ppermute | solution.py:655
  1018.3 1.4 collective-permute-start.22
  1020.9 42.0 %collective-permute-start.23 = (f32[1,1]{1,0:T(1,128)}, f32[1,1]{1,0:T(1,128)}, u32[]{:S(2)}, u32[]{:S(2)}) collective-permute-start(f32[1,1]{1,0:T(1,128)} %add.276), channel_id=1, source_target_pairs={{0,16},{8,24},{16,0},{24,8},{1,17},{9,25},{17,1},{25,9},{2,18},{10... | collective-permute-start | bytes 20 | tf_op jit(solution)/shard_map/ppermute | solution.py:680
  1063.5 3.7 collective-permute-start.24
  1067.7 3.7 collective-permute-start.25
  1072.0 4.6 collective-permute-start.26
  1077.2 311.6 %copy-start.3 = (bf16[1,512,2048]{2,1,0:T(8,128)(2,1)S(1)}, bf16[1,512,2048]{2,1,0:T(8,128)(2,1)}, u32[]{:S(2)}) copy-start(bf16[1,512,2048]{2,1,0:T(8,128)(2,1)} %param.13) | copy-start | bytes 6291460
  1077.2 311.6 %copy-start.29 = (f32[512]{0:T(512)S(1)}, f32[512]{0:T(512)}, u32[]{:S(2)}) copy-start(f32[512]{0:T(512)} %copy-done.28) | copy-start | bytes 6148
  (44 other events, 463.7 us)

commit v3 on v2

--- a/solution.py
+++ b/solution.py
@@ -10,7 +10,7 @@
 CHUNK = 256
 WIDE = jnp.float32
 LOW = jnp.bfloat16
-VMEM_BYTES = 56 * 1024 * 1024
+VMEM_BYTES = 60 * 1024 * 1024
 
 
 def dot(left, right, left_dim=1, right_dim=0):
@@ -120,31 +120,11 @@
     return sg * (1.0 + z * (1.0 - sg))
 
 
-def attend_back_kernel(
-    heads,
-    hd,
-    count,
-    rate_ref,
-    bounds_ref,
-    segc_ref,
-    segr_ref,
-    z_ref,
-    a_ref,
-    dj_ref,
-    ra_ref,
-    m_ref,
-    st_ref,
-    dz_ref,
-    o_ref,
-    later,
+def attend_back(
+    heads, hd, n, rate_ref, bounds_ref, segc_ref, segr_ref, z_ref, a_ref, dj_ref, ra_ref, m_ref,
+    st_ref, dz_ref, o_ref, later
 ):
-    n = count - 1 - pl.program_id(0)
     chunk = z_ref.shape[0]
-
-    @pl.when(pl.program_id(0) == 0)
-    def _():
-        later[...] = jnp.zeros_like(later)
-
     inner, entry_on, tail_on, carry = masks(bounds_ref, segc_ref[...], segr_ref[...], n, chunk)
     place_col, place_row = places(chunk)
     ra = ra_ref[...]
@@ -182,42 +162,6 @@
         dz_ref[:, base + 3 * hd : base + 4 * hd] = (dj * an * slope(zu)).astype(LOW)
 
 
-def attend_back(z, a, dj, ra, m, states, seg, bounds, rates, heads, hd):
-    length = z.shape[0]
-    count = length // CHUNK
-    block = lambda width: pl.BlockSpec((CHUNK, width), lambda n, *_: (count - 1 - n, 0))
-    return pl.pallas_call(
-        functools.partial(attend_back_kernel, heads, hd, count),
-        grid_spec=pltpu.PrefetchScalarGridSpec(
-            num_scalar_prefetch=2,
-            grid=(count,),
-            in_specs=[
-                block(1),
-                pl.BlockSpec((1, CHUNK), lambda n, *_: (0, count - 1 - n)),
-                block(heads * 4 * hd),
-                block(heads * hd),
-                block(heads * hd),
-                block(1),
-                block(1),
-                pl.BlockSpec((1, heads, hd, hd), lambda n, *_: (count - 1 - n, 0, 0, 0)),
-            ],
-            out_specs=[block(heads * 4 * hd), block(heads * hd)],
-            scratch_shapes=[pltpu.VMEM((heads, hd, hd), WIDE)],
-        ),
-        out_shape=[
-            jax.ShapeDtypeStruct((length, heads * 4 * hd), LOW),
-            jax.ShapeDtypeStruct((length, heads * hd), LOW),
-        ],
-        compiler_params=pltpu.CompilerParams(vmem_limit_bytes=VMEM_BYTES),
-        cost_estimate=pl.CostEstimate(
-            flops=length * heads * hd * CHUNK * 12,
-            bytes_accessed=length * heads * hd * 34,
-            transcendentals=length * heads * hd * 8,
-        ),
-        name="attend_back",
-    )(rates, bounds, seg.reshape(length, 1), seg.reshape(1, length), z, a, dj, ra, m, states)
-
-
 def empty(shape, kind):
     return pl.pallas_call(
         lambda out: None,
@@ -249,6 +193,28 @@
         compiler_params=pltpu.CompilerParams(vmem_limit_bytes=VMEM_BYTES),
         name="pack_columns",
     )(*weights, *glu)
+
+
+def unpack_kernel(seq, heads, hd, attn, first, second, o_first, o_second, *o_attn):
+    for i in range(seq):
+        for h in range(heads):
+            for m in range(4):
+                at, to = (h * 4 + m) * hd, (i * heads + h) * hd
+                o_attn[m][:, to : to + hd] = attn[i, :, at : at + hd].astype(WIDE)
+        for ref, out in ((first, o_first), (second, o_second)):
+            n = ref.shape[2]
+            out[:, i * n : (i + 1) * n] = ref[i].astype(WIDE)
+
+
+def unpack_columns(attn, first, second, heads, hd):
+    seq, r = attn.shape[:2]
+    shape = lambda n: jax.ShapeDtypeStruct((r, seq * n), WIDE)
+    return pl.pallas_call(
+        functools.partial(unpack_kernel, seq, heads, hd),
+        out_shape=[shape(first.shape[2]), shape(second.shape[2])] + [shape(heads * hd)] * 4,
+        compiler_params=pltpu.CompilerParams(vmem_limit_bytes=VMEM_BYTES),
+        name="unpack_columns",
+    )(attn, first, second)
 
 
 class Net:
@@ -307,6 +273,10 @@
         self.locals += 1
         copy.start()
         return copy
+
+    def left(self, copy):
+        copy.wait_send()
+        self.sent = [other for other in self.sent if other is not copy]
 
     def finish(self):
         for copy in self.sent:
@@ -400,6 +370,7 @@
     down_ref,
     n1_ref,
     seg_ref,
+    count_ref,
     attn_mid,
     first_mid,
     second_mid,
@@ -410,12 +381,17 @@
     full_down,
     n1_all,
     seg_all,
+    count_all,
+    seq_buf,
+    in_buf,
+    out_buf,
     send_sem,
     recv_sem,
     local_sem,
 ):
     net = Net(shape, send_sem, recv_sem, local_sem)
     net.barrier()
+    count = Total(net, count_ref, seq_buf, in_buf, out_buf)
     attn_swap = swap(net, attn_ref, attn_mid)
     seg_own = net.copy(seg_ref, seg_all.at[net.s])
     segs = [net.send(seg_ref, seg_all.at[net.s], net.at_seq(s)) for _, _, s in net.seq_peers()]
@@ -423,12 +399,12 @@
     second_swap = swap(net, second_ref, second_mid)
     rows = Rows(net, n1_ref, n1_all)
     arrive(attn_swap)
+    count.step()
     rings = [Ring(net, attn_mid, full_attn)]
-    rings[0].step()
     rings.append(Ring(net, out_ref, full_out))
-    rings[0].step()
-    rings[0].step()
-    rings[0].step()
+    for _ in range(net.outer):
+        rings[0].step()
+        count.step()
     arrive(first_swap)
     arrive(second_swap)
     rows.turn()
@@ -438,6 +414,7 @@
     for ring in rings[1:]:
         for _ in range(net.outer):
             ring.step()
+    count_all[...] = count.done()
     for ring in rings:
         ring.done()
     rows.done()
@@ -450,7 +427,7 @@
 HBM = pl.BlockSpec(memory_space=pl.ANY)
 
 
-def gather_all(shape, attn, first, second, w_out, w_down, n1, seg):
+def gather_all(shape, attn, first, second, w_out, w_down, n1, seg, count):
     seq, fsdp, inner = shape
     outer = fsdp // inner
     like = lambda v, lead: jax.ShapeDtypeStruct(lead + v.shape[-2:], v.dtype)
@@ -459,13 +436,16 @@
     outs += [ring(v) for v in (attn, first, second, w_out, w_down)]
     outs.append(jax.ShapeDtypeStruct((seq * n1.shape[0], n1.shape[1]), n1.dtype))
     outs.append(jax.ShapeDtypeStruct((seq,) + seg.shape, seg.dtype))
-    copies = 4 * (seq - 1) + 2 * seq + 5 * (outer * inner + outer)
+    outs.append(jax.ShapeDtypeStruct(count.shape, count.dtype))
+    copies = 4 * (seq - 1) + 2 * seq + 5 * (outer * inner + outer) + total_copies(shape)
+    in_vmem = pl.BlockSpec(memory_space=pltpu.VMEM)
     got = pl.pallas_call(
         functools.partial(gather_kernel, shape),
-        in_specs=[HBM] * 7,
-        out_specs=[HBM] * len(outs),
+        in_specs=[HBM] * 7 + [in_vmem],
+        out_specs=[HBM] * (len(outs) - 1) + [in_vmem],
         out_shape=outs,
-        scratch_shapes=[
+        scratch_shapes=total_scratch(shape)
+        + [
             pltpu.SemaphoreType.DMA((copies,)),
             pltpu.SemaphoreType.DMA((copies,)),
             pltpu.SemaphoreType.DMA((16,)),
@@ -474,15 +454,61 @@
             collective_id=0, has_side_effects=True, vmem_limit_bytes=VMEM_BYTES
         ),
         name="gather_all",
-    )(attn, first, second, w_out, w_down, n1, seg)
+    )(attn, first, second, w_out, w_down, n1, seg, count)
     flat = lambda v: v.reshape(-1, v.shape[-1])
     return [flat(v) for v in got[3:8]] + list(got[8:])
 
 
+class Total:
+    def __init__(self, net, own, seq_buf, in_buf, out_buf):
+        self.net, self.bufs, self.stage = net, (seq_buf, in_buf, out_buf), 0
+        self.coming = self.share(seq_buf, net.s, own[...], [net.at_seq(s) for _, _, s in net.seq_peers()])
+
+    def share(self, buf, at, value, devices):
+        buf[at] = value
+        return [self.net.send(buf.at[at], buf.at[at], device) for device in devices]
+
+    def gathered(self, buf):
+        for copy in self.coming:
+            copy.wait_recv()
+        total = buf[0]
+        for j in range(1, buf.shape[0]):
+            total = total + buf[j]
+        return total
+
+    def step(self):
+        net, (seq_buf, in_buf, out_buf) = self.net, self.bufs
+        if self.stage == 0:
+            peers = [net.at_inner(j) for j in range(1, net.inner)]
+            self.coming = self.share(in_buf, net.i, self.gathered(seq_buf), peers)
+        elif self.stage == 1:
+            self.coming = self.share(out_buf, net.o, self.gathered(in_buf), [net.at_outer(1)])
+        elif self.stage < net.outer:
+            self.coming[-1].wait_recv()
+            at = lax.rem(net.o + net.outer - self.stage + 1, net.outer)
+            self.coming = [net.send(out_buf.at[at], out_buf.at[at], net.at_outer(1))]
+        self.stage += 1
+
+    def done(self):
+        while self.stage < self.net.outer:
+            self.step()
+        return self.gathered(self.bufs[2])
+
+
+def total_scratch(shape):
+    seq, fsdp, inner = shape
+    return [pltpu.VMEM((n, 8, 128), WIDE) for n in (seq, inner, fsdp // inner)]
+
+
+def total_copies(shape):
+    seq, fsdp, inner = shape
+    return seq + inner + fsdp // inner
+
+
 class Sum:
-    def __init__(self, net, g, side, send, recv, load):
-        self.net, self.g, self.side_ref = net, g, side
-        self.send_buf, self.recv_buf, self.load = send, recv, load
+    def __init__(self, net, g, side, ring, send, load):
+        self.net, self.g, self.side_ref, self.ring_ref = net, g, side, ring
+        self.send_buf, self.load = send, load
         self.side = []
         self.ring = []
         for k in range(net.outer):
@@ -497,7 +523,7 @@
     def spot(self, k):
         return lax.rem(self.net.o + 2 * self.net.outer - 1 - k, self.net.outer)
 
-    def step(self, final=None):
+    def step(self, final):
         net, k = self.net, self.at
         self.at += 1
         o = self.spot(k)
@@ -506,118 +532,311 @@
         for j, copy in enumerate(self.side[k]):
             copy.wait_recv()
             loads.append(net.copy(self.side_ref.at[j, :, o], terms.at[j + 1]))
+        count = net.inner
         if k > 0:
             self.ring[k - 1].wait_recv()
+            loads.append(net.copy(self.ring_ref.at[k - 1], terms.at[count]))
+            count += 1
+        if k >= 2:
+            net.left(self.ring[k - 2])
         for load in loads:
             load.wait()
-        a = terms.shape[1]
 
         def one(i, _):
             total = terms[0, i].astype(WIDE)
-            for j in range(1, net.inner):
+            for j in range(1, count):
                 total = total + terms[j, i].astype(WIDE)
-            if k > 0:
-                total = total + self.recv_buf[k - 1, i].astype(WIDE)
             if k < net.outer - 1:
-                self.send_buf[k, i] = total.astype(LOW)
+                self.send_buf[k % 2, i] = total.astype(LOW)
             else:
                 final(i, total)
             return 0
 
-        lax.fori_loop(0, a, one, 0)
+        lax.fori_loop(0, terms.shape[1], one, 0)
         if k < net.outer - 1:
-            self.ring.append(net.send(self.send_buf.at[k], self.recv_buf.at[k], net.at_outer(1)))
-
-
-def scatter_kernel(shape, heads, hd, *refs):
-    names = ("down", "first", "second", "attn", "out")
-    it = iter(refs)
-    take = lambda: {name: next(it) for name in names}
-    grads = take()
-    o_down, o_first, o_second, o_out = (next(it) for _ in range(4))
-    o_attn = [next(it) for _ in range(4)]
-    sides, sends, recvs, loads = take(), take(), take(), take()
-    totals = {name: next(it) for name in ("first", "second", "attn")}
-    gots = {name: next(it) for name in ("first", "second", "attn")}
+            self.ring.append(net.send(self.send_buf.at[k % 2], self.ring_ref.at[k], net.at_outer(1)))
+
+
+GRADS = ("down", "first", "second", "attn", "out")
+SPLIT = ("first", "second", "attn")
+LOADS = ("down", "first", "attn", "out")
+
+
+def back_kernel(
+    shape, heads, hd,
+    rate_ref, bounds_ref, segc, segr, z, a, dh, ra, mean, states, w_out, w_attn, n1, loss_ref,
+    g_down, g_first, g_second,
+    dn1_ref, o_down, o_out, o_loss, got_first, got_second, got_attn, g_attn,
+    side_down, side_first, side_second, side_attn, side_out,
+    ring_down, ring_first, ring_second, ring_attn, ring_out,
+    core_in, chip_in,
+    dz_all, later, dj, o_chunk, out_acc, g_out, stage, term, wide_tile,
+    *rest
+):
+    it = iter(rest)
+    take = lambda names: {name: next(it) for name in names}
+    sends, loads = take(GRADS), take(LOADS)
+    loads["second"] = loads["first"]
+    total_bufs = [next(it) for _ in range(3)]
     send_sem, recv_sem, local_sem = (next(it) for _ in range(3))
     net = Net(shape, send_sem, recv_sem, local_sem)
+    grads = dict(down=g_down, first=g_first, second=g_second, attn=g_attn, out=g_out)
+    sides = dict(down=side_down, first=side_first, second=side_second, attn=side_attn, out=side_out)
+    rings = dict(down=ring_down, first=ring_first, second=ring_second, attn=ring_attn, out=ring_out)
+    gots = dict(first=got_first, second=got_second, attn=got_attn)
+    owned = dict(down=o_down, out=o_out)
+    length, cols = dz_all.shape
+    width = dh.shape[1]
+    count = length // CHUNK
+    wide = min(512, width)
+
     net.barrier()
-    sums = {n: Sum(net, grads[n], sides[n], sends[n], recvs[n], loads[n]) for n in names}
-
-    def run(name, final):
-        for k in range(net.outer):
+    sums, swaps, queue = {}, {}, []
+    loss = Total(net, loss_ref, *total_bufs)
+
+    def begin(name):
+        sums[name] = Sum(net, grads[name], sides[name], rings[name], sends[name], loads[name])
+        queue.extend([name] * net.outer)
+
+    def pump(times=1):
+        for _ in range(min(times, len(queue))):
+            name = queue.pop(0)
+
+            def final(i, rows):
+                if name in owned:
+                    owned[name][...] = rows
+                else:
+                    totals[i] = rows.astype(LOW)
+
+            totals = sends[name].at[(net.outer - 1) % 2]
             sums[name].step(final)
-
-    def keep(name):
-        def final(i, rows):
-            totals[name][i] = rows.astype(LOW)
-
-        return final
-
-    def place(ref):
-        def final(i, rows):
-            ref[...] = rows
-
-        return final
-
-    swaps = {}
-    run("down", place(o_down))
-    for name in ("first", "second", "attn"):
-        run(name, keep(name))
-        swaps[name] = swap(net, totals[name], gots[name])
-    run("out", place(o_out))
-    for name, ref in (("first", o_first), ("second", o_second)):
+            if name in SPLIT and sums[name].at == net.outer:
+                swaps[name] = swap(net, totals, gots[name])
+
+    loss.step()
+    for name in ("down", "first", "second"):
+        begin(name)
+
+    later[...] = jnp.zeros_like(later)
+    out_acc[...] = jnp.zeros_like(out_acc)
+
+    def chunks(top, steps):
+        def body(segc_ref, segr_ref, z_ref, a_ref, dh_ref, ra_ref, m_ref, st_ref):
+            n = top - pl.program_id(0)
+            dj[...] = dot(dh_ref[...], w_out[...], 1, 1)
+            rows = pl.ds(pl.multiple_of(n * CHUNK, CHUNK), CHUNK)
+            attend_back(
+                heads, hd, n, rate_ref, bounds_ref, segc_ref, segr_ref, z_ref, a_ref, dj, ra_ref,
+                m_ref, st_ref, dz_all.at[rows], o_chunk, later,
+            )
+
+            def add(j, _):
+                at = pl.ds(pl.multiple_of(j * wide, wide), wide)
+                out_acc[:, at] += dot(o_chunk[...], dh_ref[:, at], 0, 0)
+                return 0
+
+            lax.fori_loop(0, width // wide, add, 0)
+
+        block = lambda n: pl.BlockSpec((CHUNK, n), lambda i: (top - i, 0))
+        pltpu.emit_pipeline(
+            body,
+            grid=(steps,),
+            in_specs=[
+                block(1),
+                pl.BlockSpec((1, CHUNK), lambda i: (0, top - i)),
+                block(cols),
+                block(heads * hd),
+                block(width),
+                block(1),
+                block(1),
+                pl.BlockSpec((1, heads, hd, hd), lambda i: (top - i, 0, 0, 0)),
+            ],
+        )(segc, segr, z, a, dh, ra, mean, states)
+
+    half = count // 2
+    chunks(count - 1, half)
+    loss.step()
+    pump()
+    chunks(count - 1 - half, count - half)
+    loss.step()
+    pump()
+
+    own_rows = dn1_ref.shape[0]
+    tile = min(256, own_rows)
+    used = [None, None]
+    turns = [0]
+
+    def product(row, each):
+        x = dz_all[pl.ds(pl.multiple_of(row, tile), tile)]
+
+        def one(j, _):
+            at = pl.ds(pl.multiple_of(j * wide, wide), wide)
+            each(at, dot(x, w_attn[at, :], 1, 1))
+            return 0
+
+        lax.fori_loop(0, width // wide, one, 0)
+
+    def slot():
+        i = turns[0] % 2
+        turns[0] += 1
+        if used[i] is not None:
+            net.left(used[i])
+        return i
+
+    def row_of(chip, core, t):
+        return (chip * 2 + core) * own_rows + t * tile
+
+    near = {}
+    far = []
+
+    def give(dx):
+        chip = lax.rem(net.chip + dx, net.chips)
+        for t in range(own_rows // tile):
+            i = slot()
+
+            def store(at, part, i=i):
+                stage[i, :, at] = part.astype(LOW)
+
+            product(row_of(chip, 1 - net.core, t), store)
+            spot = core_in.at[dx, pl.ds(t * tile, tile)]
+            used[i] = near[dx, t] = net.send(
+                stage.at[i], spot, net.at_seq(net.chip * 2 + 1 - net.core)
+            )
+
+    def keep(dx):
+        chip = lax.rem(net.chip + dx, net.chips)
+        for t in range(own_rows // tile):
+            span = pl.ds(t * tile, tile)
+            near[dx, t].wait_recv()
+            loads = [net.copy(core_in.at[dx, span], term.at[0])]
+            if dx == 0:
+                for j, copies in enumerate(far):
+                    copies[t].wait_recv()
+                    loads.append(net.copy(chip_in.at[j, span], term.at[j + 1]))
+            else:
+                i = slot()
+            for load in loads:
+                load.wait()
+
+            def store(at, part):
+                total = part
+                for j in range(len(loads)):
+                    total = total + term[j, :, at].astype(WIDE)
+                if dx == 0:
+                    wide_tile[:, at] = total
+                else:
+                    stage[i, :, at] = total.astype(LOW)
+
+            product(row_of(chip, net.core, t), store)
+            if dx == 0:
+                net.copy(wide_tile, dn1_ref.at[span]).wait()
+            else:
+                used[i] = net.send(
+                    stage.at[i], chip_in.at[dx - 1, span], net.at_seq(chip * 2 + net.core)
+                )
+                far[dx - 1].append(used[i])
+
+    for dx in range(1, net.chips):
+        far.append([])
+        give(dx)
+        keep(dx)
+    pump()
+
+    parts = 2
+    spread = net.outer // parts
+    features = width // net.seq // parts
+
+    def grad_body(n1_ref, g_ref):
+        for j in range(cols // wide):
+            at = slice(j * wide, (j + 1) * wide)
+            got = dot(n1_ref[...], dz_all[:, at], 0, 0).astype(LOW)
+            g_ref[:, :, :, :, at] = got.reshape(g_ref.shape[:-1] + (wide,))
+
+    pltpu.emit_pipeline(
+        grad_body,
+        grid=(net.seq, parts),
+        in_specs=[pl.BlockSpec((length, features), lambda i, j: (0, i * parts + j))],
+        out_specs=[
+            pl.BlockSpec((1, spread) + g_attn.shape[2:], lambda i, j: (i, j, 0, 0, 0)),
+        ],
+    )(n1, g_attn)
+    begin("attn")
+    for j in range(width // wide):
+        at = slice(j * wide, (j + 1) * wide)
+        g_out[:, :, :, :, at] = out_acc[:, at].astype(LOW).reshape(g_out.shape[:-1] + (wide,))
+    begin("out")
+    pump(2)
+    give(0)
+    pump()
+    keep(0)
+    o_loss[...] = loss.done()
+    pump(len(queue))
+    for name in SPLIT:
         arrive(swaps[name])
-        n = gots[name].shape[2]
-        for i in range(net.seq):
-            ref[:, i * n : (i + 1) * n] = gots[name][i].astype(WIDE)
-    arrive(swaps["attn"])
-    for i in range(net.seq):
-        for h in range(heads):
-            for m in range(4):
-                at, to = (h * 4 + m) * hd, (i * heads + h) * hd
-                o_attn[m][:, to : to + hd] = gots["attn"][i, :, at : at + hd].astype(WIDE)
     net.finish()
 
 
-def scatter_all(shape, heads, hd, grads):
+def back_all(shape, heads, hd, rates, bounds, seg, z, a, dh, ra, mean, states, w_out, w_attn, n1, loss, grads):
     seq, fsdp, inner = shape
     outer = fsdp // inner
-    names = ("down", "first", "second", "attn", "out")
+    length, width = dh.shape
+    cols = z.shape[1]
+    own_rows = length // seq
+    chips = seq // 2
+    tile = min(256, own_rows)
     lead = {"down": 1, "out": 1, "first": seq, "second": seq, "attn": seq}
     blocks = [
         g.reshape(lead[n], outer, inner, g.shape[0] // (lead[n] * fsdp), g.shape[1])
-        for n, g in zip(names, grads)
+        for n, g in zip(GRADS, grads)
     ]
-    size = {n: (g.shape[0], g.shape[3], g.shape[4]) for n, g in zip(names, blocks)}
-    row = lambda n: jax.ShapeDtypeStruct((size[n][1], size[n][2]), WIDE)
-    wide = lambda n: jax.ShapeDtypeStruct((size[n][1], size[n][2] * seq), WIDE)
-    attn = jax.ShapeDtypeStruct((size["attn"][1], seq * heads * hd), WIDE)
-    outs = [row("down"), wide("first"), wide("second"), row("out")] + [attn] * 4
-    side = [
-        jax.ShapeDtypeStruct((inner - 1, size[n][0], outer) + size[n][1:], LOW) for n in names
+    size = {n: (g.shape[0], g.shape[3], g.shape[4]) for n, g in zip(GRADS, blocks)}
+    size["attn"] = (seq, width // (seq * fsdp), cols)
+    size["out"] = (1, width // (seq * fsdp), width)
+    whole = lambda n: (size[n][0], outer, inner) + size[n][1:]
+    low = lambda dims: jax.ShapeDtypeStruct(dims, LOW)
+    row = lambda n: jax.ShapeDtypeStruct(size[n][1:], WIDE)
+    outs = [jax.ShapeDtypeStruct((own_rows, width), WIDE), row("down"), row("out")]
+    outs += [jax.ShapeDtypeStruct((8, 128), WIDE)]
+    outs += [low(size[n]) for n in SPLIT] + [low(whole("attn"))]
+    outs += [low((inner - 1, size[n][0], outer) + size[n][1:]) for n in GRADS]
+    outs += [low((outer - 1,) + size[n]) for n in GRADS]
+    outs += [low((chips, own_rows, width)), low((max(chips - 1, 1), own_rows, width))]
+    in_vmem = pl.BlockSpec(memory_space=pltpu.VMEM)
+    smem = pl.BlockSpec(memory_space=pltpu.SMEM)
+    scratch = [
+        pltpu.VMEM((length, cols), LOW),
+        pltpu.VMEM((heads, hd, hd), WIDE),
+        pltpu.VMEM((CHUNK, heads * hd), WIDE),
+        pltpu.VMEM((CHUNK, heads * hd), LOW),
+        pltpu.VMEM((heads * hd, width), WIDE),
+        pltpu.VMEM(whole("out"), LOW),
+        pltpu.VMEM((2, tile, width), LOW),
+        pltpu.VMEM((chips, tile, width), LOW),
+        pltpu.VMEM((tile, width), WIDE),
     ]
-    scratch = [pltpu.VMEM((outer - 1,) + size[n], LOW) for n in names] * 2
-    scratch += [pltpu.VMEM((inner,) + size[n], LOW) for n in names]
-    scratch += [pltpu.VMEM(size[n], LOW) for n in ("first", "second", "attn")] * 2
-    copies = 5 * (outer * inner + outer) + 3 * seq
+    scratch += [pltpu.VMEM((2,) + size[n], LOW) for n in GRADS]
+    scratch += [pltpu.VMEM((inner + 1,) + size[n], LOW) for n in LOADS]
+    scratch += total_scratch(shape)
+    copies = 5 * (outer * inner + outer) + 3 * seq + total_copies(shape) + 2 * length // tile
     scratch += [
         pltpu.SemaphoreType.DMA((copies,)),
         pltpu.SemaphoreType.DMA((copies,)),
-        pltpu.SemaphoreType.DMA((5 * outer * inner + 8,)),
+        pltpu.SemaphoreType.DMA((5 * outer * (inner + 1) + 3 + 4 * length // tile,)),
     ]
-    got = pl.pallas_call(
-        functools.partial(scatter_kernel, shape, heads, hd),
-        in_specs=[HBM] * 5,
-        out_specs=[pl.BlockSpec(memory_space=pltpu.VMEM)] * len(outs) + [HBM] * 5,
-        out_shape=outs + side,
+    return pl.pallas_call(
+        functools.partial(back_kernel, shape, heads, hd),
+        in_specs=[smem, smem] + [HBM] * 8 + [in_vmem] * 2 + [HBM, in_vmem] + [HBM] * 3,
+        out_specs=[HBM] + [in_vmem] * 3 + [HBM] * (len(outs) - 4),
+        out_shape=outs,
         scratch_shapes=scratch,
         compiler_params=pltpu.CompilerParams(
             collective_id=1, has_side_effects=True, vmem_limit_bytes=VMEM_BYTES
         ),
-        name="scatter_all",
-    )(*blocks)
-    return got[:8]
+        name="back_all",
+    )(
+        rates, bounds, seg.reshape(length, 1), seg.reshape(1, length), z, a, dh, ra, mean, states,
+        w_out, w_attn, n1, loss, *blocks
+    )[:7]
 
 
 class Moves:
@@ -747,7 +966,7 @@
 
     shape = net_shape(seq, move.fsdp)
     keep = valid.astype(WIDE).reshape(block_len, 1)
-    count_own = jnp.sum(keep).reshape(1, 1)
+    spread = lambda v: jnp.broadcast_to(v, (8, 128))
 
     attn_own, first_own, second_own = pack_columns(
         (w_query, w_key, w_value, w_gate), (w_first, w_second), seq, heads, hd
@@ -755,7 +974,7 @@
     x32 = inputs.reshape(block_len, width).astype(WIDE)
     r1 = lax.rsqrt(jnp.mean(x32 * x32, axis=-1, keepdims=True) + 1e-6)
     n1 = x32 * r1
-    full_attn, full_first, full_second, full_out, full_down, n1_all, seg = gather_all(
+    full_attn, full_first, full_second, full_out, full_down, n1_all, seg, count = gather_all(
         shape,
         attn_own,
         first_own,
@@ -764,10 +983,11 @@
         w_down[None],
         n1.astype(LOW),
         segment_ids.reshape(1, block_len),
+        spread(jnp.sum(keep)),
     )
     seg = seg.reshape(seq * block_len)
     length = seg.shape[0]
-    count = move.sum_all(after(count_own, n1_all))
+    count = count[:1, :1]
 
     bounds = jnp.concatenate([jnp.full((1,), -1, jnp.int32), seg[CHUNK - 1 :: CHUNK]])
     rates = lax.dynamic_slice_in_dim(decay_rate, move.s * heads, heads, 0)
@@ -825,18 +1045,15 @@
     grad_first = dot(after(n2_all, mean_own), dg1, 0, 0).astype(LOW)
     grad_second = dot(after(n2_all, grad_first), dg2, 0, 0).astype(LOW)
 
-    dj = dot(dh_all, after(full_out, grad_second), 1, 1)
-    dz, o = attend_back(z, a, dj, ra_all, mean_all, states, seg, bounds, rates, heads, hd)
-    dn1_sum = product_scatter([(dz, full_attn, 1)])
-    grad_attn = dot(after(n1_all, dn1_sum.term), dz, 0, 0).astype(LOW)
-    grad_out = dot(after(o, grad_attn), dh_all, 0, 0).astype(LOW)
-    dn1 = dn1_sum.done(grad_out)
+    dn1, share_down, share_out, loss, got_first, got_second, got_attn = back_all(
+        shape, heads, hd, rates, bounds, seg, z, a, dh_all, ra_all, mean_all, states, full_out,
+        full_attn, n1_all, spread(jnp.sum(keep * error * error)),
+        (grad_down, grad_first, grad_second),
+    )
     input_grad = dh + r1 * (dn1 - n1 * jnp.mean(dn1 * n1, axis=-1, keepdims=True))
-    loss_own = after(jnp.sum(keep * error * error).reshape(1, 1), dhb)
-    loss = move.sum_all(loss_own) / (width * count)
-
-    share_down, share_first, share_second, share_out, *share_attn = scatter_all(
-        shape, heads, hd, (grad_down, grad_first, grad_second, grad_attn, grad_out)
+    loss = loss[0, 0] / (width * count)
+    share_first, share_second, *share_attn = unpack_columns(
+        got_attn, got_first, got_second, heads, hd
     )
 
     return (

time: 1420 us -> 1260 us (0.89)
  starting transfers between devices: 113 us -> 12.3 us
  matrix products: 266 us -> 205 us
  waiting for transfers between devices: 223 us -> 253 us
    ppermute x12 -> x2, starting transfers between devices: 99.3 us -> 0.68 us  [sum_axis(): v = v + lax.ppermute(v, axis, [(i, i ^ step) for i in range(size)])]
    dot_general x20 -> x15, matrix products: 266 us -> 205 us  [dot(): lax.dot_general(left, right, (((left_dim,), (right_dim,)), ((), ())), pre...]
    ppermute x8 -> x7, waiting for transfers between devices: 163 us -> 206 us  [to_chip(): return lax.ppermute(v, 'seq', self.chip_perm)]
    ppermute x12 -> x2, waiting for transfers between devices: 59.1 us -> 45.6 us  [sum_axis(): v = v + lax.ppermute(v, axis, [(i, i ^ step) for i in range(size)])]
  transfers between devices with their start and end apart: 36 -> 23, of which waited for: 17 -> 8; matrix products, arithmetic and copies ran while one was open for 8% -> 8% of each run, Pallas kernels for 22% -> 0%
where the time goes in v3:
time: 1260 us
  Pallas kernels  672 us (53%)
  waiting for transfers between devices  253 us (20%)
  matrix products  205 us (16%)
  other arithmetic  58.1 us (5%)
  local copies, waits for them, and re-layouts  51.9 us (4%)
    pallas_call x1, Pallas kernels, gather_all(): pl.pallas_call(functools.partial(gather_kernel, shape), in_specs=[HBM] *...  327 us
    pallas_call x1, Pallas kernels, back_all(): pl.pallas_call(functools.partial(back_kernel, shape, heads, hd), in_specs...  321 us
    ppermute x7, waiting for transfers between devices, to_chip(): return lax.ppermute(v, 'seq', self.chip_perm)  206 us
    dot_general x15, matrix products, dot(): lax.dot_general(left, right, (((left_dim,), (right_dim,)), ((), ())), pre...  205 us
    ppermute x2, waiting for transfers between devices, sum_axis(): v = v + lax.ppermute(v, axis, [(i, i ^ step) for i in range(size)])  45.6 us
  transfers between devices with their start and end apart: 23, of which 8 were waited for; matrix products, arithmetic and copies ran while one was open for 8% of the time, Pallas kernels for 0%

profile of v3, /device:TPU:0, one launch (start us, length us, event | category | flops | bytes accessed | tf_op | source)
XLA Modules:
  0.0 1256.3 jit_solution(3631914586056544895)
XLA Ops:
  0.7 2.1 fusion.9
  3.4 3.3 fusion.2.n1_ref
  7.3 3.2 pack_columns.1
  11.7 327.0 %gather_all.1 = (bf16[4,64,2048]{2,1,0:T(8,128)(2,1)}, bf16[4,64,1408]{2,1,0:T(8,128)(2,1)}, bf16[4,64,1408]{2,1,0:T(8,128)(2,1)}, bf16[4,4,2,64,2048]{4,3,2,1,0...) custom-call(bf16[4,64,2048]{2,1,0:T(8,128)(2,1)} %get-tuple-element., ...), custom_call_target="tpu_custom_call" | custom-call | tf_op jit(solution)/shard_map/gather_all/pallas_call | solution.py:442
  338.7 2.0 copy.24.segc_ref.segc
  341.6 24.3 %fusion.37.z_ref.z = f32[2048,2048]{1,0:T(8,128)} fusion(bf16[2048,2048]{1,0:T(8,128)(2,1)} %get-tuple-element.49.n1, bf16[2048,2048]{1,0:T(8,128)(2,1)} %bitcast.114), kind=kOutput, calls=%fused_computation.97 | convolution fusion | flops 17179869184 | bytes 33554432 | tf_op jit(solution)/shard_map/dot_general | solution.py:17
  367.0 16.8 %attend.1 = (bf16[2048,512]{1,0:T(8,128)(2,1)}, f32[2048,512]{1,0:T(8,128)}, f32[2048,1]{1,0:T(8,128)}, bf16[8,4,128,128]{3,2,1,0:T(8,128)(2,1)}) custom-call(f32[4]{0:T(128)} %dynamic_slice.65.rate_ref, s32[9]{0:T(128)} %pad_add_fusion.bounds_ref, s32[2048,1]{1,0:T(8,128)} %copy.24.segc_ref.segc, s32[1,2048]{1,0:T(1,128)} %bitcast.136, ...), custom_call_target="tpu_custom_call" | custom-call | flops 1610612736 | bytes 23068672 | tf_op jit(solution)/shard_map/attend/pallas_call | solution.py:84
  383.9 3.6 convolution_convert_fusion.5
  387.5 2.0 copy-done.15
  390.9 3.6 convolution_convert_fusion.6
  398.4 4.4 fusion.15
  406.5 44.4 %collective-permute-done.4 = f32[2048]{0:T(1024)S(1)} collective-permute-done((f32[2048]{0:T(1024)S(1)}, f32[2048]{0:T(1024)S(1)}, u32[]{:S(2)}, u32[]{:S(2)}) %collective-permute-start.4) | collective-permute-done | bytes 8224 | tf_op jit(solution)/shard_map/ppermute | solution.py:899
  451.5 4.3 multiply_reduce_fusion.2
  459.9 45.6 %collective-permute-done.6 = bf16[512,2048]{1,0:T(8,128)(2,1)} collective-permute-done((bf16[512,2048]{1,0:T(8,128)(2,1)S(1)}, bf16[512,2048]{1,0:T(8,128)(2,1)}, u32[]{:S(2)}, u32[]{:S(2)}) %collective-permute-start.6) | collective-permute-done | bytes 2097184 | tf_op jit(solution)/shard_map/ppermute | solution.py:874
  505.5 3.3 constant_dynamic-update-slice_fusion.14
  508.8 3.3 constant_dynamic-update-slice_fusion.13
  512.1 3.1 constant_dynamic-update-slice_fusion.12
  515.2 17.0 %fusion.38 = f32[2048,1408]{1,0:T(8,128)} fusion(bf16[2048,2048]{1,0:T(8,128)(2,1)} %constant_dynamic-update-slice_fusion.12, bf16[2048,1408]{1,0:T(8,128)(2,1)S(1)} %bitcast.149), kind=kOutput, calls=%fused_computation.98 | convolution fusion | flops 11811160064 | bytes 25690112 | tf_op jit(solution)/shard_map/dot_general | solution.py:17
  532.2 19.1 %multiply_convert_fusion.2 = (bf16[2048,1408]{1,0:T(8,128)(2,1)}, bf16[2048,1408]{1,0:T(8,128)(2,1)}) fusion(f32[2048,1408]{1,0:T(8,128)} %fusion.38, bf16[2048,2048]{1,0:T(8,128)(2,1)S(1)} %copy-done.12, bf16[2048,1408]{1,0:T(8,128)(2,1)} %bitcast.153), kind=kOutput, calls=%fused_computation.2 | convolution fusion | flops 11819810816 | bytes 37224448 | tf_op jit(solution)/shard_map/dot_general | solution.py:17
  551.4 10.1 convolution_convert_fusion.3
  562.3 8.7 convolution_convert_fusion.4
  572.7 2.1 fusion.12
  578.3 44.8 %collective-permute-done.10 = bf16[512,2048]{1,0:T(8,128)(2,1)} collective-permute-done((bf16[512,2048]{1,0:T(8,128)(2,1)}, bf16[512,2048]{1,0:T(8,128)(2,1)}, u32[]{:S(2)}, u32[]{:S(2)}) %collective-permute-start.10) | collective-permute-done | bytes 2097184 | tf_op jit(solution)/shard_map/ppermute | solution.py:874
  623.1 6.4 fusion.8
  629.6 2.4 constant_dynamic-update-slice_fusion.11
  633.6 45.9 %collective-permute-done.12 = bf16[512,2048]{1,0:T(8,128)(2,1)S(1)} collective-permute-done((bf16[512,2048]{1,0:T(8,128)(2,1)S(1)}, bf16[512,2048]{1,0:T(8,128)(2,1)S(1)}, u32[]{:S(2)}, u32[]{:S(2)}) %collective-permute-start.12) | collective-permute-done | bytes 2097184 | tf_op jit(solution)/shard_map/ppermute | solution.py:874
  685.2 23.4 %multiply_convert_fusion = (bf16[2048,1408]{1,0:T(8,128)(2,1)}, bf16[2048,1408]{1,0:T(8,128)(2,1)}) fusion(bf16[2048,1408]{1,0:T(8,128)(2,1)} %get-tuple-element.93, f32[2048,1408]{1,0:T(8,128)} %fusion.38, bf16[2048,2048]{1,0:T(8,128)(2,1)} %constant_dynamic-update-slice_fusion.8, bf16[1408,2048]{1,0:T(8,128)(2,1)} %bitcast.160), kind=kOutput, calls=%fused_computation | convolution fusion | flops 11831345152 | bytes 42991616 | tf_op jit(solution)/shard_map/dot_general | solution.py:17
  708.6 11.7 fusion.22
  720.2 11.0 add_convert_fusion.1
  731.2 18.5 %convolution_convert_fusion.2 = bf16[1408,2048]{1,0:T(8,128)(2,1)} fusion(bf16[2048,1408]{1,0:T(8,128)(2,1)} %get-tuple-element.59, bf16[2048,2048]{1,0:T(8,128)(2,1)} %constant_dynamic-update-slice_fusion.8), kind=kOutput, calls=%fused_computation.7 | convolution fusion | flops 11814043648 | bytes 19922944 | tf_op jit(solution)/shard_map/dot_general | solution.py:17
  749.8 10.4 fusion.19
  760.5 10.2 add_convert_fusion
  772.8 2.2 fusion.10
  779.5 4.0 convert_bitcast_fusion
  783.5 39.5 %collective-permute-done.16 = bf16[512,2048]{1,0:T(8,128)(2,1)} collective-permute-done((bf16[512,2048]{1,0:T(8,128)(2,1)}, bf16[512,2048]{1,0:T(8,128)(2,1)}, u32[]{:S(2)}, u32[]{:S(2)}) %collective-permute-start.16) | collective-permute-done | bytes 2097184 | tf_op jit(solution)/shard_map/ppermute | solution.py:874
  822.9 4.3 multiply_reduce_fusion.1
  827.3 6.6 constant_dynamic-update-slice_fusion.7
  833.9 4.4 multiply_reduce_fusion
  840.6 17.2 %convolution_convert_fusion.1 = bf16[2048,1408]{1,0:T(8,128)(2,1)} fusion(bf16[2048,2048]{1,0:T(8,128)(2,1)S(1)} %bitcast.117, bf16[2048,1408]{1,0:T(8,128)(2,1)} %get-tuple-element.60), kind=kOutput, calls=%fused_computation.6 | convolution fusion | flops 11814043648 | bytes 19922944 | tf_op jit(solution)/shard_map/dot_general | solution.py:17
  857.8 30.2 %collective-permute-done.18 = bf16[512,2048]{1,0:T(8,128)(2,1)} collective-permute-done((bf16[512,2048]{1,0:T(8,128)(2,1)S(1)}, bf16[512,2048]{1,0:T(8,128)(2,1)}, u32[]{:S(2)}, u32[]{:S(2)}) %collective-permute-start.18) | collective-permute-done | bytes 2097184 | tf_op jit(solution)/shard_map/ppermute | solution.py:874
  888.1 15.9 %convolution_convert_fusion = bf16[2048,1408]{1,0:T(8,128)(2,1)} fusion(bf16[2048,2048]{1,0:T(8,128)(2,1)S(1)} %bitcast.117, bf16[2048,1408]{1,0:T(8,128)(2,1)S(1)} %bitcast.162), kind=kOutput, calls=%fused_computation.5 | convolution fusion | flops 11814043648 | bytes 19922944 | tf_op jit(solution)/shard_map/dot_general | solution.py:17
  906.9 3.5 constant_dynamic-update-slice_fusion.6
  910.4 3.2 constant_dynamic-update-slice_fusion.5
  913.6 3.2 constant_dynamic-update-slice_fusion.4.dh
  918.0 320.6 %back_all.1 = (f32[512,2048]{1,0:T(8,128)}, f32[176,2048]{1,0:T(8,128)}, f32[64,2048]{1,0:T(8,128)}, f32[8,128]{1,0:T(8,128)}, bf16[4,64,1408]{2,1,0:T(8,128)(2,...) custom-call(f32[4]{0:T(128)} %dynamic_slice.65.rate_ref, ...), custom_call_target="tpu_custom_call" | custom-call | tf_op jit(solution)/shard_map/back_all/pallas_call | solution.py:826
  1238.7 3.0 fusion.3
  1242.9 5.2 fusion.7
  1248.8 4.0 unpack_columns.1
  (175 shorter events, 46.4 us)
Async XLA Ops:
  341.6 24.3 %copy-start.31 = (f32[16]{0:T(128)S(1)}, f32[16]{0:T(128)}, u32[]{:S(2)}) copy-start(f32[16]{0:T(128)} %param.17) | copy-start | bytes 196
  367.0 16.9 %copy-start.17 = (bf16[1,4,2,64,2048]{4,3,2,1,0:T(8,128)(2,1)S(1)}, bf16[1,4,2,64,2048]{4,3,2,1,0:T(8,128)(2,1)}, u32[]{:S(2)}) copy-start(bf16[1,4,2,64,2048]{4,3,2,1,0:T(8,128)(2,1)} %get-tuple-element.52) | copy-start | bytes 6291460
  390.9 7.5 collective-permute-start.1
  397.9 53.1 %collective-permute-start = (bf16[512,2048]{1,0:T(8,128)(2,1)}, bf16[512,2048]{1,0:T(8,128)(2,1)}, u32[]{:S(2)}, u32[]{:S(2)}) collective-permute-start(bf16[512,2048]{1,0:T(8,128)(2,1)} %dynamic-slice_bitcast_fusion.5), channel_id=1, source_target_pairs={{0,8},{8,0},{16,24},{24,16},{1,9},{9,1},{17,25},{25,17},{2,10},{10... | collective-permute-start | bytes 6291464 | tf_op jit(solution)/shard_map/ppermute | solution.py:871
  402.9 48.6 %collective-permute-start.2 = (bf16[512,2048]{1,0:T(8,128)(2,1)}, bf16[512,2048]{1,0:T(8,128)(2,1)}, u32[]{:S(2)}, u32[]{:S(2)}) collective-permute-start(bf16[512,2048]{1,0:T(8,128)(2,1)} %fusion.15), channel_id=1, source_target_pairs={{0,16},{8,24},{16,0},{24,8},{1,17},{9,25},{17,1},{25,9},{2,18},{10... | collective-permute-start | bytes 6291464 | tf_op jit(solution)/shard_map/ppermute | solution.py:874
  404.6 1.2 collective-permute-start.3
  405.9 45.0 %collective-permute-start.4 = (f32[2048]{0:T(1024)S(1)}, f32[2048]{0:T(1024)S(1)}, u32[]{:S(2)}, u32[]{:S(2)}) collective-permute-start(f32[2048]{0:T(1024)S(1)} %add.198), channel_id=1, source_target_pairs={{0,16},{8,24},{16,0},{24,8},{1,17},{9,25},{17,1},{25,9},{2,18},{10... | collective-permute-start | bytes 24584 | tf_op jit(solution)/shard_map/ppermute | solution.py:899
  406.5 45.0 %copy-start.4 = (bf16[1,512,2048]{2,1,0:T(8,128)(2,1)S(1)}, bf16[1,512,2048]{2,1,0:T(8,128)(2,1)}, u32[]{:S(2)}) copy-start(bf16[1,512,2048]{2,1,0:T(8,128)(2,1)} %param.13) | copy-start | bytes 6291460
  458.5 47.0 %collective-permute-start.6 = (bf16[512,2048]{1,0:T(8,128)(2,1)S(1)}, bf16[512,2048]{1,0:T(8,128)(2,1)}, u32[]{:S(2)}, u32[]{:S(2)}) collective-permute-start(bf16[512,2048]{1,0:T(8,128)(2,1)S(1)} %get-tuple-element.87), channel_id=1, source_target_pairs={{0,16},{8,24},{16,0},{24,8},{1,17},{9,25},{17,1},{25,9},{2,18},{10... | collective-permute-start | bytes 6291464 | tf_op jit(solution)/shard_map/ppermute | solution.py:874
  459.9 45.6 %collective-permute-start.5 = (bf16[512,2048]{1,0:T(8,128)(2,1)S(1)}, bf16[512,2048]{1,0:T(8,128)(2,1)}, u32[]{:S(2)}, u32[]{:S(2)}) collective-permute-start(bf16[512,2048]{1,0:T(8,128)(2,1)S(1)} %get-tuple-element.87), channel_id=1, source_target_pairs={{0,8},{8,0},{16,24},{24,16},{1,9},{9,1},{17,25},{25,17},{2,10},{10... | collective-permute-start | bytes 6291464 | tf_op jit(solution)/shard_map/ppermute | solution.py:871
  505.5 6.6 collective-permute-start.7
  505.5 9.7 slice-start.2
  515.2 17.0 %copy-start.12 = (bf16[2048,2048]{1,0:T(8,128)(2,1)S(1)}, bf16[2048,2048]{1,0:T(8,128)(2,1)}, u32[]{:S(2)}) copy-start(bf16[2048,2048]{1,0:T(8,128)(2,1)} %constant_dynamic-update-slice_fusion.12) | copy-start | bytes 25165828
  551.4 10.9 copy-start.32
  561.7 11.0 collective-permute-start.9
  572.6 5.7 collective-permute-start.8
  574.8 48.3 %collective-permute-start.10 = (bf16[512,2048]{1,0:T(8,128)(2,1)}, bf16[512,2048]{1,0:T(8,128)(2,1)}, u32[]{:S(2)}, u32[]{:S(2)}) collective-permute-start(bf16[512,2048]{1,0:T(8,128)(2,1)} %fusion.12), channel_id=1, source_target_pairs={{0,16},{8,24},{16,0},{24,8},{1,17},{9,25},{17,1},{25,9},{2,18},{10... | collective-permute-start | bytes 6291464 | tf_op jit(solution)/shard_map/ppermute | solution.py:874
  576.3 46.9 %copy-start.6 = (bf16[1,512,2048]{2,1,0:T(8,128)(2,1)S(1)}, bf16[1,512,2048]{2,1,0:T(8,128)(2,1)}, u32[]{:S(2)}) copy-start(bf16[1,512,2048]{2,1,0:T(8,128)(2,1)} %param.14) | copy-start | bytes 6291460
  632.2 47.4 %collective-permute-start.12 = (bf16[512,2048]{1,0:T(8,128)(2,1)S(1)}, bf16[512,2048]{1,0:T(8,128)(2,1)S(1)}, u32[]{:S(2)}, u32[]{:S(2)}) collective-permute-start(bf16[512,2048]{1,0:T(8,128)(2,1)S(1)} %get-tuple-element.85), channel_id=1, source_target_pairs={{0,16},{8,24},{16,0},{24,8},{1,17},{9,25},{17,1},{25,9},{2,18},{10... | collective-permute-start | bytes 6291464 | tf_op jit(solution)/shard_map/ppermute | solution.py:874
  633.6 45.9 %collective-permute-start.11 = (bf16[512,2048]{1,0:T(8,128)(2,1)S(1)}, bf16[512,2048]{1,0:T(8,128)(2,1)S(1)}, u32[]{:S(2)}, u32[]{:S(2)}) collective-permute-start(bf16[512,2048]{1,0:T(8,128)(2,1)S(1)} %get-tuple-element.85), channel_id=1, source_target_pairs={{0,8},{8,0},{16,24},{24,16},{1,9},{9,1},{17,25},{25,17},{2,10},{10... | collective-permute-start | bytes 6291464 | tf_op jit(solution)/shard_map/ppermute | solution.py:871
  679.5 4.2 collective-permute-start.13
  720.2 29.5 %slice-start.6 = ((s8[5767168]{0:T(1024)(128)(4,1)}), s8[1572864]{0:T(1024)(128)(4,1)S(1)}, s32[]{:S(2)}) async-start(s8[5767168]{0:T(1024)(128)(4,1)} %bitcast.155), calls=%async_computation.6 | async-start | bytes 3145728
  720.2 40.3 %slice-start.4 = ((s8[5767168]{0:T(1024)(128)(4,1)}), s8[4194304]{0:T(1024)(128)(4,1)S(1)}, s32[]{:S(2)}) async-start(s8[5767168]{0:T(1024)(128)(4,1)} %bitcast.150), calls=%async_computation.4 | async-start | bytes 8388608
  731.2 18.6 %slice-start.7 = ((s8[5767168]{0:T(1024)(128)(4,1)}), s8[4194304]{0:T(1024)(128)(4,1)S(1)}, s32[]{:S(2)}) async-start(s8[5767168]{0:T(1024)(128)(4,1)} %bitcast.155), calls=%async_computation.7 | async-start | bytes 8388608
  731.2 29.3 %slice-start.5 = ((s8[5767168]{0:T(1024)(128)(4,1)}), s8[1572864]{0:T(1024)(128)(4,1)S(1)}, s32[]{:S(2)}) async-start(s8[5767168]{0:T(1024)(128)(4,1)} %bitcast.150), calls=%async_computation.5 | async-start | bytes 3145728
  760.4 12.4 collective-permute-start.15
  772.4 11.1 collective-permute-start.14
  775.0 47.9 %collective-permute-start.16 = (bf16[512,2048]{1,0:T(8,128)(2,1)}, bf16[512,2048]{1,0:T(8,128)(2,1)}, u32[]{:S(2)}, u32[]{:S(2)}) collective-permute-start(bf16[512,2048]{1,0:T(8,128)(2,1)} %fusion.10), channel_id=1, source_target_pairs={{0,16},{8,24},{16,0},{24,8},{1,17},{9,25},{17,1},{25,9},{2,18},{10... | collective-permute-start | bytes 6291464 | tf_op jit(solution)/shard_map/ppermute | solution.py:874
  776.4 46.5 %copy-start.26 = (f32[512]{0:T(512)S(1)}, f32[512]{0:T(512)}, u32[]{:S(2)}) copy-start(f32[512]{0:T(512)} %copy-done.25) | copy-start | bytes 6148
  779.5 43.5 %copy-start.1 = (f32[512,2048]{1,0:T(8,128)S(1)}, f32[512,2048]{1,0:T(8,128)}, u32[]{:S(2)}) copy-start(f32[512,2048]{1,0:T(8,128)} %copy-done) | copy-start | bytes 12582916
  783.5 43.8 %copy-start.3 = (f32[512,2048]{1,0:T(8,128)S(1)}, f32[512,2048]{1,0:T(8,128)}, u32[]{:S(2)}) copy-start(f32[512,2048]{1,0:T(8,128)} %copy-done.2) | copy-start | bytes 12582916
  783.5 43.8 %copy-start.11 = (bf16[1024,2048]{1,0:T(8,128)(2,1)S(1)}, bf16[1024,2048]{1,0:T(8,128)(2,1)}, u32[]{:S(2)}) copy-start(bf16[1024,2048]{1,0:T(8,128)(2,1)} %copy-done.10) | copy-start | bytes 12582916
  822.9 17.7 %slice-start = ((s8[8388608]{0:T(1024)(128)(4,1)}), s8[4194304]{0:T(1024)(128)(4,1)S(1)}, s32[]{:S(2)}) async-start(s8[8388608]{0:T(1024)(128)(4,1)} %bitcast.116), calls=%async_computation | async-start | bytes 8388608
  827.2 6.6 copy-start.9
  827.3 6.6 copy-start.28
  827.3 13.4 %slice-start.1 = ((s8[8388608]{0:T(1024)(128)(4,1)}), s8[4194304]{0:T(1024)(128)(4,1)S(1)}, s32[]{:S(2)}) async-start(s8[8388608]{0:T(1024)(128)(4,1)} %bitcast.116), calls=%async_computation.1 | async-start | bytes 8388608
  838.3 49.8 %slice-start.8 = ((s8[5767168]{0:T(1024)(128)(4,1)}), s8[4194304]{0:T(1024)(128)(4,1)S(1)}, s32[]{:S(2)}) async-start(s8[5767168]{0:T(1024)(128)(4,1)} %bitcast.161), calls=%async_computation.8 | async-start | bytes 8388608
  838.3 49.8 %slice-start.9 = ((s8[5767168]{0:T(1024)(128)(4,1)}), s8[1572864]{0:T(1024)(128)(4,1)S(1)}, s32[]{:S(2)}) async-start(s8[5767168]{0:T(1024)(128)(4,1)} %bitcast.161), calls=%async_computation.9 | async-start | bytes 3145728
  838.3 65.9 %collective-permute-start.20 = (f32[512]{0:T(512)S(1)}, f32[512]{0:T(512)S(1)}, u32[]{:S(2)}, u32[]{:S(2)}) collective-permute-start(f32[512]{0:T(512)S(1)} %broadcast_multiply_fusion.2), channel_id=1, source_target_pairs={{0,8},{8,0},{16,24},{24,16},{1,9},{9,1},{17,25},{25,17},{2,10},{10... | collective-permute-start | bytes 6152 | tf_op jit(solution)/shard_map/ppermute | solution.py:871
  838.4 66.0 %collective-permute-start.21 = (f32[512]{0:T(512)S(1)}, f32[512]{0:T(512)S(1)}, u32[]{:S(2)}, u32[]{:S(2)}) collective-permute-start(f32[512]{0:T(512)S(1)} %broadcast_multiply_fusion.2), channel_id=1, source_target_pairs={{0,16},{8,24},{16,0},{24,8},{1,17},{9,25},{17,1},{25,9},{2,18},{10... | collective-permute-start | bytes 6152 | tf_op jit(solution)/shard_map/ppermute | solution.py:874
  839.9 67.0 %collective-permute-start.17 = (bf16[512,2048]{1,0:T(8,128)(2,1)S(1)}, bf16[512,2048]{1,0:T(8,128)(2,1)}, u32[]{:S(2)}, u32[]{:S(2)}) collective-permute-start(bf16[512,2048]{1,0:T(8,128)(2,1)S(1)} %copy-done.13), channel_id=1, source_target_pairs={{0,8},{8,0},{16,24},{24,16},{1,9},{9,1},{17,25},{25,17},{2,10},{10... | collective-permute-start | bytes 6291464 | tf_op jit(solution)/shard_map/ppermute | solution.py:871
  840.1 48.0 %collective-permute-start.18 = (bf16[512,2048]{1,0:T(8,128)(2,1)S(1)}, bf16[512,2048]{1,0:T(8,128)(2,1)}, u32[]{:S(2)}, u32[]{:S(2)}) collective-permute-start(bf16[512,2048]{1,0:T(8,128)(2,1)S(1)} %copy-done.13), channel_id=1, source_target_pairs={{0,16},{8,24},{16,0},{24,8},{1,17},{9,25},{17,1},{25,9},{2,18},{10... | collective-permute-start | bytes 6291464 | tf_op jit(solution)/shard_map/ppermute | solution.py:874
  888.1 25.5 %collective-permute-start.19 = (bf16[512,2048]{1,0:T(8,128)(2,1)}, bf16[512,2048]{1,0:T(8,128)(2,1)}, u32[]{:S(2)}, u32[]{:S(2)}) collective-permute-start(bf16[512,2048]{1,0:T(8,128)(2,1)} %collective-permute-done.18), channel_id=1, source_target_pairs={{0,8},{8,0},{16,24},{24,16},{1,9},{9,1},{17,25},{25,17},{2,10},{10... | collective-permute-start | bytes 6291464 | tf_op jit(solution)/shard_map/ppermute | solution.py:871
  905.2 1.5 collective-permute-start.22
  906.9 6.7 copy-start.14
  918.0 320.7 %copy-start.5 = (bf16[1,512,2048]{2,1,0:T(8,128)(2,1)S(1)}, bf16[1,512,2048]{2,1,0:T(8,128)(2,1)}, u32[]{:S(2)}) copy-start(bf16[1,512,2048]{2,1,0:T(8,128)(2,1)} %param.13) | copy-start | bytes 6291460
  918.0 320.7 %copy-start.24 = (f32[512]{0:T(512)S(1)}, f32[512]{0:T(512)}, u32[]{:S(2)}) copy-start(f32[512]{0:T(512)} %copy-done.23) | copy-start | bytes 6148
  1242.9 10.0 copy-start.20
  (18 other events, 67.3 us)

commit v4 on v3

--- a/solution.py
+++ b/solution.py
@@ -42,19 +42,19 @@
     return place_col, place_row
 
 
-def attend_kernel(
-    heads, hd, rate_ref, bounds_ref, segc_ref, segr_ref, z_ref, au_ref, a_ref, ss_ref, st_ref, state
-):
-    n = pl.program_id(0)
+def attend(heads, hd, n, rate_ref, seg_before, seg_row, z_ref, au_ref, a_ref, ss_ref, st_ref, state):
     chunk = z_ref.shape[0]
-
-    @pl.when(n == 0)
-    def _():
-        state[...] = jnp.zeros_like(state)
-
-    inner, entry_on, tail_on, carry = masks(bounds_ref, segc_ref[...], segr_ref[...], n, chunk)
+    seg_col = jnp.transpose(seg_row)[:, :1]
+    before = jnp.where(n > 0, seg_before[:1, chunk - 1 :], -1.0)
+    last = seg_row[:1, chunk - 1 :]
+    row = lax.broadcasted_iota(jnp.int32, (chunk, chunk), 0)
+    col = lax.broadcasted_iota(jnp.int32, (chunk, chunk), 1)
+    inner = (seg_col == seg_row[:1]) & (row >= col)
+    entry_on, tail_on = seg_col == before, seg_col == last
+    carry = jnp.where(before == last, 1.0, 0.0)
     place_col, place_row = places(chunk)
-    total = jnp.zeros((chunk, 1), WIDE)
+    ones = jnp.ones((8, hd), WIDE)
+    squares = jnp.zeros((8, chunk), WIDE)
     for h in range(heads):
         rate = rate_ref[h]
         base = h * 4 * hd
@@ -73,46 +73,14 @@
         state[h] = carry * jnp.exp(jnp.full((1, 1), -rate * chunk, WIDE)) * held + dot(kt, v, 0, 0)
         a_ref[:, h * hd : (h + 1) * hd] = a
         au_ref[:, h * hd : (h + 1) * hd] = (a * u).astype(LOW)
-        total = total + jnp.sum(a * a, axis=1, keepdims=True)
-    ss_ref[...] = total
-
-
-def attend(z, seg, bounds, rates, heads, hd):
-    length = z.shape[0]
-    count = length // CHUNK
-    block = lambda width: pl.BlockSpec((CHUNK, width), lambda n, *_: (n, 0))
-    return pl.pallas_call(
-        functools.partial(attend_kernel, heads, hd),
-        grid_spec=pltpu.PrefetchScalarGridSpec(
-            num_scalar_prefetch=2,
-            grid=(count,),
-            in_specs=[
-                block(1),
-                pl.BlockSpec((1, CHUNK), lambda n, *_: (0, n)),
-                block(heads * 4 * hd),
-            ],
-            out_specs=[
-                block(heads * hd),
-                block(heads * hd),
-                block(1),
-                pl.BlockSpec((1, heads, hd, hd), lambda n, *_: (n, 0, 0, 0)),
-            ],
-            scratch_shapes=[pltpu.VMEM((heads, hd, hd), WIDE)],
-        ),
-        out_shape=[
-            jax.ShapeDtypeStruct((length, heads * hd), LOW),
-            jax.ShapeDtypeStruct((length, heads * hd), WIDE),
-            jax.ShapeDtypeStruct((length, 1), WIDE),
-            jax.ShapeDtypeStruct((count, heads, hd, hd), LOW),
-        ],
-        compiler_params=pltpu.CompilerParams(vmem_limit_bytes=VMEM_BYTES),
-        cost_estimate=pl.CostEstimate(
-            flops=length * heads * hd * CHUNK * 6,
-            bytes_accessed=length * heads * hd * 22,
-            transcendentals=length * heads * hd * 4,
-        ),
-        name="attend",
-    )(rates, bounds, seg.reshape(length, 1), seg.reshape(1, length), z)
+        squares = squares + lax.dot_general(
+            ones,
+            a * a,
+            (((1,), (1,)), ((), ())),
+            precision=lax.Precision.HIGHEST,
+            preferred_element_type=WIDE,
+        )
+    ss_ref[...] = squares
 
 
 def slope(z):
@@ -320,6 +288,37 @@
             copy.wait()
 
 
+class WideRing:
+    def __init__(self, net, piece, full):
+        self.net, self.full = net, full
+        self.copies = [net.copy(piece, full.at[:, net.o, net.i])]
+        self.side = [
+            net.send(piece, full.at[:, net.o, net.i], net.at_inner(j)) for j in range(1, net.inner)
+        ]
+        self.at = 0
+        self.coming = None
+
+    def step(self):
+        net, full = self.net, self.full
+        if self.at >= net.outer:
+            return
+        if self.at == 0:
+            for copy in self.side:
+                copy.wait_recv()
+            for copy in self.copies:
+                copy.wait()
+        else:
+            self.coming.wait_recv()
+        spot = full.at[:, lax.rem(net.o + net.outer - self.at, net.outer)]
+        if self.at < net.outer - 1:
+            self.coming = net.send(spot, spot, net.at_outer(1))
+        self.at += 1
+
+    def done(self):
+        while self.at < self.net.outer:
+            self.step()
+
+
 def swap(net, blocks, got):
     own = net.copy(blocks.at[net.s], got.at[net.s])
     coming = [
@@ -362,34 +361,20 @@
 
 
 def gather_kernel(
-    shape,
-    attn_ref,
-    first_ref,
-    second_ref,
-    out_ref,
-    down_ref,
-    n1_ref,
-    seg_ref,
-    count_ref,
-    attn_mid,
-    first_mid,
-    second_mid,
-    full_attn,
-    full_first,
-    full_second,
-    full_out,
-    full_down,
-    n1_all,
-    seg_all,
-    count_all,
-    seq_buf,
-    in_buf,
-    out_buf,
-    send_sem,
-    recv_sem,
-    local_sem,
+    shape, heads, hd,
+    rate_ref, attn_ref, first_ref, second_ref, out_ref, down_ref, n1_ref, seg_ref, count_ref, x_ref,
+    attn_mid, first_mid, second_mid,
+    full_attn, full_first, full_second, full_out, full_down,
+    n1_all, z_all, a_all, states, mixed_ref, hsum_ref, n2_own, n2_all, core_in, chip_in,
+    seg_all, count_all, ss_all,
+    w_attn, w_out, au_all, state, stage, term, wide_tile, hsum_tile, x_tile, n2_tile, ss_in,
+    seq_buf, in_buf, out_buf, send_sem, recv_sem, local_sem,
 ):
     net = Net(shape, send_sem, recv_sem, local_sem)
+    length, width = n1_all.shape
+    cols = z_all.shape[1]
+    own_rows = x_ref.shape[0]
+    wide = min(512, width)
     net.barrier()
     count = Total(net, count_ref, seq_buf, in_buf, out_buf)
     attn_swap = swap(net, attn_ref, attn_mid)
@@ -400,63 +385,275 @@
     rows = Rows(net, n1_ref, n1_all)
     arrive(attn_swap)
     count.step()
-    rings = [Ring(net, attn_mid, full_attn)]
-    rings.append(Ring(net, out_ref, full_out))
+    ring_attn = Ring(net, attn_mid, full_attn)
+    ring_out = Ring(net, out_ref, full_out)
     for _ in range(net.outer):
-        rings[0].step()
+        ring_attn.step()
+        ring_out.step()
         count.step()
     arrive(first_swap)
     arrive(second_swap)
+    ring_first = Ring(net, first_mid, full_first)
+    ring_second = Ring(net, second_mid, full_second)
+    ring_first.step()
+    ring_second.step()
+    ring_down = WideRing(net, down_ref, full_down)
     rows.turn()
-    rings.append(Ring(net, first_mid, full_first))
-    rings.append(Ring(net, second_mid, full_second))
-    rings.append(Ring(net, down_ref, full_down))
-    for ring in rings[1:]:
-        for _ in range(net.outer):
-            ring.step()
-    count_all[...] = count.done()
-    for ring in rings:
-        ring.done()
-    rows.done()
+    queue = [ring_first, ring_second, ring_down] * (net.outer - 1) + [ring_down]
+
+    def pump(times=1):
+        for _ in range(min(times, len(queue))):
+            queue.pop(0).step()
+
     seg_own.wait()
     for copy in segs:
         copy.wait_recv()
+    ring_attn.done()
+    load_attn = net.copy(full_attn, w_attn)
+    rows.done()
+    ring_out.done()
+    load_out = net.copy(full_out, w_out)
+    load_attn.wait()
+    load_out.wait()
+
+    state[...] = jnp.zeros_like(state)
+    per = own_rows // CHUNK
+
+    def seg_of(n):
+        at = pl.ds(pl.multiple_of(n % per * CHUNK, CHUNK), CHUNK)
+        return jnp.broadcast_to(seg_all[n // per, :, at].astype(WIDE), (8, CHUNK))
+
+    def chunks(low, steps):
+        def body(n1_chunk, z_ref, a_ref, st_ref):
+            n = low + pl.program_id(0)
+
+            def project(j, _):
+                at = pl.ds(pl.multiple_of(j * wide, wide), wide)
+                weight = w_attn[:, :, :, :, at].reshape(width, wide)
+                z_ref[:, at] = dot(n1_chunk[...], weight)
+                return 0
+
+            lax.fori_loop(0, cols // wide, project, 0)
+            au_rows = au_all.at[pl.ds(pl.multiple_of(n * CHUNK, CHUNK), CHUNK)]
+            attend(
+                heads, hd, n, rate_ref, seg_of(jnp.maximum(n - 1, 0)), seg_of(n), z_ref, au_rows,
+                a_ref, ss_all.at[n], st_ref, state,
+            )
+
+        block = lambda n: pl.BlockSpec((CHUNK, n), lambda i: (low + i, 0))
+        pltpu.emit_pipeline(
+            body,
+            grid=(steps,),
+            in_specs=[block(width)],
+            out_specs=[
+                block(cols),
+                block(heads * hd),
+                pl.BlockSpec((1, heads, hd, hd), lambda i: (low + i, 0, 0, 0)),
+            ],
+        )(n1_all, z_all, a_all, states)
+
+    total = length // CHUNK
+    half = total // 2
+    chunks(0, half)
+    pump()
+    chunks(half, total - half)
+    near_ss = [net.send(ss_all, ss_in.at[net.s], net.at_seq(s)) for _, _, s in net.seq_peers()]
+    pump()
+
+    used = [None, None]
+    turns = [0]
+
+    def product(row, each):
+        x = au_all[pl.ds(pl.multiple_of(row, CHUNK), CHUNK)]
+
+        def one(j, _):
+            at = pl.ds(pl.multiple_of(j * wide, wide), wide)
+            weight = w_out[:, :, :, :, at].reshape(heads * hd, wide)
+            each(at, dot(x, weight))
+            return 0
+
+        lax.fori_loop(0, width // wide, one, 0)
+
+    def slot():
+        i = turns[0] % 2
+        turns[0] += 1
+        if used[i] is not None:
+            net.left(used[i])
+        return i
+
+    def row_of(chip, core, t):
+        return (chip * 2 + core) * own_rows + t * CHUNK
+
+    near = {}
+    far = []
+
+    def give(dx):
+        chip = lax.rem(net.chip + dx, net.chips)
+        for t in range(per):
+            i = slot()
+
+            def store(at, part, i=i):
+                stage[i, :, at] = part.astype(LOW)
+
+            product(row_of(chip, 1 - net.core, t), store)
+            spot = core_in.at[dx, pl.ds(t * CHUNK, CHUNK)]
+            used[i] = near[dx, t] = net.send(
+                stage.at[i], spot, net.at_seq(net.chip * 2 + 1 - net.core)
+            )
+
+    def keep(dx, finish=None):
+        chip = lax.rem(net.chip + dx, net.chips)
+        for t in range(per):
+            span = pl.ds(t * CHUNK, CHUNK)
+            near[dx, t].wait_recv()
+            loads = [net.copy(core_in.at[dx, span], term.at[0])]
+            if dx == 0:
+                loads.append(net.copy(x_ref.at[span], x_tile))
+                for j, copies in enumerate(far):
+                    copies[t].wait_recv()
+                    loads.append(net.copy(chip_in.at[j, span], term.at[j + 1]))
+            else:
+                i = slot()
+            for load in loads:
+                load.wait()
+
+            def store(at, part):
+                add = part + term[0, :, at].astype(WIDE)
+                if dx == 0:
+                    for j in range(len(far)):
+                        add = add + term[j + 1, :, at].astype(WIDE)
+                    wide_tile[:, at] = add
+                else:
+                    stage[i, :, at] = add.astype(LOW)
+
+            product(row_of(chip, net.core, t), store)
+            if dx == 0:
+                finish(t, span)
+            else:
+                used[i] = net.send(
+                    stage.at[i], chip_in.at[dx - 1, span], net.at_seq(chip * 2 + net.core)
+                )
+                far[dx - 1].append(used[i])
+
+    def finish(t, span):
+        at = net.s * per + t
+        squares = ss_in[0, at]
+        for j in range(1, net.seq):
+            squares = squares + ss_in[j, at]
+        ra = lax.rsqrt(jnp.transpose(squares)[:, :1] / width + 1e-6)
+
+        def add(j, squares):
+            at = pl.ds(pl.multiple_of(j * wide, wide), wide)
+            mixed = wide_tile[:, at] * ra
+            wide_tile[:, at] = mixed
+            hsum = x_tile[:, at].astype(WIDE) + mixed
+            hsum_tile[:, at] = hsum
+            return squares + jnp.sum(hsum * hsum, axis=1, keepdims=True)
+
+        squares = lax.fori_loop(0, width // wide, add, jnp.zeros((CHUNK, 1), WIDE))
+        r2 = lax.rsqrt(squares / width + 1e-6)
+
+        def scale(j, _):
+            at = pl.ds(pl.multiple_of(j * wide, wide), wide)
+            n2_tile[:, at] = (hsum_tile[:, at] * r2).astype(LOW)
+            return 0
+
+        lax.fori_loop(0, width // wide, scale, 0)
+        outs = [
+            net.copy(wide_tile, mixed_ref.at[span]),
+            net.copy(hsum_tile, hsum_ref.at[span]),
+            net.copy(n2_tile, n2_own.at[span]),
+        ]
+        for out in outs:
+            out.wait()
+
+    for dx in range(1, net.chips):
+        far.append([])
+        give(dx)
+        keep(dx)
+    pump()
+    give(0)
+    pump(2)
+    for copy in near_ss:
+        copy.wait_recv()
+    for copy in near_ss:
+        net.left(copy)
+    ss_in[net.s] = ss_all[...]
+    keep(0, finish)
+    rows = Rows(net, n2_own, n2_all)
+    pump(3)
+    rows.turn()
+    pump(len(queue))
+    count_all[...] = count.done()
+    for ring in (ring_first, ring_second, ring_down):
+        ring.done()
+    rows.done()
+    total_ss = ss_in[0]
+    for j in range(1, net.seq):
+        total_ss = total_ss + ss_in[j]
+    ss_all[...] = total_ss
     net.finish()
 
 
 HBM = pl.BlockSpec(memory_space=pl.ANY)
 
 
-def gather_all(shape, attn, first, second, w_out, w_down, n1, seg, count):
+def gather_all(shape, heads, hd, rates, attn, first, second, w_out, w_down, n1, seg, count, x):
     seq, fsdp, inner = shape
     outer = fsdp // inner
+    chips = seq // 2
+    own_rows, width = n1.shape
+    length = own_rows * seq
+    cols = attn.shape[2]
+    chunks = length // CHUNK
     like = lambda v, lead: jax.ShapeDtypeStruct(lead + v.shape[-2:], v.dtype)
     ring = lambda v: like(v, (v.shape[0], outer, inner))
+    low = lambda *dims: jax.ShapeDtypeStruct(dims, LOW)
+    wide = lambda *dims: jax.ShapeDtypeStruct(dims, WIDE)
     outs = [like(v, (seq,)) for v in (attn, first, second)]
     outs += [ring(v) for v in (attn, first, second, w_out, w_down)]
-    outs.append(jax.ShapeDtypeStruct((seq * n1.shape[0], n1.shape[1]), n1.dtype))
-    outs.append(jax.ShapeDtypeStruct((seq,) + seg.shape, seg.dtype))
-    outs.append(jax.ShapeDtypeStruct(count.shape, count.dtype))
-    copies = 4 * (seq - 1) + 2 * seq + 5 * (outer * inner + outer) + total_copies(shape)
+    outs += [low(length, width), wide(length, cols), wide(length, heads * hd)]
+    outs += [low(chunks, heads, hd, hd), wide(own_rows, width), wide(own_rows, width)]
+    outs += [low(own_rows, width), low(length, width)]
+    outs += [low(chips, own_rows, width), low(max(chips - 1, 1), own_rows, width)]
+    in_hbm = len(outs)
+    outs += [jax.ShapeDtypeStruct((seq,) + seg.shape, seg.dtype), wide(8, 128)]
+    outs += [wide(chunks, 8, CHUNK)]
+    copies = 7 * seq + 5 * (outer * inner + outer) + total_copies(shape) + 2 * chunks + 4 * seq
     in_vmem = pl.BlockSpec(memory_space=pltpu.VMEM)
+    smem = pl.BlockSpec(memory_space=pltpu.SMEM)
     got = pl.pallas_call(
-        functools.partial(gather_kernel, shape),
-        in_specs=[HBM] * 7 + [in_vmem],
-        out_specs=[HBM] * (len(outs) - 1) + [in_vmem],
+        functools.partial(gather_kernel, shape, heads, hd),
+        in_specs=[smem] + [HBM] * 7 + [in_vmem, HBM],
+        out_specs=[HBM] * in_hbm + [in_vmem] * 3,
         out_shape=outs,
-        scratch_shapes=total_scratch(shape)
+        scratch_shapes=[
+            pltpu.VMEM(ring(attn).shape, LOW),
+            pltpu.VMEM(ring(w_out).shape, LOW),
+            pltpu.VMEM((length, heads * hd), LOW),
+            pltpu.VMEM((heads, hd, hd), WIDE),
+            pltpu.VMEM((2, CHUNK, width), LOW),
+            pltpu.VMEM((chips, CHUNK, width), LOW),
+            pltpu.VMEM((CHUNK, width), WIDE),
+            pltpu.VMEM((CHUNK, width), WIDE),
+            pltpu.VMEM((CHUNK, width), LOW),
+            pltpu.VMEM((CHUNK, width), LOW),
+            pltpu.VMEM((seq, chunks, 8, CHUNK), WIDE),
+        ]
+        + total_scratch(shape)
         + [
             pltpu.SemaphoreType.DMA((copies,)),
             pltpu.SemaphoreType.DMA((copies,)),
-            pltpu.SemaphoreType.DMA((16,)),
+            pltpu.SemaphoreType.DMA((24 + 6 * chunks,)),
         ],
         compiler_params=pltpu.CompilerParams(
             collective_id=0, has_side_effects=True, vmem_limit_bytes=VMEM_BYTES
         ),
         name="gather_all",
-    )(attn, first, second, w_out, w_down, n1, seg, count)
+    )(rates, attn, first, second, w_out, w_down, n1, seg, count, x)
     flat = lambda v: v.reshape(-1, v.shape[-1])
-    return [flat(v) for v in got[3:8]] + list(got[8:])
+    squares = got[in_hbm + 2][:, 0].reshape(length, 1)
+    return [flat(v) for v in got[3:8]] + list(got[8:14]) + [got[15], got[in_hbm], got[in_hbm + 1], squares]
 
 
 class Total:
@@ -974,8 +1171,15 @@
     x32 = inputs.reshape(block_len, width).astype(WIDE)
     r1 = lax.rsqrt(jnp.mean(x32 * x32, axis=-1, keepdims=True) + 1e-6)
     n1 = x32 * r1
-    full_attn, full_first, full_second, full_out, full_down, n1_all, seg, count = gather_all(
+    rates = lax.dynamic_slice_in_dim(decay_rate, move.s * heads, heads, 0)
+    (
+        full_attn, full_first, full_second, full_out, full_down, n1_all, z, a, states, mixed_out,
+        hsum, n2_all, seg, count, squares,
+    ) = gather_all(
         shape,
+        heads,
+        hd,
+        rates,
         attn_own,
         first_own,
         second_own,
@@ -984,17 +1188,15 @@
         n1.astype(LOW),
         segment_ids.reshape(1, block_len),
         spread(jnp.sum(keep)),
+        inputs.reshape(block_len, width),
     )
     seg = seg.reshape(seq * block_len)
     length = seg.shape[0]
     count = count[:1, :1]
-
     bounds = jnp.concatenate([jnp.full((1,), -1, jnp.int32), seg[CHUNK - 1 :: CHUNK]])
-    rates = lax.dynamic_slice_in_dim(decay_rate, move.s * heads, heads, 0)
-
-    z = dot(n1_all, full_attn)
-    au, a, ss, states = attend(z, seg, bounds, rates, heads, hd)
-    ss_all = move.sum_seq(ss.reshape(length))
+    ra_all = lax.rsqrt(squares / width + 1e-6)
+    r2 = lax.rsqrt(jnp.mean(hsum * hsum, axis=-1, keepdims=True) + 1e-6)
+    m2 = hsum * r2
 
     def rows_of(v, chip):
         return lax.dynamic_slice_in_dim(v, chip * 2 * block_len, 2 * block_len, 0)
@@ -1005,16 +1207,6 @@
             return sum(dot(l, w, 1, d) for l, (_, w, d) in zip(left, pairs)).astype(LOW)
 
         return ScatterSeq(move, part)
-
-    out_sum = product_scatter([(au, full_out, 0)])
-    ra_all = lax.rsqrt(ss_all / width + 1e-6).reshape(length, 1)
-    ra = lax.dynamic_slice_in_dim(ra_all, move.s * block_len, block_len, 0)
-    mixed_out = out_sum.done() * ra
-    hsum = x32 + mixed_out
-    r2 = lax.rsqrt(jnp.mean(hsum * hsum, axis=-1, keepdims=True) + 1e-6)
-    m2 = hsum * r2
-    m2_low = m2.astype(LOW)
-    n2_all = move.gather_seq(m2_low)
 
     g1 = dot(n2_all, full_first)
     g2 = dot(n2_all, full_second)

time: 1260 us -> 1100 us (0.87)
  waiting for transfers between devices: 253 us -> 157 us
  matrix products: 205 us -> 176 us
  Pallas kernels: 672 us -> 655 us
    ppermute x7 -> x5, waiting for transfers between devices: 206 us -> 157 us  [to_chip(): return lax.ppermute(v, 'seq', self.chip_perm)]
    ppermute x2 -> x0, waiting for transfers between devices: 45.6 us -> none  [sum_axis(): v = v + lax.ppermute(v, axis, [(i, i ^ step) for i in range(size)])]
    dot_general x15 -> x12, matrix products: 205 us -> 176 us  [dot(): lax.dot_general(left, right, (((left_dim,), (right_dim,)), ((), ())), pre...]
    pallas_call x2 -> x1, Pallas kernels: 344 us -> 328 us  [gather_all(): pl.pallas_call(functools.partial(gather_kernel, shape, heads, hd), in_spe...]
  transfers between devices with their start and end apart: 23 -> 15, of which waited for: 8 -> 4; matrix products, arithmetic and copies ran while one was open for 8% -> 8% of each run, Pallas kernels for 0% -> 0%
where the time goes in v4:
time: 1100 us; the launch traced here: 1090 us
  Pallas kernels  655 us (60%)
  matrix products  176 us (16%)
  waiting for transfers between devices  157 us (14%)
  other arithmetic  48 us (4%)
  local copies, waits for them, and re-layouts  40.6 us (4%)
    pallas_call x1, Pallas kernels, gather_all(): pl.pallas_call(functools.partial(gather_kernel, shape, heads, hd), in_spe...  328 us
    pallas_call x1, Pallas kernels, back_all(): pl.pallas_call(functools.partial(back_kernel, shape, heads, hd), in_specs...  320 us
    dot_general x12, matrix products, dot(): lax.dot_general(left, right, (((left_dim,), (right_dim,)), ((), ())), pre...  176 us
    ppermute x5, waiting for transfers between devices, to_chip(): return lax.ppermute(v, 'seq', self.chip_perm)  157 us
  transfers between devices with their start and end apart: 15, of which 4 were waited for; matrix products, arithmetic and copies ran while one was open for 8% of the time, Pallas kernels for 0%

profile of v4, /device:TPU:0, one launch (start us, length us, event | category | flops | bytes accessed | tf_op | source)
XLA Modules:
  0.0 1089.9 jit_solution(10423793299839542783)
XLA Ops:
  0.7 2.1 fusion.8
  3.4 3.3 fusion.2.n1_ref
  7.9 3.2 pack_columns.1
  12.3 327.8 %gather_all.1 = (bf16[4,64,2048]{2,1,0:T(8,128)(2,1)}, bf16[4,64,1408]{2,1,0:T(8,128)(2,1)}, bf16[4,64,1408]{2,1,0:T(8,128)(2,1)}, bf16[4,4,2,64,2048]{4,3,2,1,0...) custom-call(f32[4]{0:T(128)} %dynamic_slice.46.rate_ref, ...), custom_call_target="tpu_custom_call" | custom-call | tf_op jit(solution)/shard_map/gather_all/pallas_call | solution.py:625
  340.1 18.6 %fusion.30 = f32[2048,1408]{1,0:T(8,128)} fusion(bf16[2048,2048]{1,0:T(8,128)(2,1)} %get-tuple-element.71, bf16[2048,1408]{1,0:T(8,128)(2,1)} %bitcast.119), kind=kOutput, calls=%fused_computation.78 | convolution fusion | flops 11811160064 | bytes 25690112 | tf_op jit(solution)/shard_map/dot_general | solution.py:17
  358.8 18.9 %multiply_convert_fusion.2 = (bf16[2048,1408]{1,0:T(8,128)(2,1)}, bf16[2048,1408]{1,0:T(8,128)(2,1)}) fusion(f32[2048,1408]{1,0:T(8,128)} %fusion.30, bf16[2048,2048]{1,0:T(8,128)(2,1)S(1)} %copy-done.18, bf16[2048,1408]{1,0:T(8,128)(2,1)} %bitcast.124), kind=kOutput, calls=%fused_computation.2 | convolution fusion | flops 11819810816 | bytes 37224448 | tf_op jit(solution)/shard_map/dot_general | solution.py:17
  377.6 10.1 convolution_convert_fusion.3
  387.8 2.0 copy-done.10
  389.8 1.5 dynamic-slice_bitcast_fusion.2
  391.2 9.9 convolution_convert_fusion.4
  401.2 2.0 copy-done.9
  403.2 1.4 dynamic-slice_bitcast_fusion.3
  405.1 3.7 fusion.12
  408.8 1.5 collective-permute-start.2
  412.3 44.3 %collective-permute-done.2 = bf16[512,2048]{1,0:T(8,128)(2,1)} collective-permute-done((bf16[512,2048]{1,0:T(8,128)(2,1)}, bf16[512,2048]{1,0:T(8,128)(2,1)}, u32[]{:S(2)}, u32[]{:S(2)}) %collective-permute-start.2) | collective-permute-done | bytes 2097184 | tf_op jit(solution)/shard_map/ppermute | solution.py:1071
  456.6 5.7 fusion.9
  462.3 2.9 constant_dynamic-update-slice_fusion.11
  465.6 1.5 collective-permute-start.4
  467.1 45.5 %collective-permute-done.4 = bf16[512,2048]{1,0:T(8,128)(2,1)} collective-permute-done((bf16[512,2048]{1,0:T(8,128)(2,1)}, bf16[512,2048]{1,0:T(8,128)(2,1)}, u32[]{:S(2)}, u32[]{:S(2)}) %collective-permute-start.4) | collective-permute-done | bytes 2097184 | tf_op jit(solution)/shard_map/ppermute | solution.py:1071
  512.6 3.1 constant_dynamic-update-slice_fusion.10
  515.7 3.2 constant_dynamic-update-slice_fusion.9
  518.9 3.1 constant_dynamic-update-slice_fusion.8
  522.0 23.5 %multiply_convert_fusion = (bf16[2048,1408]{1,0:T(8,128)(2,1)}, bf16[2048,1408]{1,0:T(8,128)(2,1)}) fusion(bf16[2048,1408]{1,0:T(8,128)(2,1)} %get-tuple-element.96, f32[2048,1408]{1,0:T(8,128)} %fusion.30, bf16[2048,2048]{1,0:T(8,128)(2,1)} %constant_dynamic-update-slice_fusion.8, bf16[1408,2048]{1,0:T(8,128)(2,1)} %bitcast.129), kind=kOutput, calls=%fused_computation | convolution fusion | flops 11831345152 | bytes 42991616 | tf_op jit(solution)/shard_map/dot_general | solution.py:17
  545.5 11.7 %fusion.19 = f32[1024,2048]{1,0:T(8,128)} fusion(bf16[2048,1408]{1,0:T(8,128)(2,1)} %bitcast.125, bf16[2048,1408]{1,0:T(8,128)(2,1)} %get-tuple-element.61, s32[]{:T(128)S(6)} %select_n.91), kind=kOutput, calls=%fused_computation.42 | convolution fusion | flops 5905580032 | bytes 17039364 | tf_op jit(solution)/shard_map/dot_general | solution.py:17
  557.2 11.0 %add_convert_fusion.1 = bf16[1024,2048]{1,0:T(8,128)(2,1)S(1)} fusion(f32[1024,2048]{1,0:T(8,128)} %fusion.19, bf16[2048,1408]{1,0:T(8,128)(2,1)} %bitcast.120, bf16[2048,1408]{1,0:T(8,128)(2,1)} %get-tuple-element.62, s32[]{:T(128)S(6)} %select_n.91), kind=kOutput, calls=%fused_computation.4 | convolution fusion | flops 5909774336 | bytes 21233668 | tf_op jit(solution)/shard_map/dot_general | solution.py:17
  568.2 16.8 %convolution_convert_fusion.2 = bf16[1408,2048]{1,0:T(8,128)(2,1)} fusion(bf16[2048,1408]{1,0:T(8,128)(2,1)} %get-tuple-element.60, bf16[2048,2048]{1,0:T(8,128)(2,1)S(1)} %bitcast.93), kind=kOutput, calls=%fused_computation.7 | convolution fusion | flops 11814043648 | bytes 19922944 | tf_op jit(solution)/shard_map/dot_general | solution.py:17
  585.0 12.0 %fusion.16 = f32[1024,2048]{1,0:T(8,128)} fusion(bf16[2048,1408]{1,0:T(8,128)(2,1)} %bitcast.126, bf16[2048,1408]{1,0:T(8,128)(2,1)} %get-tuple-element.61, s32[]{:T(128)S(6)} %select_n.86), kind=kOutput, calls=%fused_computation.39 | convolution fusion | flops 5905580032 | bytes 17039364 | tf_op jit(solution)/shard_map/dot_general | solution.py:17
  597.8 10.0 add_convert_fusion
  607.9 1.6 dynamic-slice_bitcast_fusion.1
  609.5 2.1 fusion.10
  611.7 1.5 collective-permute-start.8
  614.3 1.3 copy.29.segc
  619.3 3.8 convert_bitcast_fusion
  623.1 36.9 %collective-permute-done.8 = bf16[512,2048]{1,0:T(8,128)(2,1)} collective-permute-done((bf16[512,2048]{1,0:T(8,128)(2,1)}, bf16[512,2048]{1,0:T(8,128)(2,1)}, u32[]{:S(2)}, u32[]{:S(2)}) %collective-permute-start.8) | collective-permute-done | bytes 2097184 | tf_op jit(solution)/shard_map/ppermute | solution.py:1071
  660.0 4.1 multiply_reduce_fusion.1
  664.2 7.3 constant_dynamic-update-slice_fusion.7
  671.5 2.7 multiply_reduce_fusion
  674.3 1.6 collective-permute-start.13
  676.5 17.4 %convolution_convert_fusion.1 = bf16[2048,1408]{1,0:T(8,128)(2,1)} fusion(bf16[2048,2048]{1,0:T(8,128)(2,1)S(1)} %bitcast.118, bf16[2048,1408]{1,0:T(8,128)(2,1)} %get-tuple-element.61), kind=kOutput, calls=%fused_computation.6 | convolution fusion | flops 11814043648 | bytes 19922944 | tf_op jit(solution)/shard_map/dot_general | solution.py:17
  694.0 30.2 %collective-permute-done.10 = bf16[512,2048]{1,0:T(8,128)(2,1)} collective-permute-done((bf16[512,2048]{1,0:T(8,128)(2,1)}, bf16[512,2048]{1,0:T(8,128)(2,1)}, u32[]{:S(2)}, u32[]{:S(2)}) %collective-permute-start.10) | collective-permute-done | bytes 2097184 | tf_op jit(solution)/shard_map/ppermute | solution.py:1071
  724.2 15.6 %convolution_convert_fusion = bf16[2048,1408]{1,0:T(8,128)(2,1)} fusion(bf16[2048,2048]{1,0:T(8,128)(2,1)S(1)} %bitcast.118, bf16[2048,1408]{1,0:T(8,128)(2,1)S(1)} %bitcast.131), kind=kOutput, calls=%fused_computation.5 | convolution fusion | flops 11814043648 | bytes 19922944 | tf_op jit(solution)/shard_map/dot_general | solution.py:17
  742.8 1.5 constant_dynamic-update-slice_fusion.6
  744.3 3.2 constant_dynamic-update-slice_fusion.5
  747.5 3.1 constant_dynamic-update-slice_fusion.4.dh
  751.9 320.3 %back_all.1 = (f32[512,2048]{1,0:T(8,128)}, f32[176,2048]{1,0:T(8,128)}, f32[64,2048]{1,0:T(8,128)}, f32[8,128]{1,0:T(8,128)}, bf16[4,64,1408]{2,1,0:T(8,128)(2,...) custom-call(f32[4]{0:T(128)} %dynamic_slice.46.rate_ref, ...), custom_call_target="tpu_custom_call" | custom-call | tf_op jit(solution)/shard_map/back_all/pallas_call | solution.py:1023
  1072.2 3.0 fusion.3
  1076.4 5.2 fusion.7
  1082.4 4.0 unpack_columns.1
  (112 shorter events, 18.1 us)
Async XLA Ops:
  0.6 6.0 copy-start.17
  0.7 6.6 copy-start.19
  2.8 0.6 copy-start.15
  340.1 18.6 %copy-start.18 = (bf16[2048,2048]{1,0:T(8,128)(2,1)S(1)}, bf16[2048,2048]{1,0:T(8,128)(2,1)}, u32[]{:S(2)}) copy-start(bf16[2048,2048]{1,0:T(8,128)(2,1)} %get-tuple-element.71) | copy-start | bytes 25165828
  387.8 2.0 copy-start.10
  391.2 13.9 %collective-permute-start.1 = (bf16[512,2048]{1,0:T(8,128)(2,1)}, bf16[512,2048]{1,0:T(8,128)(2,1)S(1)}, u32[]{:S(2)}, u32[]{:S(2)}) collective-permute-start(bf16[512,2048]{1,0:T(8,128)(2,1)} %dynamic-slice_bitcast_fusion.2), channel_id=1, source_target_pairs={{0,8},{8,0},{16,24},{24,16},{1,9},{9,1},{17,25},{25,17},{2,10},{10... | collective-permute-start | bytes 6291464 | tf_op jit(solution)/shard_map/ppermute | solution.py:1068
  401.2 2.0 copy-start.9
  404.6 7.7 collective-permute-start
  408.8 47.9 %collective-permute-start.2 = (bf16[512,2048]{1,0:T(8,128)(2,1)}, bf16[512,2048]{1,0:T(8,128)(2,1)}, u32[]{:S(2)}, u32[]{:S(2)}) collective-permute-start(bf16[512,2048]{1,0:T(8,128)(2,1)} %fusion.12), channel_id=1, source_target_pairs={{0,16},{8,24},{16,0},{24,8},{1,17},{9,25},{17,1},{25,9},{2,18},{10... | collective-permute-start | bytes 6291464 | tf_op jit(solution)/shard_map/ppermute | solution.py:1071
  410.3 46.4 %copy-start.4 = (bf16[1,512,2048]{2,1,0:T(8,128)(2,1)S(1)}, bf16[1,512,2048]{2,1,0:T(8,128)(2,1)}, u32[]{:S(2)}) copy-start(bf16[1,512,2048]{2,1,0:T(8,128)(2,1)} %param.14) | copy-start | bytes 6291460
  462.3 3.3 copy-start
  465.6 47.0 %collective-permute-start.4 = (bf16[512,2048]{1,0:T(8,128)(2,1)}, bf16[512,2048]{1,0:T(8,128)(2,1)}, u32[]{:S(2)}, u32[]{:S(2)}) collective-permute-start(bf16[512,2048]{1,0:T(8,128)(2,1)} %get-tuple-element.91), channel_id=1, source_target_pairs={{0,16},{8,24},{16,0},{24,8},{1,17},{9,25},{17,1},{25,9},{2,18},{10... | collective-permute-start | bytes 6291464 | tf_op jit(solution)/shard_map/ppermute | solution.py:1071
  467.1 45.5 %collective-permute-start.3 = (bf16[512,2048]{1,0:T(8,128)(2,1)}, bf16[512,2048]{1,0:T(8,128)(2,1)}, u32[]{:S(2)}, u32[]{:S(2)}) collective-permute-start(bf16[512,2048]{1,0:T(8,128)(2,1)} %get-tuple-element.91), channel_id=1, source_target_pairs={{0,8},{8,0},{16,24},{24,16},{1,9},{9,1},{17,25},{25,17},{2,10},{10... | collective-permute-start | bytes 6291464 | tf_op jit(solution)/shard_map/ppermute | solution.py:1068
  512.6 6.3 collective-permute-start.5
  545.5 22.7 %slice-start = ((s8[8388608]{0:T(1024)(128)(4,1)}), s8[4194304]{0:T(1024)(128)(4,1)S(1)}, s32[]{:S(2)}) async-start(s8[8388608]{0:T(1024)(128)(4,1)} %bitcast.92), calls=%async_computation | async-start | bytes 8388608
  557.2 11.0 %slice-start.1 = ((s8[8388608]{0:T(1024)(128)(4,1)}), s8[4194304]{0:T(1024)(128)(4,1)S(1)}, s32[]{:S(2)}) async-start(s8[8388608]{0:T(1024)(128)(4,1)} %bitcast.92), calls=%async_computation.1 | async-start | bytes 8388608
  557.2 40.6 %slice-start.4 = ((s8[5767168]{0:T(1024)(128)(4,1)}), s8[4194304]{0:T(1024)(128)(4,1)S(1)}, s32[]{:S(2)}) async-start(s8[5767168]{0:T(1024)(128)(4,1)} %bitcast.121), calls=%async_computation.4 | async-start | bytes 8388608
  568.2 29.6 %slice-start.5 = ((s8[5767168]{0:T(1024)(128)(4,1)}), s8[1572864]{0:T(1024)(128)(4,1)S(1)}, s32[]{:S(2)}) async-start(s8[5767168]{0:T(1024)(128)(4,1)} %bitcast.121), calls=%async_computation.5 | async-start | bytes 3145728
  597.3 12.3 %collective-permute-start.7 = (bf16[512,2048]{1,0:T(8,128)(2,1)S(1)}, bf16[512,2048]{1,0:T(8,128)(2,1)S(1)}, u32[]{:S(2)}, u32[]{:S(2)}) collective-permute-start(bf16[512,2048]{1,0:T(8,128)(2,1)S(1)} %dynamic-slice_bitcast_fusion), channel_id=1, source_target_pairs={{0,8},{8,0},{16,24},{24,16},{1,9},{9,1},{17,25},{25,17},{2,10},{10... | collective-permute-start | bytes 6291464 | tf_op jit(solution)/shard_map/ppermute | solution.py:1068
  607.9 3.8 copy-start.6
  609.5 13.7 %collective-permute-start.6 = (bf16[512,2048]{1,0:T(8,128)(2,1)}, bf16[512,2048]{1,0:T(8,128)(2,1)}, u32[]{:S(2)}, u32[]{:S(2)}) collective-permute-start(bf16[512,2048]{1,0:T(8,128)(2,1)} %dynamic-slice_bitcast_fusion.1), channel_id=1, source_target_pairs={{0,8},{8,0},{16,24},{24,16},{1,9},{9,1},{17,25},{25,17},{2,10},{10... | collective-permute-start | bytes 6291464 | tf_op jit(solution)/shard_map/ppermute | solution.py:1068
  611.7 2.6 copy-start.14
  611.7 48.3 %collective-permute-start.8 = (bf16[512,2048]{1,0:T(8,128)(2,1)}, bf16[512,2048]{1,0:T(8,128)(2,1)}, u32[]{:S(2)}, u32[]{:S(2)}) collective-permute-start(bf16[512,2048]{1,0:T(8,128)(2,1)} %fusion.10), channel_id=1, source_target_pairs={{0,16},{8,24},{16,0},{24,8},{1,17},{9,25},{17,1},{25,9},{2,18},{10... | collective-permute-start | bytes 6291464 | tf_op jit(solution)/shard_map/ppermute | solution.py:1071
  617.9 42.1 %copy-start.3 = (f32[512,2048]{1,0:T(8,128)S(1)}, f32[512,2048]{1,0:T(8,128)}, u32[]{:S(2)}) copy-start(f32[512,2048]{1,0:T(8,128)} %get-tuple-element.51) | copy-start | bytes 12582916
  623.1 41.0 %copy-start.1 = (f32[512,2048]{1,0:T(8,128)S(1)}, f32[512,2048]{1,0:T(8,128)}, u32[]{:S(2)}) copy-start(f32[512,2048]{1,0:T(8,128)} %copy-done) | copy-start | bytes 12582916
  623.1 41.0 %copy-start.7 = (bf16[1024,2048]{1,0:T(8,128)(2,1)S(1)}, bf16[1024,2048]{1,0:T(8,128)(2,1)}, u32[]{:S(2)}) copy-start(bf16[1024,2048]{1,0:T(8,128)(2,1)} %copy-done.6) | copy-start | bytes 12582916
  664.1 12.4 %slice-start.2 = ((s8[8388608]{0:T(1024)(128)(4,1)}), s8[4194304]{0:T(1024)(128)(4,1)S(1)}, s32[]{:S(2)}) async-start(s8[8388608]{0:T(1024)(128)(4,1)} %bitcast.117), calls=%async_computation.2 | async-start | bytes 8388608
  664.2 7.3 copy-start.11
  664.2 12.4 %slice-start.3 = ((s8[8388608]{0:T(1024)(128)(4,1)}), s8[4194304]{0:T(1024)(128)(4,1)S(1)}, s32[]{:S(2)}) async-start(s8[8388608]{0:T(1024)(128)(4,1)} %bitcast.117), calls=%async_computation.3 | async-start | bytes 8388608
  674.2 50.0 %slice-start.6 = ((s8[5767168]{0:T(1024)(128)(4,1)}), s8[4194304]{0:T(1024)(128)(4,1)S(1)}, s32[]{:S(2)}) async-start(s8[5767168]{0:T(1024)(128)(4,1)} %bitcast.130), calls=%async_computation.6 | async-start | bytes 8388608
  674.2 50.0 %slice-start.7 = ((s8[5767168]{0:T(1024)(128)(4,1)}), s8[1572864]{0:T(1024)(128)(4,1)S(1)}, s32[]{:S(2)}) async-start(s8[5767168]{0:T(1024)(128)(4,1)} %bitcast.130), calls=%async_computation.7 | async-start | bytes 3145728
  674.2 65.9 %collective-permute-start.12 = (f32[512]{0:T(512)S(1)}, f32[512]{0:T(512)S(1)}, u32[]{:S(2)}, u32[]{:S(2)}) collective-permute-start(f32[512]{0:T(512)S(1)} %broadcast_multiply_fusion.2), channel_id=1, source_target_pairs={{0,8},{8,0},{16,24},{24,16},{1,9},{9,1},{17,25},{25,17},{2,10},{10... | collective-permute-start | bytes 6152 | tf_op jit(solution)/shard_map/ppermute | solution.py:1068
  674.3 65.9 %collective-permute-start.13 = (f32[512]{0:T(512)S(1)}, f32[512]{0:T(512)S(1)}, u32[]{:S(2)}, u32[]{:S(2)}) collective-permute-start(f32[512]{0:T(512)S(1)} %broadcast_multiply_fusion.2), channel_id=1, source_target_pairs={{0,16},{8,24},{16,0},{24,8},{1,17},{9,25},{17,1},{25,9},{2,18},{10... | collective-permute-start | bytes 6152 | tf_op jit(solution)/shard_map/ppermute | solution.py:1071
  675.9 66.9 %collective-permute-start.9 = (bf16[512,2048]{1,0:T(8,128)(2,1)}, bf16[512,2048]{1,0:T(8,128)(2,1)S(1)}, u32[]{:S(2)}, u32[]{:S(2)}) collective-permute-start(bf16[512,2048]{1,0:T(8,128)(2,1)} %get-tuple-element.64), channel_id=1, source_target_pairs={{0,8},{8,0},{16,24},{24,16},{1,9},{9,1},{17,25},{25,17},{2,10},{10... | collective-permute-start | bytes 6291464 | tf_op jit(solution)/shard_map/ppermute | solution.py:1068
  676.0 48.2 %collective-permute-start.10 = (bf16[512,2048]{1,0:T(8,128)(2,1)}, bf16[512,2048]{1,0:T(8,128)(2,1)}, u32[]{:S(2)}, u32[]{:S(2)}) collective-permute-start(bf16[512,2048]{1,0:T(8,128)(2,1)} %get-tuple-element.64), channel_id=1, source_target_pairs={{0,16},{8,24},{16,0},{24,8},{1,17},{9,25},{17,1},{25,9},{2,18},{10... | collective-permute-start | bytes 6291464 | tf_op jit(solution)/shard_map/ppermute | solution.py:1071
  724.2 23.3 %collective-permute-start.11 = (bf16[512,2048]{1,0:T(8,128)(2,1)}, bf16[512,2048]{1,0:T(8,128)(2,1)}, u32[]{:S(2)}, u32[]{:S(2)}) collective-permute-start(bf16[512,2048]{1,0:T(8,128)(2,1)} %collective-permute-done.10), channel_id=1, source_target_pairs={{0,8},{8,0},{16,24},{24,16},{1,9},{9,1},{17,25},{25,17},{2,10},{10... | collective-permute-start | bytes 6291464 | tf_op jit(solution)/shard_map/ppermute | solution.py:1068
  741.1 1.5 collective-permute-start.14
  742.8 4.7 copy-start.8
  751.9 320.3 %copy-start.2 = (bf16[1,512,2048]{2,1,0:T(8,128)(2,1)S(1)}, bf16[1,512,2048]{2,1,0:T(8,128)(2,1)}, u32[]{:S(2)}) copy-start(bf16[1,512,2048]{2,1,0:T(8,128)(2,1)} %param.13) | copy-start | bytes 6291460
  751.9 320.3 %copy-start.16 = (f32[512]{0:T(512)S(1)}, f32[512]{0:T(512)}, u32[]{:S(2)}) copy-start(f32[512]{0:T(512)} %copy-done.15) | copy-start | bytes 6148
  1072.2 4.3 copy-start.5
  1076.4 10.0 copy-start.13
  1081.6 5.6 copy-start.12

commit v5 on v4

--- a/solution.py
+++ b/solution.py
@@ -335,10 +335,10 @@
 
 
 class Rows:
-    def __init__(self, net, own, whole):
-        t = own.shape[0]
+    def __init__(self, net, own, whole, start=0):
+        t, each = own.shape[0], whole.shape[0] // net.seq
         self.net, self.whole = net, whole
-        spot = lambda s: whole.at[pl.ds(pl.multiple_of(s * t, t), t)]
+        spot = lambda s: whole.at[pl.ds(pl.multiple_of(s * each + start, t), t)]
         self.spot = spot
         self.far = [
             net.send(own, spot(net.s), net.at_seq(lax.rem(net.chip + dx, net.chips) * 2 + net.core))
@@ -1036,102 +1036,316 @@
     )[:7]
 
 
-class Moves:
-    def __init__(self):
-        self.seq = lax.axis_size("seq")
-        self.fsdp = lax.axis_size("fsdp")
-        self.inner = 2 if self.fsdp == 8 else 4
-        self.outer = self.fsdp // self.inner
-        self.chips = self.seq // 2
-        s = lax.axis_index("seq")
-        f = lax.axis_index("fsdp")
-        self.s, self.f = s, f
-        self.chip, self.core = s // 2, s % 2
-        self.out_at, self.in_at = f // self.inner, f % self.inner
-        chips, inner, outer = self.chips, self.inner, self.outer
-        self.core_perm = [(i, i ^ 1) for i in range(self.seq)]
-        self.chip_perm = [
-            (x * 2 + c, (x + 1) % chips * 2 + c) for x in range(chips) for c in range(2)
+def spans(n, step=512):
+    return [slice(at, min(at + step, n)) for at in range(0, n, step)]
+
+
+def glu_kernel(
+    shape,
+    n2_all, w_first, w_second, w_down, hsum_ref, teacher_ref, keep_ref, scale_ref, mixed_ref,
+    layer_out, g_down, g_first, g_second, dh_ref, dh_all, dy_all, dy_own, dh_own,
+    core_y, chip_y, core_n, chip_n,
+    loss_ref, mean_all,
+    one_all, two_all, p_all, dy_wide, stage, term, wide_tile, hsum_tile, mixed_tile, low_tile, sent_tile,
+    send_sem, recv_sem, local_sem,
+):
+    net = Net(shape, send_sem, recv_sem, local_sem)
+    width = n2_all.shape[1]
+    ffs = p_all.shape[1]
+    own_rows = hsum_ref.shape[0]
+    per = own_rows // CHUNK
+    wide = min(512, width)
+    blocks = width // wide
+    net.barrier()
+
+    def rows_at(n):
+        return pl.ds(pl.multiple_of(n * CHUNK, CHUNK), CHUNK)
+
+    def of_chip(dx):
+        return lax.rem(net.chip + dx, net.chips)
+
+    def tiles(dx, src, body):
+        base = of_chip(dx) * 2 * per
+        pltpu.emit_pipeline(
+            lambda ref: body(base + pl.program_id(0), ref),
+            grid=(2 * per,),
+            in_specs=[pl.BlockSpec((CHUNK, width), lambda i: (base + i, 0))],
+        )(src)
+
+    def columns(each):
+        def one(j, _):
+            each(pl.ds(pl.multiple_of(j * wide, wide), wide))
+            return 0
+
+        lax.fori_loop(0, blocks, one, 0)
+
+    used = [None, None]
+    turns = [0]
+
+    def slot():
+        i = turns[0] % 2
+        turns[0] += 1
+        if used[i] is not None:
+            net.left(used[i])
+        return i
+
+    class Exchange:
+        def __init__(self, product, core_in, chip_in):
+            self.product, self.core_in, self.chip_in = product, core_in, chip_in
+            self.near, self.far = {}, {}
+
+        def give(self, dx):
+            for t in range(per):
+                i = slot()
+                rows = rows_at((of_chip(dx) * 2 + 1 - net.core) * per + t)
+
+                def store(at):
+                    stage[i, :, at] = self.product(rows, at).astype(LOW)
+
+                columns(store)
+                used[i] = self.near[dx, t] = net.send(
+                    stage.at[i],
+                    self.core_in.at[dx, pl.ds(t * CHUNK, CHUNK)],
+                    net.at_seq(net.chip * 2 + 1 - net.core),
+                )
+
+        def keep(self, dx, finish=None):
+            for t in range(per):
+                span = pl.ds(t * CHUNK, CHUNK)
+                rows = rows_at((of_chip(dx) * 2 + net.core) * per + t)
+                self.near[dx, t].wait_recv()
+                loads = [net.copy(self.core_in.at[dx, span], term.at[0])]
+                if dx == 0:
+                    for j in range(1, net.chips):
+                        self.far[j, t].wait_recv()
+                        loads.append(net.copy(self.chip_in.at[j - 1, span], term.at[j]))
+                    loads.append(net.copy(hsum_ref.at[span], hsum_tile))
+                else:
+                    i = slot()
+                for load in loads:
+                    load.wait()
+
+                def store(at):
+                    total = self.product(rows, at) + term[0, :, at].astype(WIDE)
+                    if dx == 0:
+                        for j in range(1, net.chips):
+                            total = total + term[j, :, at].astype(WIDE)
+                        wide_tile[:, at] = total
+                    else:
+                        stage[i, :, at] = total.astype(LOW)
+
+                columns(store)
+                if dx == 0:
+                    finish(t, span)
+                else:
+                    used[i] = self.far[dx, t] = net.send(
+                        stage.at[i],
+                        self.chip_in.at[dx - 1, span],
+                        net.at_seq(of_chip(dx) * 2 + net.core),
+                    )
+
+    def hidden(n, n2):
+        rows = rows_at(n)
+        for b in spans(ffs):
+            one = dot(n2[...], w_first[:, b])
+            two = dot(n2[...], w_second[:, b])
+            one_all[rows, b] = one.astype(LOW)
+            two_all[rows, b] = two.astype(LOW)
+            p_all[rows, b] = (one * two).astype(LOW)
+
+    y_sum = Exchange(lambda rows, at: dot(p_all[rows, :], w_down[:, at]), core_y, chip_y)
+    for dx in range(1, net.chips):
+        tiles(dx, n2_all, hidden)
+        y_sum.give(dx)
+        y_sum.keep(dx)
+    tiles(0, n2_all, hidden)
+    y_sum.give(0)
+
+    loss_ref[...] = jnp.zeros_like(loss_ref)
+    dy_rows = []
+
+    def finish_y(t, span):
+        net.copy(teacher_ref.at[span], sent_tile).wait()
+        keep = keep_ref[span, :]
+        scale = scale_ref[:1, :1] * keep
+
+        def one(j, squares):
+            at = pl.ds(pl.multiple_of(j * wide, wide), wide)
+            y = hsum_tile[:, at] + wide_tile[:, at]
+            low_tile[:, at] = y.astype(LOW)
+            error = y - sent_tile[:, at].astype(WIDE)
+            dy = scale * error
+            dy_wide[span, at] = dy
+            stage[1, :, at] = dy.astype(LOW)
+            return squares + jnp.sum(keep * error * error, axis=1, keepdims=True)
+
+        squares = lax.fori_loop(0, blocks, one, jnp.zeros((CHUNK, 1), WIDE))
+        loss_ref[...] += jnp.broadcast_to(jnp.sum(squares, axis=0, keepdims=True), (8, 128))
+        outs = [
+            net.copy(low_tile, layer_out.at[span]),
+            net.copy(stage.at[1], dy_own.at[span]),
         ]
-        self.out_perm = [
-            (o * inner + i, (o + 1) % outer * inner + i)
-            for o in range(outer)
-            for i in range(inner)
-        ]
-        self.in_perm = [
-            (o * inner + i, o * inner + (i + 1) % inner)
-            for o in range(outer)
-            for i in range(inner)
-        ]
-
-    def to_core(self, v):
-        return lax.ppermute(v, "seq", self.core_perm)
-
-    def to_chip(self, v):
-        return lax.ppermute(v, "seq", self.chip_perm)
-
-    def to_out(self, v):
-        return lax.ppermute(v, "fsdp", self.out_perm)
-
-    def to_in(self, v):
-        return lax.ppermute(v, "fsdp", self.in_perm)
-
-    def gather_seq(self, v):
-        whole = empty((self.seq * v.shape[0],) + v.shape[1:], v.dtype)
-        t = v.shape[0]
-        now = v
-        for k in range(self.chips):
-            later = self.to_chip(now) if k < self.chips - 1 else None
-            other = self.to_core(now)
-            chip = (self.chip - k) % self.chips
-            place = lambda whole, part, i: lax.dynamic_update_slice_in_dim(whole, part, i * t, 0)
-            whole = place(whole, now, chip * 2 + self.core)
-            whole = place(whole, other, chip * 2 + 1 - self.core)
-            now = later
-        return whole
-
-    def sum_axis(self, v, axis, size):
-        step = 1
-        while step < size:
-            v = v + lax.ppermute(v, axis, [(i, i ^ step) for i in range(size)])
-            step *= 2
-        return v
-
-    def sum_seq(self, v):
-        return self.sum_axis(v, "seq", self.seq)
-
-    def sum_all(self, v):
-        return self.sum_axis(self.sum_seq(v), "fsdp", self.fsdp)
-
-
-class ScatterSeq:
-    def __init__(self, move, part, kind=LOW):
-        self.move, self.part, self.kind = move, part, kind
-        self.held = None
-        self.term = None
-        for k in range(move.chips - 1):
-            total = self.own(k)
-            self.held = move.to_chip(total.astype(kind))
-
-    def own(self, k, *tokens):
-        move = self.move
-        self.term = self.part((move.chip - 1 - k) % move.chips, *tokens)
-        term = self.term.reshape((2, -1) + self.term.shape[1:])
-        give = lax.dynamic_index_in_dim(term, 1 - move.core, 0, False)
-        keep = lax.dynamic_index_in_dim(term, move.core, 0, False)
-        total = keep.astype(WIDE) + move.to_core(give).astype(WIDE)
-        if self.held is not None:
-            total = total + self.held.astype(WIDE)
-        return total
-
-    def done(self, *tokens):
-        return self.own(self.move.chips - 1, *tokens)
-
-
-def after(v, *tokens):
-    if not tokens:
-        return v
-    return lax.optimization_barrier((v,) + tokens)[0]
+        for out in outs:
+            out.wait()
+        dy_rows.append(Rows(net, dy_own.at[span], dy_all, t * CHUNK))
+
+    def free_stage():
+        for i in range(2):
+            if used[i] is not None:
+                net.left(used[i])
+            used[i] = None
+
+    free_stage()
+    y_sum.keep(0, finish_y)
+
+    def slopes(n, dy):
+        rows = rows_at(n)
+        for b in spans(ffs):
+            dp = dot(dy[...], w_down[b, :], 1, 1)
+            one = one_all[rows, b].astype(WIDE)
+            two = two_all[rows, b].astype(WIDE)
+            one_all[rows, b] = (dp * two).astype(LOW)
+            two_all[rows, b] = (dp * one).astype(LOW)
+
+    n_sum = Exchange(
+        lambda rows, at: dot(one_all[rows, :], w_first[at, :], 1, 1)
+        + dot(two_all[rows, :], w_second[at, :], 1, 1),
+        core_n,
+        chip_n,
+    )
+    for rows in dy_rows:
+        rows.near[0].wait_recv()
+        rows.near = rows.near[1:]
+        rows.own.wait()
+    tiles(0, dy_all, slopes)
+    n_sum.give(0)
+    for rows in dy_rows:
+        rows.turn()
+    for rows in dy_rows:
+        for copy in rows.near:
+            copy.wait_recv()
+    for dx in range(1, net.chips):
+        tiles(dx, dy_all, slopes)
+        n_sum.give(dx)
+        n_sum.keep(dx)
+
+    length = p_all.shape[0]
+    step = 256
+
+    def grad_down(dy, out):
+        for b in spans(ffs):
+            out[b, :] = dot(p_all[:, b], dy[...], 0, 0).astype(LOW)
+
+    pltpu.emit_pipeline(
+        grad_down,
+        grid=(width // step,),
+        in_specs=[pl.BlockSpec((length, step), lambda i: (0, i))],
+        out_specs=[pl.BlockSpec((ffs, step), lambda i: (0, i))],
+    )(dy_all, g_down)
+
+    def grad_columns(held, target):
+        def body(n2, out):
+            for b in spans(ffs):
+                out[:, b] = dot(n2[...], held[:, b], 0, 0).astype(LOW)
+
+        pltpu.emit_pipeline(
+            body,
+            grid=(width // step,),
+            in_specs=[pl.BlockSpec((length, step), lambda i: (0, i))],
+            out_specs=[pl.BlockSpec((step, ffs), lambda i: (i, 0))],
+        )(n2_all, target)
+
+    grad_columns(one_all, g_first)
+    dh_rows = []
+    means = []
+
+    def finish_n(t, span):
+        net.copy(mixed_ref.at[span], mixed_tile).wait()
+
+        def add(j, sums):
+            at = pl.ds(pl.multiple_of(j * wide, wide), wide)
+            hsum = hsum_tile[:, at]
+            return (
+                sums[0] + jnp.sum(hsum * hsum, axis=1, keepdims=True),
+                sums[1] + jnp.sum(hsum * wide_tile[:, at], axis=1, keepdims=True),
+            )
+
+        zero = jnp.zeros((CHUNK, 1), WIDE)
+        squares, cross = lax.fori_loop(0, blocks, add, (zero, zero))
+        r2 = lax.rsqrt(squares / width + 1e-6)
+        mean = r2 * cross / width
+
+        def one(j, total):
+            at = pl.ds(pl.multiple_of(j * wide, wide), wide)
+            m2 = hsum_tile[:, at] * r2
+            dh = dy_wide[span, at] + r2 * (wide_tile[:, at] - m2 * mean)
+            wide_tile[:, at] = dh
+            low = dh.astype(LOW)
+            low_tile[:, at] = low
+            return total + jnp.sum(low.astype(WIDE) * mixed_tile[:, at], axis=1, keepdims=True)
+
+        total = lax.fori_loop(0, blocks, one, zero) / width
+        at = net.s * per + t
+        mean_all[at] = jnp.transpose(jnp.broadcast_to(total, (CHUNK, 128)))[:8]
+        for _, _, s in net.seq_peers():
+            means.append(net.send(mean_all.at[at], mean_all.at[at], net.at_seq(s)))
+        outs = [net.copy(wide_tile, dh_ref.at[span]), net.copy(low_tile, dh_own.at[span])]
+        for out in outs:
+            out.wait()
+        dh_rows.append(Rows(net, dh_own.at[span], dh_all, t * CHUNK))
+
+    n_sum.keep(0, finish_n)
+    grad_columns(two_all, g_second)
+    for rows in dh_rows:
+        rows.turn()
+    for rows in dh_rows:
+        rows.done()
+    for copy in means:
+        copy.wait_recv()
+    net.finish()
+
+
+def glu_all(shape, n2_all, w_first, w_second, w_down, hsum, teacher, keep, scale, mixed):
+    seq, fsdp, inner = shape
+    length, width = n2_all.shape
+    ffs = w_first.shape[1]
+    own_rows = length // seq
+    chips = seq // 2
+    chunks = length // CHUNK
+    low = lambda *dims: jax.ShapeDtypeStruct(dims, LOW)
+    wide = lambda *dims: jax.ShapeDtypeStruct(dims, WIDE)
+    outs = [low(own_rows, width), low(ffs, width), low(width, ffs), low(width, ffs)]
+    outs += [wide(own_rows, width), low(length, width), low(length, width)]
+    outs += [low(own_rows, width)] * 2
+    outs += [low(chips, own_rows, width), low(max(chips - 1, 1), own_rows, width)] * 2
+    in_hbm = len(outs)
+    outs += [wide(8, 128), wide(chunks, 8, CHUNK)]
+    in_vmem = pl.BlockSpec(memory_space=pltpu.VMEM)
+    copies = 16 * chunks + 16 * seq
+    return pl.pallas_call(
+        functools.partial(glu_kernel, shape),
+        in_specs=[HBM] + [in_vmem] * 3 + [HBM] * 2 + [in_vmem] * 2 + [HBM],
+        out_specs=[HBM] * in_hbm + [in_vmem] * 2,
+        out_shape=outs,
+        scratch_shapes=[pltpu.VMEM((length, ffs), LOW)] * 3
+        + [
+            pltpu.VMEM((own_rows, width), WIDE),
+            pltpu.VMEM((2, CHUNK, width), LOW),
+            pltpu.VMEM((chips, CHUNK, width), LOW),
+            pltpu.VMEM((CHUNK, width), WIDE),
+            pltpu.VMEM((CHUNK, width), WIDE),
+            pltpu.VMEM((CHUNK, width), WIDE),
+            pltpu.VMEM((CHUNK, width), LOW),
+            pltpu.VMEM((CHUNK, width), LOW),
+            pltpu.SemaphoreType.DMA((copies,)),
+            pltpu.SemaphoreType.DMA((copies,)),
+            pltpu.SemaphoreType.DMA((16 * chunks,)),
+        ],
+        compiler_params=pltpu.CompilerParams(
+            collective_id=2, has_side_effects=True, vmem_limit_bytes=VMEM_BYTES
+        ),
+        name="glu_all",
+    )(n2_all, w_first, w_second, w_down, hsum, teacher, keep, scale, mixed)
 
 
 def on_device(
@@ -1149,8 +1363,7 @@
     w_second,
     w_down,
 ):
-    move = Moves()
-    seq = move.seq
+    seq, fsdp = lax.axis_size("seq"), lax.axis_size("fsdp")
     batch, block_len, width = inputs.shape
     assert batch == 1
     heads_all = decay_rate.shape[0]
@@ -1161,7 +1374,7 @@
     ffs = ff // seq
     cols = heads * 4 * hd
 
-    shape = net_shape(seq, move.fsdp)
+    shape = net_shape(seq, fsdp)
     keep = valid.astype(WIDE).reshape(block_len, 1)
     spread = lambda v: jnp.broadcast_to(v, (8, 128))
 
@@ -1171,7 +1384,7 @@
     x32 = inputs.reshape(block_len, width).astype(WIDE)
     r1 = lax.rsqrt(jnp.mean(x32 * x32, axis=-1, keepdims=True) + 1e-6)
     n1 = x32 * r1
-    rates = lax.dynamic_slice_in_dim(decay_rate, move.s * heads, heads, 0)
+    rates = lax.dynamic_slice_in_dim(decay_rate, lax.axis_index("seq") * heads, heads, 0)
     (
         full_attn, full_first, full_second, full_out, full_down, n1_all, z, a, states, mixed_out,
         hsum, n2_all, seg, count, squares,
@@ -1195,51 +1408,26 @@
     count = count[:1, :1]
     bounds = jnp.concatenate([jnp.full((1,), -1, jnp.int32), seg[CHUNK - 1 :: CHUNK]])
     ra_all = lax.rsqrt(squares / width + 1e-6)
-    r2 = lax.rsqrt(jnp.mean(hsum * hsum, axis=-1, keepdims=True) + 1e-6)
-    m2 = hsum * r2
-
-    def rows_of(v, chip):
-        return lax.dynamic_slice_in_dim(v, chip * 2 * block_len, 2 * block_len, 0)
-
-    def product_scatter(pairs):
-        def part(chip, *tokens):
-            left = [rows_of(after(v, *tokens), chip) for v, _, _ in pairs]
-            return sum(dot(l, w, 1, d) for l, (_, w, d) in zip(left, pairs)).astype(LOW)
-
-        return ScatterSeq(move, part)
-
-    g1 = dot(n2_all, full_first)
-    g2 = dot(n2_all, full_second)
-    p = (g1 * g2).astype(LOW)
-    g1 = g1.astype(LOW)
-    g2 = g2.astype(LOW)
-    y_sum = product_scatter([(p, full_down, 0)])
-    y = hsum + y_sum.done()
-    layer_out = y.astype(LOW).reshape(1, block_len, width)
-
-    error = y - teacher.reshape(block_len, width).astype(WIDE)
-    tokens = block_len * seq * move.fsdp
-    dy = tokens / count * keep * error
-    dyb = dy.astype(LOW)
-    dy_all = move.gather_seq(dyb)
-
-    dp = dot(dy_all, full_down, 1, 1)
-    dg1 = (dp * g2.astype(WIDE)).astype(LOW)
-    dg2 = (dp * g1.astype(WIDE)).astype(LOW)
-    dn2_sum = product_scatter([(dg1, full_first, 1), (dg2, full_second, 1)])
-    grad_down = dot(after(p, dn2_sum.term), dy_all, 0, 0).astype(LOW)
-    dn2 = dn2_sum.done(grad_down)
-    dh = dy + r2 * (dn2 - m2 * jnp.mean(dn2 * m2, axis=-1, keepdims=True))
-    dhb = dh.astype(LOW)
-    mean_own = jnp.mean(after(dhb, dn2_sum.term).astype(WIDE) * mixed_out, axis=-1)
-    dh_all = move.gather_seq(dhb)
-    mean_all = move.gather_seq(mean_own).reshape(length, 1)
-    grad_first = dot(after(n2_all, mean_own), dg1, 0, 0).astype(LOW)
-    grad_second = dot(after(n2_all, grad_first), dg2, 0, 0).astype(LOW)
+
+    tokens = block_len * seq * fsdp
+    layer_out, grad_down, grad_first, grad_second, dh, dh_all, *_, loss_own, means = glu_all(
+        shape,
+        n2_all,
+        full_first,
+        full_second,
+        full_down,
+        hsum,
+        teacher.reshape(block_len, width),
+        keep,
+        spread(tokens / count),
+        mixed_out,
+    )
+    layer_out = layer_out.reshape(1, block_len, width)
+    mean_all = means[:, 0].reshape(length, 1)
 
     dn1, share_down, share_out, loss, got_first, got_second, got_attn = back_all(
         shape, heads, hd, rates, bounds, seg, z, a, dh_all, ra_all, mean_all, states, full_out,
-        full_attn, n1_all, spread(jnp.sum(keep * error * error)),
+        full_attn, n1_all, loss_own,
         (grad_down, grad_first, grad_second),
     )
     input_grad = dh + r1 * (dn1 - n1 * jnp.mean(dn1 * n1, axis=-1, keepdims=True))

time: 1100 us -> 1020 us (0.927)
  Pallas kernels: 655 us -> 975 us
  matrix products: 176 us -> 0 us
  waiting for transfers between devices: 157 us -> 0 us
  other arithmetic: 48 us -> 14.1 us
  local copies, waits for them, and re-layouts: 40.6 us -> 15.2 us
    pallas_call x3 -> x1, Pallas kernels: 0.01 us -> 317 us  [glu_all(): pl.pallas_call(functools.partial(glu_kernel, shape), in_specs=[HBM] + [in...]
    dot_general x12 -> x0, matrix products: 176 us -> none  [dot(): lax.dot_general(left, right, (((left_dim,), (right_dim,)), ((), ())), pre...]
    ppermute x15 -> x0, waiting for transfers between devices: 157 us -> none  [the longest x5 157 us: to_chip(): return lax.ppermute(v, 'seq', self.chip_perm)]
    dynamic_update_slice x10 -> x0, local copies, waits for them, and re-layouts: 18.3 us -> none  [gather_seq(): lax.dynamic_update_slice_in_dim(whole, part, i * t, 0)]
    reduce_sum x3 -> x0, other arithmetic: 12.5 us -> none  [the longest x1 5.66 us: on_device(): jnp.sum(keep * error * error)]
  transfers between devices with their start and end apart: 15 -> 0, of which waited for: 4 -> 0; matrix products, arithmetic and copies ran while one was open for 8% -> 0% of each run, Pallas kernels for 0% -> 0%
where the time goes in v5:
time: 1020 us; the launch traced here: 1010 us
  Pallas kernels  975 us (96%)
  local copies, waits for them, and re-layouts  15.2 us (1%)
  other arithmetic  14.1 us (1%)
    pallas_call x1, Pallas kernels, gather_all(): pl.pallas_call(functools.partial(gather_kernel, shape, heads, hd), in_spe...  328 us
    pallas_call x1, Pallas kernels, back_all(): pl.pallas_call(functools.partial(back_kernel, shape, heads, hd), in_specs...  322 us
    pallas_call x1, Pallas kernels, glu_all(): pl.pallas_call(functools.partial(glu_kernel, shape), in_specs=[HBM] + [in...  317 us

profile of v5, /device:TPU:0, one launch (start us, length us, event | category | flops | bytes accessed | tf_op | source)
XLA Modules:
  0.0 1008.2 jit_solution(1115114952451029742)
XLA Ops:
  0.6 0.0 copy-start
  0.7 1.4 dynamic_slice.3.rate_ref
  2.0 0.0 copy-start.7
  2.0 3.2 pack_columns.1
  5.2 2.1 fusion.8
  7.3 0.0 copy-done
  7.3 1.7 fusion.2.n1_ref
  9.1 0.0 copy-done.7
  9.1 0.6 convert_reduce_fusion
  9.7 1.2 broadcast_in_dim.20.count_ref
  10.9 327.9 %gather_all.1 = (bf16[4,64,2048]{2,1,0:T(8,128)(2,1)}, bf16[4,64,1408]{2,1,0:T(8,128)(2,1)}, bf16[4,64,1408]{2,1,0:T(8,128)(2,1)}, bf16[4,4,2,64,2048]{4,3,2,1,0...) custom-call(f32[4]{0:T(128)} %dynamic_slice.3.rate_ref, ...), custom_call_target="tpu_custom_call" | custom-call | tf_op jit(solution)/shard_map/gather_all/pallas_call | solution.py:625
  338.8 1.2 slice.15
  340.7 0.6 broadcast_in_dim.22.scale_ref
  341.3 0.9 copy.24.keep_ref
  342.1 0.0 copy-start.6
  342.1 317.4 %glu_all.1 = (bf16[512,2048]{1,0:T(8,128)(2,1)}, bf16[1408,2048]{1,0:T(8,128)(2,1)}, bf16[2048,1408]{1,0:T(8,128)(2,1)}, bf16[2048,1408]{1,0:T(8,128)(2,1)}, f32...) custom-call(bf16[2048,2048]{1,0:T(8,128)(2,1)} %get-tuple-element.53, ...), custom_call_target="tpu_custom_call" | custom-call | tf_op jit(solution)/shard_map/glu_all/pallas_call | solution.py:1325
  659.5 0.8 slice.18
  660.4 1.3 copy.27.mean
  661.7 0.0 copy-done.6
  661.7 1.3 copy.25.segc
  663.0 0.1 slice.16
  663.1 0.6 pad_add_fusion.bounds_ref
  663.7 0.9 add_rsqrt_fusion
  664.6 1.3 copy.26.ra
  665.9 0.0 copy-start.1
  665.9 322.0 %back_all.1 = (f32[512,2048]{1,0:T(8,128)}, f32[176,2048]{1,0:T(8,128)}, f32[64,2048]{1,0:T(8,128)}, f32[8,128]{1,0:T(8,128)}, bf16[4,64,1408]{2,1,0:T(8,128)(2,...) custom-call(f32[4]{0:T(128)} %dynamic_slice.3.rate_ref, ...), custom_call_target="tpu_custom_call" | custom-call | tf_op jit(solution)/shard_map/back_all/pallas_call | solution.py:1023
  988.0 4.0 unpack_columns.1
  992.0 0.0 copy-start.2
  992.0 0.0 copy-done.1
  992.0 3.0 fusion.3
  995.1 0.4 copy-done.2
  995.5 0.0 copy-start.3
  995.5 5.3 fusion.7
  1000.7 0.0 copy-start.5
  1000.7 0.0 copy-start.4
  1000.7 1.3 slice.19
  1003.4 0.0 copy-done.3
  1003.4 1.3 copy.31
  1004.7 0.0 copy-done.5
  1004.7 0.8 copy.32
  1005.5 0.0 copy-done.4
  1005.5 1.1 copy.33
  (3 shorter events, 0.0 us)
Async XLA Ops:
  0.6 6.7 copy-start
  2.0 7.0 copy-start.7
  342.1 319.6 %copy-start.6 = (s32[4,1,512]{2,1,0:T(1,128)S(1)}, s32[4,1,512]{2,1,0:T(1,128)}, u32[]{:S(2)}) copy-start(s32[4,1,512]{2,1,0:T(1,128)} %get-tuple-element.61) | copy-start | bytes 24580
  665.9 326.1 %copy-start.1 = (bf16[1,512,2048]{2,1,0:T(8,128)(2,1)S(1)}, bf16[1,512,2048]{2,1,0:T(8,128)(2,1)}, u32[]{:S(2)}) copy-start(bf16[1,512,2048]{2,1,0:T(8,128)(2,1)} %param.13) | copy-start | bytes 6291460
  992.0 3.5 copy-start.2
  995.5 7.9 copy-start.3
  1000.7 4.0 copy-start.5
  1000.7 4.8 copy-start.4

commit v6 on v5

--- a/solution.py
+++ b/solution.py
@@ -703,19 +703,20 @@
 
 
 class Sum:
-    def __init__(self, net, g, side, ring, send, load):
+    def __init__(self, net, g, side, ring, send, load, there=False):
         self.net, self.g, self.side_ref, self.ring_ref = net, g, side, ring
         self.send_buf, self.load = send, load
         self.side = []
         self.ring = []
-        for k in range(net.outer):
+        self.at = 0
+        self.there = there
+        for k in range(0 if there else net.outer):
             o = self.spot(k)
             now = []
             for j in range(1, net.inner):
                 to = lax.rem(net.i + j, net.inner)
                 now.append(net.send(g.at[:, o, to], side.at[j - 1, :, o], net.at_inner(j)))
             self.side.append(now)
-        self.at = 0
 
     def spot(self, k):
         return lax.rem(self.net.o + 2 * self.net.outer - 1 - k, self.net.outer)
@@ -726,8 +727,9 @@
         o = self.spot(k)
         terms = self.load
         loads = [net.copy(self.g.at[:, o, net.i], terms.at[0])]
-        for j, copy in enumerate(self.side[k]):
-            copy.wait_recv()
+        for j in range(net.inner - 1):
+            if not self.there:
+                self.side[k][j].wait_recv()
             loads.append(net.copy(self.side_ref.at[j, :, o], terms.at[j + 1]))
         count = net.inner
         if k > 0:
@@ -754,33 +756,31 @@
             self.ring.append(net.send(self.send_buf.at[k % 2], self.ring_ref.at[k], net.at_outer(1)))
 
 
-GRADS = ("down", "first", "second", "attn", "out")
-SPLIT = ("first", "second", "attn")
-LOADS = ("down", "first", "attn", "out")
+GRADS = ("down", "second", "attn", "out")
+SPLIT = ("second", "attn")
 
 
 def back_kernel(
     shape, heads, hd,
     rate_ref, bounds_ref, segc, segr, z, a, dh, ra, mean, states, w_out, w_attn, n1, loss_ref,
-    g_down, g_first, g_second,
-    dn1_ref, o_down, o_out, o_loss, got_first, got_second, got_attn, g_attn,
-    side_down, side_first, side_second, side_attn, side_out,
-    ring_down, ring_first, ring_second, ring_attn, ring_out,
+    g_down, g_second, side_second,
+    dn1_ref, o_down, o_out, o_loss, got_second, got_attn, g_attn,
+    side_down, side_attn, side_out,
+    ring_down, ring_second, ring_attn, ring_out,
     core_in, chip_in,
     dz_all, later, dj, o_chunk, out_acc, g_out, stage, term, wide_tile,
     *rest
 ):
     it = iter(rest)
     take = lambda names: {name: next(it) for name in names}
-    sends, loads = take(GRADS), take(LOADS)
-    loads["second"] = loads["first"]
+    sends, loads = take(GRADS), take(GRADS)
     total_bufs = [next(it) for _ in range(3)]
     send_sem, recv_sem, local_sem = (next(it) for _ in range(3))
     net = Net(shape, send_sem, recv_sem, local_sem)
-    grads = dict(down=g_down, first=g_first, second=g_second, attn=g_attn, out=g_out)
-    sides = dict(down=side_down, first=side_first, second=side_second, attn=side_attn, out=side_out)
-    rings = dict(down=ring_down, first=ring_first, second=ring_second, attn=ring_attn, out=ring_out)
-    gots = dict(first=got_first, second=got_second, attn=got_attn)
+    grads = dict(down=g_down, second=g_second, attn=g_attn, out=g_out)
+    sides = dict(down=side_down, second=side_second, attn=side_attn, out=side_out)
+    rings = dict(down=ring_down, second=ring_second, attn=ring_attn, out=ring_out)
+    gots = dict(second=got_second, attn=got_attn)
     owned = dict(down=o_down, out=o_out)
     length, cols = dz_all.shape
     width = dh.shape[1]
@@ -792,7 +792,8 @@
     loss = Total(net, loss_ref, *total_bufs)
 
     def begin(name):
-        sums[name] = Sum(net, grads[name], sides[name], rings[name], sends[name], loads[name])
+        there = name == "second"
+        sums[name] = Sum(net, grads[name], sides[name], rings[name], sends[name], loads[name], there)
         queue.extend([name] * net.outer)
 
     def pump(times=1):
@@ -811,8 +812,9 @@
                 swaps[name] = swap(net, totals, gots[name])
 
     loss.step()
-    for name in ("down", "first", "second"):
+    for name in ("second", "down"):
         begin(name)
+    pump()
 
     later[...] = jnp.zeros_like(later)
     out_acc[...] = jnp.zeros_like(out_acc)
@@ -973,7 +975,7 @@
     net.finish()
 
 
-def back_all(shape, heads, hd, rates, bounds, seg, z, a, dh, ra, mean, states, w_out, w_attn, n1, loss, grads):
+def back_all(shape, heads, hd, rates, bounds, seg, z, a, dh, ra, mean, states, w_out, w_attn, n1, loss, g_down, g_second, side_second):
     seq, fsdp, inner = shape
     outer = fsdp // inner
     length, width = dh.shape
@@ -981,12 +983,10 @@
     own_rows = length // seq
     chips = seq // 2
     tile = min(256, own_rows)
-    lead = {"down": 1, "out": 1, "first": seq, "second": seq, "attn": seq}
-    blocks = [
-        g.reshape(lead[n], outer, inner, g.shape[0] // (lead[n] * fsdp), g.shape[1])
-        for n, g in zip(GRADS, grads)
-    ]
-    size = {n: (g.shape[0], g.shape[3], g.shape[4]) for n, g in zip(GRADS, blocks)}
+    g_down = g_down.reshape(1, outer, inner, g_down.shape[0] // fsdp, width)
+    size = {
+        n: (g.shape[0], g.shape[3], g.shape[4]) for n, g in (("down", g_down), ("second", g_second))
+    }
     size["attn"] = (seq, width // (seq * fsdp), cols)
     size["out"] = (1, width // (seq * fsdp), width)
     whole = lambda n: (size[n][0], outer, inner) + size[n][1:]
@@ -995,7 +995,9 @@
     outs = [jax.ShapeDtypeStruct((own_rows, width), WIDE), row("down"), row("out")]
     outs += [jax.ShapeDtypeStruct((8, 128), WIDE)]
     outs += [low(size[n]) for n in SPLIT] + [low(whole("attn"))]
-    outs += [low((inner - 1, size[n][0], outer) + size[n][1:]) for n in GRADS]
+    outs += [
+        low((inner - 1, size[n][0], outer) + size[n][1:]) for n in GRADS if n != "second"
+    ]
     outs += [low((outer - 1,) + size[n]) for n in GRADS]
     outs += [low((chips, own_rows, width)), low((max(chips - 1, 1), own_rows, width))]
     in_vmem = pl.BlockSpec(memory_space=pltpu.VMEM)
@@ -1012,7 +1014,7 @@
         pltpu.VMEM((tile, width), WIDE),
     ]
     scratch += [pltpu.VMEM((2,) + size[n], LOW) for n in GRADS]
-    scratch += [pltpu.VMEM((inner + 1,) + size[n], LOW) for n in LOADS]
+    scratch += [pltpu.VMEM((inner + 1,) + size[n], LOW) for n in GRADS]
     scratch += total_scratch(shape)
     copies = 5 * (outer * inner + outer) + 3 * seq + total_copies(shape) + 2 * length // tile
     scratch += [
@@ -1032,8 +1034,8 @@
         name="back_all",
     )(
         rates, bounds, seg.reshape(length, 1), seg.reshape(1, length), z, a, dh, ra, mean, states,
-        w_out, w_attn, n1, loss, *blocks
-    )[:7]
+        w_out, w_attn, n1, loss, g_down, g_second, side_second
+    )[:6]
 
 
 def spans(n, step=512):
@@ -1044,9 +1046,9 @@
     shape,
     n2_all, w_first, w_second, w_down, hsum_ref, teacher_ref, keep_ref, scale_ref, mixed_ref,
     layer_out, g_down, g_first, g_second, dh_ref, dh_all, dy_all, dy_own, dh_own,
-    core_y, chip_y, core_n, chip_n,
+    core_y, chip_y, core_n, chip_n, side_first, side_second, ring_first, got_first,
     loss_ref, mean_all,
-    one_all, two_all, p_all, dy_wide, stage, term, wide_tile, hsum_tile, mixed_tile, low_tile, sent_tile,
+    one_all, two_all, p_all, dy_wide, stage, term, wide_tile, hsum_tile, mixed_tile, low_tile, sent_tile, sum_send, sum_load,
     send_sem, recv_sem, local_sem,
 ):
     net = Net(shape, send_sem, recv_sem, local_sem)
@@ -1236,26 +1238,40 @@
         for b in spans(ffs):
             out[b, :] = dot(p_all[:, b], dy[...], 0, 0).astype(LOW)
 
-    pltpu.emit_pipeline(
-        grad_down,
-        grid=(width // step,),
-        in_specs=[pl.BlockSpec((length, step), lambda i: (0, i))],
-        out_specs=[pl.BlockSpec((ffs, step), lambda i: (0, i))],
-    )(dy_all, g_down)
+    parts = 2
+    spread = net.outer // parts
+    features = width // net.seq // parts
 
     def grad_columns(held, target):
         def body(n2, out):
             for b in spans(ffs):
-                out[:, b] = dot(n2[...], held[:, b], 0, 0).astype(LOW)
+                got = dot(n2[...], held[:, b], 0, 0).astype(LOW)
+                out[:, :, :, :, b] = got.reshape(out.shape[:-1] + (got.shape[1],))
 
         pltpu.emit_pipeline(
             body,
-            grid=(width // step,),
-            in_specs=[pl.BlockSpec((length, step), lambda i: (0, i))],
-            out_specs=[pl.BlockSpec((step, ffs), lambda i: (i, 0))],
+            grid=(net.seq, parts),
+            in_specs=[pl.BlockSpec((length, features), lambda i, j: (0, i * parts + j))],
+            out_specs=[
+                pl.BlockSpec((1, spread) + target.shape[2:], lambda i, j: (i, j, 0, 0, 0)),
+            ],
         )(n2_all, target)
 
+    def no_final(i, rows):
+        sum_send[(net.outer - 1) % 2, i] = rows.astype(LOW)
+
     grad_columns(one_all, g_first)
+    sum_first = Sum(net, g_first, side_first, ring_first, sum_send, sum_load)
+    grad_columns(two_all, g_second)
+    sides = []
+    for k in range(net.outer):
+        o = sum_first.spot(k)
+        for j in range(1, net.inner):
+            to = lax.rem(net.i + j, net.inner)
+            sides.append(
+                net.send(g_second.at[:, o, to], side_second.at[j - 1, :, o], net.at_inner(j))
+            )
+    sum_first.step(no_final)
     dh_rows = []
     means = []
 
@@ -1295,13 +1311,25 @@
         dh_rows.append(Rows(net, dh_own.at[span], dh_all, t * CHUNK))
 
     n_sum.keep(0, finish_n)
-    grad_columns(two_all, g_second)
+    sum_first.step(no_final)
+    pltpu.emit_pipeline(
+        grad_down,
+        grid=(width // step,),
+        in_specs=[pl.BlockSpec((length, step), lambda i: (0, i))],
+        out_specs=[pl.BlockSpec((ffs, step), lambda i: (0, i))],
+    )(dy_all, g_down)
+    while sum_first.at < net.outer:
+        sum_first.step(no_final)
+    swap_first = swap(net, sum_send.at[(net.outer - 1) % 2], got_first)
     for rows in dh_rows:
         rows.turn()
     for rows in dh_rows:
         rows.done()
     for copy in means:
         copy.wait_recv()
+    for copy in sides:
+        copy.wait_recv()
+    arrive(swap_first)
     net.finish()
 
 
@@ -1314,14 +1342,19 @@
     chunks = length // CHUNK
     low = lambda *dims: jax.ShapeDtypeStruct(dims, LOW)
     wide = lambda *dims: jax.ShapeDtypeStruct(dims, WIDE)
-    outs = [low(own_rows, width), low(ffs, width), low(width, ffs), low(width, ffs)]
+    outer = fsdp // inner
+    r = width // (seq * fsdp)
+    whole = low(seq, outer, inner, r, ffs)
+    outs = [low(own_rows, width), low(ffs, width), whole, whole]
     outs += [wide(own_rows, width), low(length, width), low(length, width)]
     outs += [low(own_rows, width)] * 2
     outs += [low(chips, own_rows, width), low(max(chips - 1, 1), own_rows, width)] * 2
+    outs += [low(inner - 1, seq, outer, r, ffs)] * 2 + [low(outer - 1, seq, r, ffs)]
+    outs += [low(seq, r, ffs)]
     in_hbm = len(outs)
     outs += [wide(8, 128), wide(chunks, 8, CHUNK)]
     in_vmem = pl.BlockSpec(memory_space=pltpu.VMEM)
-    copies = 16 * chunks + 16 * seq
+    copies = 16 * chunks + 16 * seq + 3 * outer * inner
     return pl.pallas_call(
         functools.partial(glu_kernel, shape),
         in_specs=[HBM] + [in_vmem] * 3 + [HBM] * 2 + [in_vmem] * 2 + [HBM],
@@ -1337,9 +1370,11 @@
             pltpu.VMEM((CHUNK, width), WIDE),
             pltpu.VMEM((CHUNK, width), LOW),
             pltpu.VMEM((CHUNK, width), LOW),
+            pltpu.VMEM((2, seq, r, ffs), LOW),
+            pltpu.VMEM((inner + 1, seq, r, ffs), LOW),
             pltpu.SemaphoreType.DMA((copies,)),
             pltpu.SemaphoreType.DMA((copies,)),
-            pltpu.SemaphoreType.DMA((16 * chunks,)),
+            pltpu.SemaphoreType.DMA((16 * chunks + outer * (inner + 1) + seq,)),
         ],
         compiler_params=pltpu.CompilerParams(
             collective_id=2, has_side_effects=True, vmem_limit_bytes=VMEM_BYTES
@@ -1410,7 +1445,7 @@
     ra_all = lax.rsqrt(squares / width + 1e-6)
 
     tokens = block_len * seq * fsdp
-    layer_out, grad_down, grad_first, grad_second, dh, dh_all, *_, loss_own, means = glu_all(
+    layer_out, grad_down, _, grad_second, dh, dh_all, *others, loss_own, means = glu_all(
         shape,
         n2_all,
         full_first,
@@ -1424,11 +1459,12 @@
     )
     layer_out = layer_out.reshape(1, block_len, width)
     mean_all = means[:, 0].reshape(length, 1)
-
-    dn1, share_down, share_out, loss, got_first, got_second, got_attn = back_all(
+    side_second, got_first = others[-3], others[-1]
+
+    dn1, share_down, share_out, loss, got_second, got_attn = back_all(
         shape, heads, hd, rates, bounds, seg, z, a, dh_all, ra_all, mean_all, states, full_out,
         full_attn, n1_all, loss_own,
-        (grad_down, grad_first, grad_second),
+        grad_down, grad_second, side_second,
     )
     input_grad = dh + r1 * (dn1 - n1 * jnp.mean(dn1 * n1, axis=-1, keepdims=True))
     loss = loss[0, 0] / (width * count)

time: 1020 us -> 980 us (0.961)
  Pallas kernels: 975 us -> 936 us
    pallas_call x1, Pallas kernels: 322 us -> 249 us  [back_all(): pl.pallas_call(functools.partial(back_kernel, shape, heads, hd), in_specs...]
    pallas_call x1, Pallas kernels: 317 us -> 352 us  [glu_all(): pl.pallas_call(functools.partial(glu_kernel, shape), in_specs=[HBM] + [in...]
where the time goes in v6:
time: 980 us; the launch traced here: 970 us
  Pallas kernels  936 us (96%)
  local copies, waits for them, and re-layouts  15.2 us (2%)
  other arithmetic  14.1 us (1%)
    pallas_call x1, Pallas kernels, glu_all(): pl.pallas_call(functools.partial(glu_kernel, shape), in_specs=[HBM] + [in...  352 us
    pallas_call x1, Pallas kernels, gather_all(): pl.pallas_call(functools.partial(gather_kernel, shape, heads, hd), in_spe...  328 us
    pallas_call x1, Pallas kernels, back_all(): pl.pallas_call(functools.partial(back_kernel, shape, heads, hd), in_specs...  249 us

profile of v6, /device:TPU:0, one launch (start us, length us, event | category | flops | bytes accessed | tf_op | source)
XLA Modules:
  0.0 969.6 jit_solution(11688845845127054076)
XLA Ops:
  0.6 0.0 copy-start
  0.7 1.4 dynamic_slice.3.rate_ref
  2.0 0.0 copy-start.7
  2.0 3.2 pack_columns.1
  5.2 2.1 fusion.8
  7.3 0.0 copy-done
  7.3 1.7 fusion.2.n1_ref
  9.1 0.0 copy-done.7
  9.1 0.6 convert_reduce_fusion
  9.7 1.2 broadcast_in_dim.20.count_ref
  10.9 327.9 %gather_all.1 = (bf16[4,64,2048]{2,1,0:T(8,128)(2,1)}, bf16[4,64,1408]{2,1,0:T(8,128)(2,1)}, bf16[4,64,1408]{2,1,0:T(8,128)(2,1)}, bf16[4,4,2,64,2048]{4,3,2,1,0...) custom-call(f32[4]{0:T(128)} %dynamic_slice.3.rate_ref, ...), custom_call_target="tpu_custom_call" | custom-call | tf_op jit(solution)/shard_map/gather_all/pallas_call | solution.py:625
  338.8 1.2 slice.15
  340.7 0.6 broadcast_in_dim.22.scale_ref
  341.3 0.9 copy.24.keep_ref
  342.2 0.0 copy-start.6
  342.2 351.9 %glu_all.1 = (bf16[512,2048]{1,0:T(8,128)(2,1)}, bf16[1408,2048]{1,0:T(8,128)(2,1)}, bf16[4,4,2,64,1408]{4,3,2,1,0:T(8,128)(2,1)}, bf16[4,4,2,64,1408]{4,3,2,1,0...) custom-call(bf16[2048,2048]{1,0:T(8,128)(2,1)} %get-tuple-element.53, ...), custom_call_target="tpu_custom_call" | custom-call | tf_op jit(solution)/shard_map/glu_all/pallas_call | solution.py:1358
  694.1 0.8 slice.18
  695.0 1.3 copy.27.mean
  696.3 0.0 copy-done.6
  696.3 1.3 copy.25.segc
  697.7 0.1 slice.16
  697.8 0.6 pad_add_fusion.bounds_ref
  698.4 0.9 add_rsqrt_fusion
  699.2 1.3 copy.26.ra
  700.6 0.0 copy-start.1
  700.6 248.8 %back_all.1 = (f32[512,2048]{1,0:T(8,128)}, f32[176,2048]{1,0:T(8,128)}, f32[64,2048]{1,0:T(8,128)}, f32[8,128]{1,0:T(8,128)}, bf16[4,64,1408]{2,1,0:T(8,128)(2,...) custom-call(f32[4]{0:T(128)} %dynamic_slice.3.rate_ref, ...), custom_call_target="tpu_custom_call" | custom-call | tf_op jit(solution)/shard_map/back_all/pallas_call | solution.py:1025
  949.4 4.0 unpack_columns.1
  953.4 0.0 copy-start.2
  953.4 0.0 copy-done.1
  953.4 3.0 fusion.3
  956.5 0.4 copy-done.2
  956.9 0.0 copy-start.3
  956.9 5.3 fusion.7
  962.1 0.0 copy-start.5
  962.1 0.0 copy-start.4
  962.1 1.3 slice.19
  964.8 0.0 copy-done.3
  964.8 1.3 copy.31
  966.1 0.0 copy-done.5
  966.1 0.8 copy.32
  966.9 0.0 copy-done.4
  966.9 1.1 copy.33
  (3 shorter events, 0.0 us)
Async XLA Ops:
  0.6 6.7 copy-start
  2.0 7.0 copy-start.7
  342.2 354.2 %copy-start.6 = (s32[4,1,512]{2,1,0:T(1,128)S(1)}, s32[4,1,512]{2,1,0:T(1,128)}, u32[]{:S(2)}) copy-start(s32[4,1,512]{2,1,0:T(1,128)} %get-tuple-element.61) | copy-start | bytes 24580
  700.6 252.8 %copy-start.1 = (bf16[1,512,2048]{2,1,0:T(8,128)(2,1)S(1)}, bf16[1,512,2048]{2,1,0:T(8,128)(2,1)}, u32[]{:S(2)}) copy-start(bf16[1,512,2048]{2,1,0:T(8,128)(2,1)} %param.13) | copy-start | bytes 6291460
  953.4 3.5 copy-start.2
  956.9 7.9 copy-start.3
  962.1 4.0 copy-start.5
  962.1 4.8 copy-start.4

commit v7 on v6

--- a/solution.py
+++ b/solution.py
@@ -703,14 +703,14 @@
 
 
 class Sum:
-    def __init__(self, net, g, side, ring, send, load, there=False):
+    def __init__(self, net, g, side, ring, send, load, early=None, there=0):
         self.net, self.g, self.side_ref, self.ring_ref = net, g, side, ring
         self.send_buf, self.load = send, load
         self.side = []
         self.ring = []
         self.at = 0
-        self.there = there
-        for k in range(0 if there else net.outer):
+        self.early, self.there = early, there
+        for k in range(there, net.outer):
             o = self.spot(k)
             now = []
             for j in range(1, net.inner):
@@ -728,9 +728,10 @@
         terms = self.load
         loads = [net.copy(self.g.at[:, o, net.i], terms.at[0])]
         for j in range(net.inner - 1):
-            if not self.there:
-                self.side[k][j].wait_recv()
-            loads.append(net.copy(self.side_ref.at[j, :, o], terms.at[j + 1]))
+            side = self.early if k < self.there else self.side_ref
+            if k >= self.there:
+                self.side[k - self.there][j].wait_recv()
+            loads.append(net.copy(side.at[j, :, o], terms.at[j + 1]))
         count = net.inner
         if k > 0:
             self.ring[k - 1].wait_recv()
@@ -757,15 +758,21 @@
 
 
 GRADS = ("down", "second", "attn", "out")
+
+
+def early_steps(outer):
+    return outer // 2
+
+
 SPLIT = ("second", "attn")
 
 
 def back_kernel(
     shape, heads, hd,
     rate_ref, bounds_ref, segc, segr, z, a, dh, ra, mean, states, w_out, w_attn, n1, loss_ref,
-    g_down, g_second, side_second,
+    g_down, g_second, early_second,
     dn1_ref, o_down, o_out, o_loss, got_second, got_attn, g_attn,
-    side_down, side_attn, side_out,
+    side_down, side_second, side_attn, side_out,
     ring_down, ring_second, ring_attn, ring_out,
     core_in, chip_in,
     dz_all, later, dj, o_chunk, out_acc, g_out, stage, term, wide_tile,
@@ -792,8 +799,8 @@
     loss = Total(net, loss_ref, *total_bufs)
 
     def begin(name):
-        there = name == "second"
-        sums[name] = Sum(net, grads[name], sides[name], rings[name], sends[name], loads[name], there)
+        early = (early_second, early_steps(net.outer)) if name == "second" else ()
+        sums[name] = Sum(net, grads[name], sides[name], rings[name], sends[name], loads[name], *early)
         queue.extend([name] * net.outer)
 
     def pump(times=1):
@@ -995,9 +1002,7 @@
     outs = [jax.ShapeDtypeStruct((own_rows, width), WIDE), row("down"), row("out")]
     outs += [jax.ShapeDtypeStruct((8, 128), WIDE)]
     outs += [low(size[n]) for n in SPLIT] + [low(whole("attn"))]
-    outs += [
-        low((inner - 1, size[n][0], outer) + size[n][1:]) for n in GRADS if n != "second"
-    ]
+    outs += [low((inner - 1, size[n][0], outer) + size[n][1:]) for n in GRADS]
     outs += [low((outer - 1,) + size[n]) for n in GRADS]
     outs += [low((chips, own_rows, width)), low((max(chips - 1, 1), own_rows, width))]
     in_vmem = pl.BlockSpec(memory_space=pltpu.VMEM)
@@ -1264,7 +1269,7 @@
     sum_first = Sum(net, g_first, side_first, ring_first, sum_send, sum_load)
     grad_columns(two_all, g_second)
     sides = []
-    for k in range(net.outer):
+    for k in range(early_steps(net.outer)):
         o = sum_first.spot(k)
         for j in range(1, net.inner):
             to = lax.rem(net.i + j, net.inner)

time: 980 us -> 949 us (0.968)
  Pallas kernels: 936 us -> 905 us
    pallas_call x1, Pallas kernels: 352 us -> 321 us  [glu_all(): pl.pallas_call(functools.partial(glu_kernel, shape), in_specs=[HBM] + [in...]
where the time goes in v7:
time: 949 us; the launch traced here: 939 us
  Pallas kernels  905 us (95%)
  local copies, waits for them, and re-layouts  15.2 us (2%)
  other arithmetic  14.1 us (1%)
    pallas_call x1, Pallas kernels, gather_all(): pl.pallas_call(functools.partial(gather_kernel, shape, heads, hd), in_spe...  328 us
    pallas_call x1, Pallas kernels, glu_all(): pl.pallas_call(functools.partial(glu_kernel, shape), in_specs=[HBM] + [in...  321 us
    pallas_call x1, Pallas kernels, back_all(): pl.pallas_call(functools.partial(back_kernel, shape, heads, hd), in_specs...  249 us

profile of v7, /device:TPU:0, one launch (start us, length us, event | category | flops | bytes accessed | tf_op | source)
XLA Modules:
  0.0 938.6 jit_solution(10843823902860658277)
XLA Ops:
  0.6 0.0 copy-start
  0.7 1.4 dynamic_slice.3.rate_ref
  2.0 0.0 copy-start.7
  2.0 3.2 pack_columns.1
  5.2 2.1 fusion.8
  7.3 0.0 copy-done
  7.3 1.7 fusion.2.n1_ref
  9.1 0.0 copy-done.7
  9.1 0.6 convert_reduce_fusion
  9.7 1.2 broadcast_in_dim.20.count_ref
  10.9 327.9 %gather_all.1 = (bf16[4,64,2048]{2,1,0:T(8,128)(2,1)}, bf16[4,64,1408]{2,1,0:T(8,128)(2,1)}, bf16[4,64,1408]{2,1,0:T(8,128)(2,1)}, bf16[4,4,2,64,2048]{4,3,2,1,0...) custom-call(f32[4]{0:T(128)} %dynamic_slice.3.rate_ref, ...), custom_call_target="tpu_custom_call" | custom-call | tf_op jit(solution)/shard_map/gather_all/pallas_call | solution.py:625
  338.8 1.2 slice.15
  340.7 0.6 broadcast_in_dim.22.scale_ref
  341.3 0.9 copy.24.keep_ref
  342.2 0.0 copy-start.6
  342.2 321.1 %glu_all.1 = (bf16[512,2048]{1,0:T(8,128)(2,1)}, bf16[1408,2048]{1,0:T(8,128)(2,1)}, bf16[4,4,2,64,1408]{4,3,2,1,0:T(8,128)(2,1)}, bf16[4,4,2,64,1408]{4,3,2,1,0...) custom-call(bf16[2048,2048]{1,0:T(8,128)(2,1)} %get-tuple-element.53, ...), custom_call_target="tpu_custom_call" | custom-call | tf_op jit(solution)/shard_map/glu_all/pallas_call | solution.py:1363
  663.3 0.8 slice.18
  664.1 1.3 copy.27.mean
  665.4 0.0 copy-done.6
  665.4 1.3 copy.25.segc
  666.8 0.1 slice.16
  666.9 0.6 pad_add_fusion.bounds_ref
  667.5 0.9 add_rsqrt_fusion
  668.3 1.3 copy.26.ra
  669.7 0.0 copy-start.1
  669.7 248.7 %back_all.1 = (f32[512,2048]{1,0:T(8,128)}, f32[176,2048]{1,0:T(8,128)}, f32[64,2048]{1,0:T(8,128)}, f32[8,128]{1,0:T(8,128)}, bf16[4,64,1408]{2,1,0:T(8,128)(2,...) custom-call(f32[4]{0:T(128)} %dynamic_slice.3.rate_ref, ...), custom_call_target="tpu_custom_call" | custom-call | tf_op jit(solution)/shard_map/back_all/pallas_call | solution.py:1030
  918.4 4.0 unpack_columns.1
  922.4 0.0 copy-start.2
  922.4 0.0 copy-done.1
  922.4 3.0 fusion.3
  925.4 0.4 copy-done.2
  925.9 0.0 copy-start.3
  925.9 5.3 fusion.7
  931.1 0.0 copy-start.5
  931.1 0.0 copy-start.4
  931.1 1.3 slice.19
  933.8 0.0 copy-done.3
  933.8 1.3 copy.31
  935.1 0.0 copy-done.5
  935.1 0.8 copy.32
  935.9 0.0 copy-done.4
  935.9 1.1 copy.33
  (3 shorter events, 0.0 us)
Async XLA Ops:
  0.6 6.7 copy-start
  2.0 7.0 copy-start.7
  342.2 323.3 %copy-start.6 = (s32[4,1,512]{2,1,0:T(1,128)S(1)}, s32[4,1,512]{2,1,0:T(1,128)}, u32[]{:S(2)}) copy-start(s32[4,1,512]{2,1,0:T(1,128)} %get-tuple-element.61) | copy-start | bytes 24580
  669.7 252.7 %copy-start.1 = (bf16[1,512,2048]{2,1,0:T(8,128)(2,1)S(1)}, bf16[1,512,2048]{2,1,0:T(8,128)(2,1)}, u32[]{:S(2)}) copy-start(bf16[1,512,2048]{2,1,0:T(8,128)(2,1)} %param.13) | copy-start | bytes 6291460
  922.4 3.5 copy-start.2
  925.9 7.9 copy-start.3
  931.1 4.0 copy-start.5
  931.1 4.8 copy-start.4
